TPU v7x, 32 devices: a whole 2x2x4 slice. The times are simulated.
32 devices in a mesh: dp: 4 (over x, core), tp: 8 (over z, y).
Axes of the slice: x: 2, y: 2, z: 4, core: 2. Of those that a mesh axis runs over, the one named last changes fastest.
Arguments:
- out_grad: bfloat16 [512, 7168], P(('dp', 'tp')), may hold values from -1.5 to 1.5
- gate_pre: bfloat16 [512, 12288], P('dp', 'tp'), may hold values from -8 to 8
- up_pre: bfloat16 [512, 12288], P('dp', 'tp'), may hold values from -6 to 6
- down_weight: bfloat16 [7168, 12288], P(None, 'tp'), may hold values from -0.0625 to 0.0625
- block_scales: bfloat16 [56, 96], P(None, 'tp'), may hold values from 0.25 to 4
Outputs:
- gate_grad: bfloat16 [512, 12288], P('dp', 'tp')
- up_grad: bfloat16 [512, 12288], P('dp', 'tp')
- down_grad: bfloat16 [7168, 12288], P('dp', 'tp')
All inputs are finite; a program needn't handle non-finite values.
Results may differ from a plain program's by a relative error of at most 0.028.
Values may be sent and summed in bfloat16 or wider, within the bound.
No kernel may reach another device: no remote copies, remote signals or barrier semaphores. Data moves between devices by JAX's collectives and lax.ppermute only.
A program may use at most 128 MiB of HBM per device.

v0:
```python
import jax
import jax.numpy as jnp
from jax import lax
from jax.sharding import PartitionSpec as P


def tile_quant(values, tile_axis):
    largest = jnp.max(jnp.abs(values), axis=tile_axis, keepdims=True)
    tile_scale = (largest + 1e-06) / 448.0
    payload = (values / tile_scale).astype(jnp.bfloat16)
    return (payload.astype(jnp.float32) * tile_scale).astype(jnp.bfloat16)


def per_device(out_grad, gate_pre, up_pre, down_weight, block_scales):
    width = down_weight.shape[0]
    hidden_units = down_weight.shape[1]
    weight_deq = (
        down_weight.reshape(width // 128, 128, hidden_units // 128, 128)
        * block_scales[:, None, :, None]
    ).reshape(width, hidden_units)
    grad_tokens = lax.all_gather(out_grad, "tp", axis=0, tiled=True)
    local_tokens = grad_tokens.shape[0]
    grad_full = grad_tokens.astype(jnp.float32)
    grad_rowq = tile_quant(grad_full.reshape(local_tokens, width // 128, 128), 2).reshape(
        local_tokens, width
    )
    grad_colq = tile_quant(grad_full.reshape(local_tokens // 128, 128, width), 1).reshape(
        local_tokens, width
    )
    hidden_grad = jnp.dot(grad_rowq, weight_deq, preferred_element_type=jnp.float32)
    gate_val = gate_pre.astype(jnp.float32)
    up_val = up_pre.astype(jnp.float32)
    sigma = 1.0 / (1.0 + jnp.exp(-gate_val))
    gate_grad = (hidden_grad * up_val * sigma * (1.0 + gate_val * (1.0 - sigma))).astype(
        jnp.bfloat16
    )
    up_grad = (hidden_grad * gate_val * sigma).astype(jnp.bfloat16)
    hidden_val = gate_val * sigma * up_val
    hidden_colq = tile_quant(hidden_val.reshape(local_tokens // 128, 128, hidden_units), 1).reshape(
        local_tokens, hidden_units
    )
    width_dev = width // lax.axis_size("dp")
    every_cols = lax.all_to_all(grad_colq, "dp", split_axis=1, concat_axis=0, tiled=True)
    start_sum = jnp.zeros((width_dev, hidden_units), jnp.float32)
    hidden_piece = lax.all_gather(hidden_colq, "dp", axis=0, tiled=True)
    block_count = hidden_piece.shape[0] // local_tokens

    def one_block(block_num, inner):
        hidden_block = lax.dynamic_slice_in_dim(
            hidden_piece, block_num * local_tokens, local_tokens, 0
        )
        grad_block = lax.dynamic_slice_in_dim(every_cols, block_num * local_tokens, local_tokens, 0)
        term = lax.dot_general(
            grad_block, hidden_block, (((0,), (0,)), ((), ())), preferred_element_type=jnp.float32
        )
        term = lax.optimization_barrier(term.astype(jnp.bfloat16)).astype(jnp.float32)
        return inner + term

    summed = lax.fori_loop(0, block_count, one_block, start_sum)
    return (gate_grad, up_grad, summed.astype(jnp.bfloat16))


def solution(mesh):
    placed = (P(("dp", "tp"), None), P("dp", "tp"), P("dp", "tp"), P(None, "tp"), P(None, "tp"))
    return jax.shard_map(
        per_device,
        mesh=mesh,
        in_specs=placed,
        out_specs=(P("dp", "tp"), P("dp", "tp"), P("dp", "tp")),
        check_vma=False,
    )
```

profile of v0, /device:TPU:0, one launch (start us, length us, event | category | flops | bytes accessed | tf_op | source)
XLA Modules:
  0.0 213.6 jit_solution(7156497056831395032)
XLA Ops:
  7.2 0.0 all-gather.3.cloned.1.call-start
  7.2 0.7 all-gather.3.cloned.1.call-update
  7.9 0.0 copy-start.1
  7.9 0.0 copy-start.2
  7.9 0.0 all-gather.5.cloned.1.call-start
  8.0 28.9 %copy.10 = bf16[7168,1536]{0,1:T(8,128)(2,1)} copy(bf16[7168,1536]{1,0:T(8,128)(2,1)} %param.10) | data formatting | bytes 44040192 | tf_op args[3]
  36.8 0.0 copy-done.1
  36.8 0.0 copy-done.2
  36.8 0.3 abs_reduce_fusion
  37.1 22.0 %all-gather.3.cloned.1.call-done = bf16[128,7168]{1,0:T(8,128)(2,1)} async-done(((bf16[16,7168]{1,0:T(8,128)(2,1)}), bf16[128,7168]{1,0:T(8,128)(2,1)}) %all-gather.3.cloned.1.call-update) | async-done | bytes 1835024 | tf_op jit(solution)/shard_map/all_gather | solution.py:21
  59.2 1.7 fusion.5
  60.9 3.4 %multiply_convert_fusion = (bf16[128,7168]{1,0:T(8,128)(2,1)}, f32[16,8,56,128]{3,1,2,0:T(8,128)S(1)}) fusion(bf16[128,7168]{1,0:T(8,128)(2,1)} %all-gather.3.cloned.1.call-done, f32[7168]{0:T(1024)S(1)} %add_multiply_fusion.1), kind=kLoop, calls=%fused_computation.17 | loop fusion | flops 6422528 | bytes 7368704 | tf_op jit(solution)/shard_map/convert_element_type | solution.py:11
  64.4 2.5 %copy.13 = f32[16,8,56,128]{3,2,1,0:T(8,128)} copy(f32[16,8,56,128]{3,1,2,0:T(8,128)S(1)} %get-tuple-element.107) | data formatting | bytes 7340032
  66.9 3.1 %reduce_max.27 = f32[128,56]{1,0:T(8,128)S(1)} reduce(f32[128,56,128]{2,1,0:T(8,128)} %bitcast.31, f32[]{:T(128)} %constant.41.clone.1), dimensions={2}, to_apply=%region_0.0 | reduce | flops 910336 | bytes 3698692 | tf_op jit(solution)/shard_map/reduce_max | solution.py:8
  69.9 2.4 %div.52 = f32[128,56,128]{2,1,0:T(8,128)} broadcast(f32[128,56]{1,0:T(8,128)S(1)} %add_multiply_fusion), dimensions={0,1} | broadcast | bytes 3698688 | tf_op jit(solution)/shard_map/div | solution.py:10
  72.3 0.0 copy-done.3
  72.3 8.0 %mul.65 = bf16[56,128,12,128]{1,0,3,2:T(8,128)(2,1)} broadcast(bf16[56,12]{0,1:T(8,128)(2,1)S(1)} %copy-done.3), dimensions={0,2} | broadcast | bytes 22021440 | tf_op jit(solution)/shard_map/mul | solution.py:18
  80.4 18.5 %fusion.19 = (bf16[128,1536]{1,0:T(8,128)(2,1)}, bf16[128,1536]{1,0:T(8,128)(2,1)}, bf16[128,1536]{1,0:T(8,128)(2,1)}) fusion(bf16[128,1536]{1,0:T(8,128)(2,1)S(1)} %copy-done.1, bf16[128,1536]{1,0:T(8,128)(2,1)S(1)} %copy-done.2, f32[1536]{0:T(1024)S(1)} %add_multiply_fusion.2, bf16[7168,1536]{0,1:T(8,128)(2,1)} %copy.10, ...), kind=kOutput, calls=%fused_computation.33 | convolution fusion | flops 2839412736 | bytes 51517440 | tf_op jit(solution)/shard_map/dot_general | solution.py:30
  98.9 0.0 all-gather.5.cloned.1.call-update
  98.9 2.8 %copy.30 = bf16[16,4,8,1792]{3,2,0,1:T(8,128)(2,1)} copy(bf16[16,4,8,1792]{3,2,1,0:T(8,128)(2,1)} %bitcast.34) | data formatting | bytes 3670016 | tf_op jit(solution)/shard_map/all_to_all | solution.py:43
  101.8 3.6 %all-to-all-start = ((bf16[128,4,1792]{2,0,1:T(8,128)(2,1)}), bf16[128,4,1792]{2,0,1:T(8,128)(2,1)S(1)}, u32[]{:S(2)}, u32[]{:S(2)}) async-start(bf16[128,4,1792]{2,0,1:T(8,128)(2,1)} %bitcast.33), calls=%async_computation | async-start | bytes 3670016 | tf_op jit(solution)/shard_map/all_to_all | solution.py:43
  105.4 30.5 %all-to-all-done = bf16[128,4,1792]{2,0,1:T(8,128)(2,1)S(1)} async-done(((bf16[128,4,1792]{2,0,1:T(8,128)(2,1)}), bf16[128,4,1792]{2,0,1:T(8,128)(2,1)S(1)}, u32[]{:S(2)}, u32[]{:S(2)}) %all-to-all-start) | async-done | bytes 1835040 | tf_op jit(solution)/shard_map/all_to_all | solution.py:43
  135.9 63.6 %while.14 = (s32[]{:T(128)}, f32[1792,1536]{1,0:T(8,128)}, bf16[512,1792]{1,0:T(8,128)(2,1)S(1)}, bf16[512,1536]{1,0:T(8,128)(2,1)}, s32[]{:T(128)}, /*index=5*/s32[]{:T(128)}, s32[]{:T(128)}, s32[]{:T(128)}) while((s32[]{:T(128)}, f32[1792,1536]{1,0:T(8,128)}, bf16[512,1792]{1,0:T(8,128)(2,1)S(1)}, bf16[512,1536]{1,0:T(8,128)(2,1)}, ...), condition=%wide.region_4.0_spmd.clone, body=%wide.region_3.0_spmd.clone.sunk | while | flops 715653120 | bytes 33883276 | solution.py:59
  135.9 5.1 %convolution_convert_fusion.2 = bf16[1792,1536]{1,0:T(8,128)(2,1)} fusion(bf16[512,1792]{1,0:T(8,128)(2,1)S(1)} %get-tuple-element.154, s32[]{:T(128)S(6)} %select_n.10, bf16[512,1536]{1,0:T(8,128)(2,1)} %get-tuple-element.155), kind=kOutput, calls=%fused_computation.1.clone.1 | convolution fusion | flops 707395584 | bytes 6358016 | tf_op jit(solution)/shard_map/while/body/eval_jaxpr/dot_general | solution.py:53
  141.0 8.5 %select_add_fusion.2 = f32[1792,1536]{1,0:T(8,128)} fusion(f32[1792,1536]{1,0:T(8,128)} %get-tuple-element.145, bf16[1792,1536]{1,0:T(8,128)(2,1)} %convolution_convert_fusion.2, pred[]{:T(512)S(6)} %compare.3), kind=kLoop, calls=%fused_computation.clone.1 | loop fusion | flops 8257536 | bytes 27525120 | tf_op jit(solution)/shard_map/while/body/eval_jaxpr/add | solution.py:57
  149.5 5.1 %convolution_convert_fusion.2 = bf16[1792,1536]{1,0:T(8,128)(2,1)} fusion(bf16[512,1792]{1,0:T(8,128)(2,1)S(1)} %get-tuple-element.154, s32[]{:T(128)S(6)} %select_n.10, bf16[512,1536]{1,0:T(8,128)(2,1)} %get-tuple-element.155), kind=kOutput, calls=%fused_computation.1.clone.1 | convolution fusion | flops 707395584 | bytes 6358016 | tf_op jit(solution)/shard_map/while/body/eval_jaxpr/dot_general | solution.py:53
  154.6 11.6 %select_add_fusion.2 = f32[1792,1536]{1,0:T(8,128)} fusion(f32[1792,1536]{1,0:T(8,128)} %get-tuple-element.145, bf16[1792,1536]{1,0:T(8,128)(2,1)} %convolution_convert_fusion.2, pred[]{:T(512)S(6)} %compare.3), kind=kLoop, calls=%fused_computation.clone.1 | loop fusion | flops 8257536 | bytes 27525120 | tf_op jit(solution)/shard_map/while/body/eval_jaxpr/add | solution.py:57
  166.2 5.1 %convolution_convert_fusion.2 = bf16[1792,1536]{1,0:T(8,128)(2,1)} fusion(bf16[512,1792]{1,0:T(8,128)(2,1)S(1)} %get-tuple-element.154, s32[]{:T(128)S(6)} %select_n.10, bf16[512,1536]{1,0:T(8,128)(2,1)} %get-tuple-element.155), kind=kOutput, calls=%fused_computation.1.clone.1 | convolution fusion | flops 707395584 | bytes 6358016 | tf_op jit(solution)/shard_map/while/body/eval_jaxpr/dot_general | solution.py:53
  171.2 11.6 %select_add_fusion.2 = f32[1792,1536]{1,0:T(8,128)} fusion(f32[1792,1536]{1,0:T(8,128)} %get-tuple-element.145, bf16[1792,1536]{1,0:T(8,128)(2,1)} %convolution_convert_fusion.2, pred[]{:T(512)S(6)} %compare.3), kind=kLoop, calls=%fused_computation.clone.1 | loop fusion | flops 8257536 | bytes 27525120 | tf_op jit(solution)/shard_map/while/body/eval_jaxpr/add | solution.py:57
  182.9 5.1 %convolution_convert_fusion.2 = bf16[1792,1536]{1,0:T(8,128)(2,1)} fusion(bf16[512,1792]{1,0:T(8,128)(2,1)S(1)} %get-tuple-element.154, s32[]{:T(128)S(6)} %select_n.10, bf16[512,1536]{1,0:T(8,128)(2,1)} %get-tuple-element.155), kind=kOutput, calls=%fused_computation.1.clone.1 | convolution fusion | flops 707395584 | bytes 6358016 | tf_op jit(solution)/shard_map/while/body/eval_jaxpr/dot_general | solution.py:53
  187.9 11.6 %select_add_fusion.2 = f32[1792,1536]{1,0:T(8,128)} fusion(f32[1792,1536]{1,0:T(8,128)} %get-tuple-element.145, bf16[1792,1536]{1,0:T(8,128)(2,1)} %convolution_convert_fusion.2, pred[]{:T(512)S(6)} %compare.3), kind=kLoop, calls=%fused_computation.clone.1 | loop fusion | flops 8257536 | bytes 27525120 | tf_op jit(solution)/shard_map/while/body/eval_jaxpr/add | solution.py:57
  199.5 7.3 %convert_element_type.82 = bf16[1792,1536]{1,0:T(8,128)(2,1)} convert(f32[1792,1536]{1,0:T(8,128)} %get-tuple-element.82) | non-fusion elementwise | flops 2752512 | bytes 16515072 | tf_op jit(solution)/shard_map/convert_element_type | solution.py:60
  (8 shorter events, 0.0 us)
Async XLA Ops:
  7.2 52.0 %all-gather.3.cloned.1.call-start = ((), (), s32[]{:S(2)}) async-start(), calls=%async_computation.1 | async-start | bytes 2064384 | tf_op jit(solution)/shard_map/all_gather | solution.py:21
  7.9 28.9 %copy-start.1 = (bf16[128,1536]{1,0:T(8,128)(2,1)S(1)}, bf16[128,1536]{1,0:T(8,128)(2,1)}, u32[]{:S(2)}) copy-start(bf16[128,1536]{1,0:T(8,128)(2,1)} %param.8) | copy-start | bytes 1179652
  7.9 28.9 %copy-start.2 = (bf16[128,1536]{1,0:T(8,128)(2,1)S(1)}, bf16[128,1536]{1,0:T(8,128)(2,1)}, u32[]{:S(2)}) copy-start(bf16[128,1536]{1,0:T(8,128)(2,1)} %param.9) | copy-start | bytes 1179652
  7.9 128.0 %all-gather.5.cloned.1.call-start = ((), (), s32[]{:S(2)}) async-start(), calls=%async_computation.2 | async-start | bytes 1966080 | tf_op jit(solution)/shard_map/all_gather | solution.py:45
  66.9 5.5 %copy-start.3 = (bf16[56,12]{0,1:T(8,128)(2,1)S(1)}, bf16[56,12]{0,1:T(8,128)(2,1)}, u32[]{:S(2)}) copy-start(bf16[56,12]{0,1:T(8,128)(2,1)} %param.11) | copy-start | bytes 4036
  72.3 8.0 %copy-start = (bf16[128,7168]{1,0:T(8,128)(2,1)S(1)}, bf16[128,7168]{1,0:T(8,128)(2,1)}, u32[]{:S(2)}) copy-start(bf16[128,7168]{1,0:T(8,128)(2,1)} %all-gather.3.cloned.1.call-done) | copy-start | bytes 5505028
  101.8 34.2 %all-to-all-start = ((bf16[128,4,1792]{2,0,1:T(8,128)(2,1)}), bf16[128,4,1792]{2,0,1:T(8,128)(2,1)S(1)}, u32[]{:S(2)}, u32[]{:S(2)}) async-start(bf16[128,4,1792]{2,0,1:T(8,128)(2,1)} %bitcast.33), calls=%async_computation | async-start | bytes 3670016 | tf_op jit(solution)/shard_map/all_to_all | solution.py:43
Sparse Core Ops, SparseCore 0:
  10.2 48.9 all-gather.2
  99.1 26.7 all-gather.4
where the time goes:
time: 215 us; the launch traced here: 214 us
  other arithmetic  59.2 us (28%)
  waiting for transfers between devices  53.3 us (25%)
  local copies, waits for them, and re-layouts  44.6 us (21%)
  matrix products  38.8 us (18%)
  between operations  14.1 us (7%)
  starting transfers between devices  3.68 us (2%)
    add x4, other arithmetic, one_block(): return inner + term  43.4 us
    unnamed x10, local copies, waits for them, and re-layouts  31.4 us
    all_to_all x1, waiting for transfers between devices, per_device(): lax.all_to_all(grad_colq, 'dp', split_axis=1, concat_axis=0, tiled=True)  30.5 us
    all_gather x1, waiting for transfers between devices, per_device(): grad_tokens = lax.all_gather(out_grad, 'tp', axis=0, tiled=True)  22 us
    dot_general x4, matrix products, one_block(): lax.dot_general(grad_block, hidden_block, (((0,), (0,)), ((), ())), prefe...  20.2 us
    dot_general x1, matrix products, per_device(): jnp.dot(grad_rowq, weight_deq, preferred_element_type=jnp.float32)  18.5 us
    mul x1, local copies, waits for them, and re-layouts, per_device(): down_weight.reshape(width // 128, 128, hidden_units // 128, 128)  8.02 us
    convert_element_type x1, other arithmetic, per_device(): return (gate_grad, up_grad, summed.astype(jnp.bfloat16))  7.25 us
  transfers between devices with their start and end apart: 3, of which 2 were waited for; matrix products, arithmetic and copies ran while one was open for 15% of the time, Pallas kernels for 0%

commit v1 on v0

--- a/solution.py
+++ b/solution.py
@@ -1,7 +1,14 @@
 import jax
 import jax.numpy as jnp
 from jax import lax
+from jax.experimental import pallas as pl
+from jax.experimental.pallas import tpu as pltpu
 from jax.sharding import PartitionSpec as P
+
+BF16 = jnp.bfloat16
+F32 = jnp.float32
+BOTH = ("dp", "tp")
+TILE = 128
 
 
 def tile_quant(values, tile_axis):
@@ -11,7 +18,14 @@
     return (payload.astype(jnp.float32) * tile_scale).astype(jnp.bfloat16)
 
 
-def per_device(out_grad, gate_pre, up_pre, down_weight, block_scales):
+def fast_quant(values, tile_axis):
+    largest = jnp.max(jnp.abs(values), axis=tile_axis, keepdims=True)
+    tile_scale = (largest + 1e-06) / 448.0
+    payload = (values * (1.0 / tile_scale)).astype(BF16)
+    return (payload.astype(F32) * tile_scale).astype(BF16)
+
+
+def any_mesh(out_grad, gate_pre, up_pre, down_weight, block_scales):
     width = down_weight.shape[0]
     hidden_units = down_weight.shape[1]
     weight_deq = (
@@ -60,7 +74,311 @@
     return (gate_grad, up_grad, summed.astype(jnp.bfloat16))
 
 
+def whole(shape):
+    return pl.BlockSpec(shape, lambda *_: (0,) * len(shape))
+
+
+def split_columns(table, out_grad, parts):
+    rows, width = out_grad.shape
+    part = width // parts
+
+    def body(table_ref, grad_ref, *outs):
+        for j, out in enumerate(outs):
+            start = pl.multiple_of((table_ref[0] ^ j) * part, TILE)
+            out[...] = grad_ref[:, pl.ds(start, part)]
+
+    return pl.pallas_call(
+        body,
+        name="split_columns",
+        out_shape=[jax.ShapeDtypeStruct((rows, part), BF16)] * parts,
+        grid_spec=pltpu.PrefetchScalarGridSpec(
+            num_scalar_prefetch=1,
+            grid=(1,),
+            in_specs=[whole((rows, width))],
+            out_specs=[whole((rows, part))] * parts,
+        ),
+    )(table, out_grad)
+
+
+def hidden_quant(gate_pre, up_pre):
+    tokens, units = gate_pre.shape
+    block = units // 2 if units % 256 == 0 else units
+
+    def body(gate_ref, up_ref, out_ref):
+        gate = gate_ref[...].astype(F32)
+        sigma = 1.0 / (1.0 + jnp.exp(-gate))
+        out_ref[...] = fast_quant(gate * sigma * up_ref[...].astype(F32), 0)
+
+    spec = pl.BlockSpec((tokens, block), lambda i: (0, i))
+    return pl.pallas_call(
+        body,
+        name="hidden_quant",
+        out_shape=jax.ShapeDtypeStruct((tokens, units), BF16),
+        grid=(units // block,),
+        in_specs=[spec, spec],
+        out_specs=spec,
+        cost_estimate=pl.CostEstimate(flops=20 * tokens * units, bytes_accessed=6 * tokens * units, transcendentals=tokens * units),
+    )(gate_pre, up_pre)
+
+
+def partial_hidden(table, pieces_p, pieces_q, down_weight, scales, step):
+    count = len(pieces_p)
+    rows2, part = pieces_p[0].shape
+    rows = rows2 // 2
+    units = down_weight.shape[1]
+    total = 4 * count * rows
+    each = count * rows
+
+    def body(table_ref, scale_ref, *refs):
+        p_refs, q_refs = refs[:count], refs[count : 2 * count]
+        weight_ref = refs[2 * count]
+        outs = refs[2 * count + 1 : 2 * count + 5]
+        quant_ref = refs[2 * count + 5]
+        at = pl.program_id(0)
+
+        @pl.when(at == 0)
+        def _():
+            for half, group in enumerate((p_refs, q_refs)):
+                for k, ref in enumerate(group):
+                    for c in range(part // TILE):
+                        cols = slice(c * TILE, (c + 1) * TILE)
+                        deq = fast_quant(ref[:, cols].astype(F32), 1)
+                        for s in range(2):
+                            base = (2 * half + s) * each + k * rows
+                            quant_ref[base : base + rows, cols] = deq[s * rows : (s + 1) * rows]
+
+        row0 = table_ref[0] * (part // TILE)
+        col0 = at * (step // TILE)
+        blocks = []
+        for a in range(part // TILE):
+            line = []
+            for b in range(step // TILE):
+                scale = jnp.full((TILE, TILE), scale_ref[row0 + a, col0 + b], F32).astype(BF16)
+                line.append(
+                    weight_ref[a * TILE : (a + 1) * TILE, b * TILE : (b + 1) * TILE] * scale
+                )
+            blocks.append(jnp.concatenate(line, axis=1))
+        weight = jnp.concatenate(blocks, axis=0)
+        result = jnp.dot(quant_ref[...], weight, preferred_element_type=F32)
+        for j, out in enumerate(outs):
+            out[...] = result[j * each : (j + 1) * each].astype(out.dtype)
+
+    return pl.pallas_call(
+        body,
+        name="partial_hidden",
+        out_shape=[jax.ShapeDtypeStruct((each, units), BF16)] * 4,
+        grid_spec=pltpu.PrefetchScalarGridSpec(
+            num_scalar_prefetch=2,
+            grid=(units // step,),
+            in_specs=[whole((rows2, part))] * (2 * count)
+            + [pl.BlockSpec((part, step), lambda i, tab, sc: (tab[0], i))],
+            out_specs=[pl.BlockSpec((each, step), lambda i, tab, sc: (0, i))] * 4,
+            scratch_shapes=[pltpu.VMEM((total, part), BF16)],
+        ),
+        compiler_params=pltpu.CompilerParams(vmem_limit_bytes=40 * 1024 * 1024),
+        cost_estimate=pl.CostEstimate(flops=2 * total * part * units, bytes_accessed=2 * part * units, transcendentals=0),
+    )(table, scales, *pieces_p, *pieces_q, down_weight)
+
+
+def down_product(table, pieces_p, pieces_q, hiddens, step):
+    count = len(pieces_p)
+    rows2, part = pieces_p[0].shape
+    rows = rows2 // 2
+    tokens, units = hiddens[0].shape
+
+    def body(table_ref, *refs):
+        p_refs, q_refs = refs[:count], refs[count : 2 * count]
+        h_refs = refs[2 * count : 2 * count + 4]
+        out_ref = refs[2 * count + 4]
+        hid_ref, quant_ref = refs[2 * count + 5 :]
+        at = pl.program_id(0)
+
+        @pl.when(at == 0)
+        def _():
+            for j, ref in enumerate(h_refs):
+                hid_ref[j * tokens : (j + 1) * tokens, :] = ref[...]
+
+        cols = pl.ds(pl.multiple_of(at * step, TILE), step)
+        for j in range(4):
+            group = (p_refs, q_refs)[j // 2]
+            low = (j % 2) * rows
+            vals = [ref[low : low + rows, cols].astype(F32) for ref in group]
+            top = jnp.abs(vals[0])
+            for v in vals[1:]:
+                top = jnp.maximum(top, jnp.abs(v))
+            scale = (jnp.max(top, axis=0, keepdims=True) + 1e-06) / 448.0
+            inverse = 1.0 / scale
+            for k, v in enumerate(vals):
+                payload = (v * inverse).astype(BF16)
+                start = pl.multiple_of(j * tokens + table_ref[1 + k], rows)
+                quant_ref[pl.ds(start, rows), :] = (payload.astype(F32) * scale).astype(BF16)
+        out_ref[...] = lax.dot_general(
+            quant_ref[...], hid_ref[...], (((0,), (0,)), ((), ())), preferred_element_type=F32
+        ).astype(BF16)
+
+    return pl.pallas_call(
+        body,
+        name="down_product",
+        out_shape=jax.ShapeDtypeStruct((part, units), BF16),
+        grid_spec=pltpu.PrefetchScalarGridSpec(
+            num_scalar_prefetch=1,
+            grid=(part // step,),
+            in_specs=[whole((rows2, part))] * (2 * count) + [whole((tokens, units))] * 4,
+            out_specs=pl.BlockSpec((step, units), lambda i, tab: (i, 0)),
+            scratch_shapes=[pltpu.VMEM((4 * tokens, units), BF16), pltpu.VMEM((4 * tokens, step), BF16)],
+        ),
+        compiler_params=pltpu.CompilerParams(vmem_limit_bytes=40 * 1024 * 1024),
+        cost_estimate=pl.CostEstimate(flops=8 * part * tokens * units, bytes_accessed=2 * part * units, transcendentals=0),
+    )(table, *pieces_p, *pieces_q, *hiddens)
+
+
+def last_step(table, gate_pre, up_pre, groups):
+    tokens, units = gate_pre.shape
+    sizes = [len(g) for g in groups]
+    flat = [a for g in groups for a in g]
+    lengths = [g[0].shape[0] for g in groups]
+    block = units // 2 if units % 256 == 0 else units
+
+    def body(table_ref, gate_ref, up_ref, *refs):
+        ins, (gate_out, up_out) = refs[:-2], refs[-2:]
+        rows = tokens // (table.shape[0] - 1)
+        at = piece = 0
+        for size, length in zip(sizes, lengths):
+            for first in range(0, length, rows):
+                where = pl.ds(pl.multiple_of(table_ref[1 + piece], rows), rows)
+                grad = ins[at][first : first + rows, :].astype(F32)
+                for ref in ins[at + 1 : at + size]:
+                    grad = grad + ref[first : first + rows, :].astype(F32)
+                gate = gate_ref[where, :].astype(F32)
+                up = up_ref[where, :].astype(F32)
+                sigma = 1.0 / (1.0 + jnp.exp(-gate))
+                gate_out[where, :] = (grad * up * sigma * (1.0 + gate * (1.0 - sigma))).astype(BF16)
+                up_out[where, :] = (grad * gate * sigma).astype(BF16)
+                piece += 1
+            at += size
+
+    spec = pl.BlockSpec((tokens, block), lambda i, tab: (0, i))
+    return pl.pallas_call(
+        body,
+        name="last_step",
+        out_shape=[jax.ShapeDtypeStruct((tokens, units), BF16)] * 2,
+        grid_spec=pltpu.PrefetchScalarGridSpec(
+            num_scalar_prefetch=1,
+            grid=(units // block,),
+            in_specs=[spec, spec]
+            + [pl.BlockSpec((a.shape[0], block), lambda i, tab: (0, i)) for a in flat],
+            out_specs=[spec, spec],
+        ),
+        cost_estimate=pl.CostEstimate(flops=20 * tokens * units, bytes_accessed=12 * tokens * units, transcendentals=tokens * units),
+    )(table, gate_pre, up_pre, *flat)
+
+
+def fold(own, received):
+    return (own[0].astype(F32) + received[0].astype(F32)), (
+        own[1].astype(F32) + received[1].astype(F32)
+    ).astype(BF16)
+
+
+def ring_place(index, count):
+    return jnp.where(index % 2 == 0, index // 2, count - 1 - index // 2)
+
+
+def ring_index(place, count):
+    return jnp.where(place < count // 2, 2 * place, 2 * (count - 1 - place) + 1)
+
+
+def pair_mesh(n_tp, out_grad, gate_pre, up_pre, down_weight, block_scales):
+    rows = out_grad.shape[0]
+    half = n_tp // 2
+    order = [2 * i for i in range(half)] + [2 * (n_tp - 1 - i) + 1 for i in range(half, n_tp)]
+    up = {order[i]: order[(i + 1) % n_tp] for i in range(n_tp)}
+    down = {v: k for k, v in up.items()}
+
+    def permute(value, target):
+        pairs = []
+        for d in range(4):
+            for t in range(n_tp):
+                dd, tt = target(d, t)
+                pairs.append((d * n_tp + t, dd * n_tp + tt))
+        return lax.ppermute(value, BOTH, pairs)
+
+    def flip(value, bits):
+        return permute(value, lambda d, t: (d ^ bits, t))
+
+    def send_up(value):
+        return permute(value, lambda d, t: (d, up[t]))
+
+    def send_down(value):
+        return permute(value, lambda d, t: (d, down[t]))
+
+    offsets = [0]
+    for k in range(1, half):
+        offsets += [-k, k]
+    offsets.append(half)
+    place = ring_place(lax.axis_index("tp"), n_tp)
+    sources = ring_index((place + jnp.array(offsets, jnp.int32)) % n_tp, n_tp)
+    table = jnp.concatenate(
+        [lax.axis_index("dp").reshape(1), sources * rows]
+    ).astype(jnp.int32)
+    scales = block_scales.astype(F32)
+
+    parts = split_columns(table, out_grad, 4)
+    from_core = flip(parts[1], 1)
+    from_chip = flip(parts[2], 2)
+    from_far = flip(parts[3], 3)
+    hidden_own = hidden_quant(gate_pre, up_pre)
+    block_p = jnp.concatenate([parts[0], from_core], axis=0)
+    block_q = jnp.concatenate([from_chip, from_far], axis=0)
+
+    pieces_p, pieces_q = {0: block_p}, {0: block_q}
+    for k in range(1, half + 1):
+        pieces_p[-k] = send_up(pieces_p[1 - k])
+        if k < half:
+            pieces_p[k] = send_down(pieces_p[k - 1])
+            pieces_q[-k] = send_up(pieces_q[1 - k])
+        pieces_q[k] = send_down(pieces_q[k - 1])
+    pieces_p[half] = pieces_p[-half]
+    list_p = [pieces_p[o] for o in offsets]
+    list_q = [pieces_q[o] for o in offsets]
+
+    hidden_chip = flip(hidden_own, 2)
+    hidden_core = flip(hidden_own, 1)
+    hidden_far = flip(hidden_chip, 1)
+
+    first = n_tp - 3
+    groups = []
+    part1 = partial_hidden(table, list_p[:first], list_q[:first], down_weight, scales, 256)
+    got0, got2 = flip(part1[1], 1), flip(part1[3], 1)
+    sum0, sum2 = fold((part1[0], part1[2]), (got0, got2))
+    groups.append([sum0, flip(sum2, 2)])
+    part2 = partial_hidden(table, list_p[first:], list_q[first:], down_weight, scales, 256)
+    groups.append([part2[0]] + [flip(part2[j], j) for j in (1, 2, 3)])
+    down_grad = down_product(
+        table, list_p, list_q, [hidden_own, hidden_core, hidden_chip, hidden_far], 256
+    )
+    gate_grad, up_grad = last_step(table, gate_pre, up_pre, groups)
+    return gate_grad, up_grad, down_grad
+
+
 def solution(mesh):
+    n_dp, n_tp = mesh.shape["dp"], mesh.shape["tp"]
+
+    def per_device(out_grad, gate_pre, up_pre, down_weight, block_scales):
+        part = down_weight.shape[0] // n_dp
+        rows = out_grad.shape[0]
+        fits = (
+            n_dp == 4
+            and n_tp >= 4
+            and n_tp % 2 == 0
+            and rows % 16 == 0
+            and rows * n_tp == 128
+            and part % 256 == 0
+            and gate_pre.shape[1] % 256 == 0
+        )
+        if fits:
+            return pair_mesh(n_tp, out_grad, gate_pre, up_pre, down_weight, block_scales)
+        return any_mesh(out_grad, gate_pre, up_pre, down_weight, block_scales)
+
     placed = (P(("dp", "tp"), None), P("dp", "tp"), P("dp", "tp"), P(None, "tp"), P(None, "tp"))
     return jax.shard_map(
         per_device,

time: 215 us -> 78 us (0.36)
  other arithmetic: 59.2 us -> 2.18 us
  local copies, waits for them, and re-layouts: 44.6 us -> 2.95 us
  matrix products: 38.8 us -> 0 us
  waiting for transfers between devices: 53.3 us -> 20.6 us
  Pallas kernels: 0 us -> 29.3 us
  starting transfers between devices: 3.68 us -> 21.6 us
  between operations: 14.1 us -> 0.76 us
    add x4 -> x1, other arithmetic: 43.4 us -> 0.84 us  [fold(): own[0].astype(F32) + received[0].astype(F32)]
    dot_general x5 -> x0, matrix products: 38.8 us -> none  [the longest x4 20.2 us: one_block(): lax.dot_general(grad_block, hidden_block, (((0,), (0,)), ((), ())), prefe...]
    all_to_all x1 -> x0, waiting for transfers between devices: 30.5 us -> none  [per_device(): lax.all_to_all(grad_colq, 'dp', split_axis=1, concat_axis=0, tiled=True)]
    pallas_call x0 -> x6, Pallas kernels: none -> 29.3 us  [the longest x2 14.5 us: partial_hidden(): pl.pallas_call(body, name='partial_hidden', out_shape=[jax.ShapeDtypeStru...]
    unnamed x10 -> x17, local copies, waits for them, and re-layouts: 31.4 us -> 2.94 us
    all_gather x2 -> x0, waiting for transfers between devices: 22 us -> none  [the longest x1 22 us: per_device(): grad_tokens = lax.all_gather(out_grad, 'tp', axis=0, tiled=True)]
    ppermute x0 -> x26, starting transfers between devices: none -> 21.6 us  [permute(): return lax.ppermute(value, BOTH, pairs)]
    ppermute x0 -> x26, waiting for transfers between devices: none -> 20.6 us  [permute(): return lax.ppermute(value, BOTH, pairs)]
  transfers between devices with their start and end apart: 3 -> 26, of which waited for: 2 -> 10; matrix products, arithmetic and copies ran while one was open for 15% -> 3% of each run, Pallas kernels for 0% -> 26%
where the time goes in v1:
time: 78 us; the launch traced here: 77.4 us
  Pallas kernels  29.3 us (38%)
  starting transfers between devices  21.6 us (28%)
  waiting for transfers between devices  20.6 us (26%)
  local copies, waits for them, and re-layouts  2.95 us (4%)
  other arithmetic  2.18 us (3%)
    ppermute x26, starting transfers between devices, permute(): return lax.ppermute(value, BOTH, pairs)  21.6 us
    ppermute x26, waiting for transfers between devices, permute(): return lax.ppermute(value, BOTH, pairs)  20.6 us
    pallas_call x2, Pallas kernels, partial_hidden(): pl.pallas_call(body, name='partial_hidden', out_shape=[jax.ShapeDtypeStru...  14.5 us
    pallas_call x1, Pallas kernels, down_product(): pl.pallas_call(body, name='down_product', out_shape=jax.ShapeDtypeStruct(...  7.11 us
    pallas_call x1, Pallas kernels, last_step(): pl.pallas_call(body, name='last_step', out_shape=[jax.ShapeDtypeStruct((t...  3.33 us
    unnamed x17, local copies, waits for them, and re-layouts  2.94 us
    pallas_call x1, Pallas kernels, split_columns(): pl.pallas_call(body, name='split_columns', out_shape=[jax.ShapeDtypeStruc...  2.29 us
    pallas_call x1, Pallas kernels, hidden_quant(): pl.pallas_call(body, name='hidden_quant', out_shape=jax.ShapeDtypeStruct(...  2.14 us
  transfers between devices with their start and end apart: 26, of which 10 were waited for; matrix products, arithmetic and copies ran while one was open for 3% of the time, Pallas kernels for 26%

profile of v1, /device:TPU:0, one launch (start us, length us, event | category | flops | bytes accessed | tf_op | source)
XLA Modules:
  0.0 77.4 jit_solution(7625772761764954362)
XLA Ops:
  0.7 0.7 fusion.1
  1.3 0.6 pad_add_fusion.table_ref
  1.9 2.3 %split_columns.1 = (bf16[16,1792]{1,0:T(8,128)(2,1)}, bf16[16,1792]{1,0:T(8,128)(2,1)}, bf16[16,1792]{1,0:T(8,128)(2,1)}, bf16[16,1792]{1,0:T(8,128)(2,1)}) custom-call(s32[9]{0:T(128)} %pad_add_fusion.table_ref, bf16[16,7168]{1,0:T(8,128)(2,1)} %grad_ref.1), custom_call_target="tpu_custom_call" | custom-call | tf_op jit(solution)/shard_map/split_columns/pallas_call | solution.py:90
  4.2 2.9 %collective-permute-start.5 = (bf16[16,1792]{1,0:T(8,128)(2,1)}, bf16[16,1792]{1,0:T(8,128)(2,1)S(1)}, u32[]{:S(2)}, u32[]{:S(2)}) collective-permute-start(bf16[16,1792]{1,0:T(8,128)(2,1)} %get-tuple-element.19), channel_id=1, source_target_pairs={{0,16},{1,17},{2,18},{3,19},{4,20},{5,21},{6,22},{7,23},{8,24},{9,... | collective-permute-start | bytes 172040 | tf_op jit(solution)/shard_map/ppermute | solution.py:303
  7.3 0.8 %constant_dynamic-update-slice_fusion.1 = bf16[32,1792]{1,0:T(8,128)(2,1)S(1)} fusion(bf16[16,1792]{1,0:T(8,128)(2,1)} %get-tuple-element.17), kind=kLoop, calls=%fused_computation.3 | loop fusion | bytes 114688
  8.1 1.4 %collective-permute-done.5 = bf16[16,1792]{1,0:T(8,128)(2,1)S(1)} collective-permute-done((bf16[16,1792]{1,0:T(8,128)(2,1)}, bf16[16,1792]{1,0:T(8,128)(2,1)S(1)}, u32[]{:S(2)}, u32[]{:S(2)}) %collective-permute-start.5) | collective-permute-done | bytes 57376 | tf_op jit(solution)/shard_map/ppermute | solution.py:303
  9.5 1.8 %collective-permute-done.6 = bf16[16,1792]{1,0:T(8,128)(2,1)S(1)} collective-permute-done((bf16[16,1792]{1,0:T(8,128)(2,1)}, bf16[16,1792]{1,0:T(8,128)(2,1)S(1)}, u32[]{:S(2)}, u32[]{:S(2)}) %collective-permute-start.6) | collective-permute-done | bytes 57376 | tf_op jit(solution)/shard_map/ppermute | solution.py:303
  11.3 1.5 %collective-permute-start.8 = (bf16[32,1792]{1,0:T(8,128)(2,1)S(1)}, bf16[32,1792]{1,0:T(8,128)(2,1)S(1)}, u32[]{:S(2)}, u32[]{:S(2)}) collective-permute-start(bf16[32,1792]{1,0:T(8,128)(2,1)S(1)} %constant_dynamic-update-slice_fusion.2.refs_5_.refs_8_), channel_id=1, source_target_pairs={{0,1},{1,3},{2,0},{3,5},{4,2},{5,7},{6,4},{7,6},{8,9},{9,11},{10,8... | collective-permute-start | bytes 344072 | tf_op jit(solution)/shard_map/ppermute | solution.py:303
  13.4 1.6 %collective-permute-start.7 = (bf16[32,1792]{1,0:T(8,128)(2,1)S(1)}, bf16[32,1792]{1,0:T(8,128)(2,1)S(1)}, u32[]{:S(2)}, u32[]{:S(2)}) collective-permute-start(bf16[32,1792]{1,0:T(8,128)(2,1)S(1)} %constant_dynamic-update-slice_fusion.2.refs_5_.refs_8_), channel_id=1, source_target_pairs={{0,2},{1,0},{2,4},{3,1},{4,6},{5,3},{6,7},{7,5},{8,10},{9,8},{10,1... | collective-permute-start | bytes 344072 | tf_op jit(solution)/shard_map/ppermute | solution.py:303
  15.4 2.1 %hidden_quant.1.refs_16_ = bf16[128,1536]{1,0:T(8,128)(2,1)} custom-call(bf16[128,1536]{1,0:T(8,128)(2,1)} %gate_ref.3, bf16[128,1536]{1,0:T(8,128)(2,1)} %up_ref.3), custom_call_target="tpu_custom_call" | custom-call | flops 3932160 | bytes 1179648 | tf_op jit(solution)/shard_map/hidden_quant/pallas_call | solution.py:113
  18.0 2.0 %collective-permute-start.10 = (bf16[32,1792]{1,0:T(8,128)(2,1)S(1)}, bf16[32,1792]{1,0:T(8,128)(2,1)S(1)}, u32[]{:S(2)}, u32[]{:S(2)}) collective-permute-start(bf16[32,1792]{1,0:T(8,128)(2,1)S(1)} %collective-permute-done.8.refs_7_.refs_10_), channel_id=1, source_target_pairs={{0,1},{1,3},{2,0},{3,5},{4,2},{5,7},{6,4},{7,6},{8,9},{9,11},{10,8... | collective-permute-start | bytes 344072 | tf_op jit(solution)/shard_map/ppermute | solution.py:303
  20.1 2.0 %collective-permute-start.9 = (bf16[32,1792]{1,0:T(8,128)(2,1)S(1)}, bf16[32,1792]{1,0:T(8,128)(2,1)S(1)}, u32[]{:S(2)}, u32[]{:S(2)}) collective-permute-start(bf16[32,1792]{1,0:T(8,128)(2,1)S(1)} %collective-permute-done.7.refs_6_.refs_9_), channel_id=1, source_target_pairs={{0,2},{1,0},{2,4},{3,1},{4,6},{5,3},{6,7},{7,5},{8,10},{9,8},{10,1... | collective-permute-start | bytes 344072 | tf_op jit(solution)/shard_map/ppermute | solution.py:303
  22.2 0.8 %copy.9 = bf16[56,12]{1,0:T(8,128)(2,1)S(1)} copy(bf16[56,12]{0,1:T(8,128)(2,1)} %param.10) | data formatting | bytes 2688 | tf_op args[4]
  23.3 2.5 %collective-permute-start.18 = (bf16[32,1792]{1,0:T(8,128)(2,1)S(1)}, bf16[32,1792]{1,0:T(8,128)(2,1)S(1)}, u32[]{:S(2)}, u32[]{:S(2)}) collective-permute-start(bf16[32,1792]{1,0:T(8,128)(2,1)S(1)} %collective-permute-done.10.refs_9_.refs_12_), channel_id=1, source_target_pairs={{0,1},{1,3},{2,0},{3,5},{4,2},{5,7},{6,4},{7,6},{8,9},{9,11},{10,8... | collective-permute-start | bytes 344072 | tf_op jit(solution)/shard_map/ppermute | solution.py:303
  25.8 1.3 %collective-permute-done.9.refs_8_.refs_11_ = bf16[32,1792]{1,0:T(8,128)(2,1)S(1)} collective-permute-done((bf16[32,1792]{1,0:T(8,128)(2,1)S(1)}, bf16[32,1792]{1,0:T(8,128)(2,1)S(1)}, u32[]{:S(2)}, u32[]{:S(2)}) %collective-permute-start.9) | collective-permute-done | bytes 114720 | tf_op jit(solution)/shard_map/ppermute | solution.py:303
  27.1 0.6 copy-done.2
  27.7 7.6 %partial_hidden.2 = (bf16[80,1536]{1,0:T(8,128)(2,1)S(1)}, bf16[80,1536]{1,0:T(8,128)(2,1)S(1)}, bf16[80,1536]{1,0:T(8,128)(2,1)S(1)}, bf16[80,1536]{1,0:T(8,128)(2,1)S(1)}) custom-call(s32[9]{0:T(128)S(1)} %copy-done.2, f32[56,12]{1,0:T(8,128)S(1)} %convert_element_type.18.scale_ref, bf16[32,1792]{1,0:T(8,128)(2,1)S(1)} %constant_dynamic-update-slice_fusion.refs_0_, ...), custom_call_target="tpu_custom_call" | custom-call | flops 1761607680 | bytes 5505024 | tf_op jit(solution)/shard_map/partial_hidden/pallas_call | solution.py:166
  35.4 1.5 %collective-permute-start.17 = (bf16[32,1792]{1,0:T(8,128)(2,1)S(1)}, bf16[32,1792]{1,0:T(8,128)(2,1)S(1)}, u32[]{:S(2)}, u32[]{:S(2)}) collective-permute-start(bf16[32,1792]{1,0:T(8,128)(2,1)S(1)} %collective-permute-done.9.refs_8_.refs_11_), channel_id=1, source_target_pairs={{0,2},{1,0},{2,4},{3,1},{4,6},{5,3},{6,7},{7,5},{8,10},{9,8},{10,1... | collective-permute-start | bytes 344072 | tf_op jit(solution)/shard_map/ppermute | solution.py:303
  37.5 1.6 %collective-permute-start.19 = (bf16[32,1792]{1,0:T(8,128)(2,1)S(1)}, bf16[32,1792]{1,0:T(8,128)(2,1)S(1)}, u32[]{:S(2)}, u32[]{:S(2)}) collective-permute-start(bf16[32,1792]{1,0:T(8,128)(2,1)S(1)} %collective-permute-done.18.refs_4_.refs_14_), channel_id=1, source_target_pairs={{0,1},{1,3},{2,0},{3,5},{4,2},{5,7},{6,4},{7,6},{8,9},{9,11},{10,8... | collective-permute-start | bytes 344072 | tf_op jit(solution)/shard_map/ppermute | solution.py:303
  39.6 1.4 %collective-permute-done.17.refs_3_.refs_13_ = bf16[32,1792]{1,0:T(8,128)(2,1)S(1)} collective-permute-done((bf16[32,1792]{1,0:T(8,128)(2,1)S(1)}, bf16[32,1792]{1,0:T(8,128)(2,1)S(1)}, u32[]{:S(2)}, u32[]{:S(2)}) %collective-permute-start.17) | collective-permute-done | bytes 114720 | tf_op jit(solution)/shard_map/ppermute | solution.py:303
  41.0 1.9 %collective-permute-done.15.refs_1_.refs_6_ = bf16[32,1792]{1,0:T(8,128)(2,1)S(1)} collective-permute-done((bf16[32,1792]{1,0:T(8,128)(2,1)S(1)}, bf16[32,1792]{1,0:T(8,128)(2,1)S(1)}, u32[]{:S(2)}, u32[]{:S(2)}) %collective-permute-start.15) | collective-permute-done | bytes 114720 | tf_op jit(solution)/shard_map/ppermute | solution.py:303
  42.9 1.7 %collective-permute-done.19.refs_5_.refs_15_ = bf16[32,1792]{1,0:T(8,128)(2,1)S(1)} collective-permute-done((bf16[32,1792]{1,0:T(8,128)(2,1)S(1)}, bf16[32,1792]{1,0:T(8,128)(2,1)S(1)}, u32[]{:S(2)}, u32[]{:S(2)}) %collective-permute-start.19) | collective-permute-done | bytes 114720 | tf_op jit(solution)/shard_map/ppermute | solution.py:303
  44.6 6.8 %partial_hidden.3 = (bf16[48,1536]{1,0:T(8,128)(2,1)S(1)}, bf16[48,1536]{1,0:T(8,128)(2,1)S(1)}, bf16[48,1536]{1,0:T(8,128)(2,1)S(1)}, bf16[48,1536]{1,0:T(8,128)(2,1)S(1)}) custom-call(s32[9]{0:T(128)S(1)} %copy-done.2, f32[56,12]{1,0:T(8,128)S(1)} %convert_element_type.18.scale_ref, bf16[32,1792]{1,0:T(8,128)(2,1)S(1)} %collective-permute-done.14.refs_0_.refs_5_, ...), custom_call_target="tpu_custom_call" | custom-call | flops 1056964608 | bytes 5505024 | tf_op jit(solution)/shard_map/partial_hidden/pallas_call | solution.py:166
  52.0 1.1 %collective-permute-start.21 = (bf16[48,1536]{1,0:T(8,128)(2,1)S(1)}, bf16[48,1536]{1,0:T(8,128)(2,1)S(1)}, u32[]{:S(2)}, u32[]{:S(2)}) collective-permute-start(bf16[48,1536]{1,0:T(8,128)(2,1)S(1)} %get-tuple-element.27), channel_id=1, source_target_pairs={{0,16},{1,17},{2,18},{3,19},{4,20},{5,21},{6,22},{7,23},{8,24},{9,... | collective-permute-start | bytes 442376 | tf_op jit(solution)/shard_map/ppermute | solution.py:303
  53.6 1.1 %collective-permute-start.13 = (bf16[80,1536]{1,0:T(8,128)(2,1)S(1)}, bf16[80,1536]{1,0:T(8,128)(2,1)S(1)}, u32[]{:S(2)}, u32[]{:S(2)}) collective-permute-start(bf16[80,1536]{1,0:T(8,128)(2,1)S(1)} %add_convert_fusion), channel_id=1, source_target_pairs={{0,16},{1,17},{2,18},{3,19},{4,20},{5,21},{6,22},{7,23},{8,24},{9,... | collective-permute-start | bytes 737288 | tf_op jit(solution)/shard_map/ppermute | solution.py:303
  54.7 0.8 %convert_add_fusion.refs_0_ = f32[80,1536]{1,0:T(8,128)} fusion(bf16[80,1536]{1,0:T(8,128)(2,1)S(1)} %collective-permute-done.11, bf16[80,1536]{1,0:T(8,128)(2,1)S(1)} %get-tuple-element.21), kind=kLoop, calls=%fused_computation.1 | loop fusion | flops 368640 | bytes 983040 | tf_op jit(solution)/shard_map/add | solution.py:277
  55.6 3.1 %collective-permute-done.21.refs_4_ = bf16[48,1536]{1,0:T(8,128)(2,1)S(1)} collective-permute-done((bf16[48,1536]{1,0:T(8,128)(2,1)S(1)}, bf16[48,1536]{1,0:T(8,128)(2,1)S(1)}, u32[]{:S(2)}, u32[]{:S(2)}) %collective-permute-start.21) | collective-permute-done | bytes 147488 | tf_op jit(solution)/shard_map/ppermute | solution.py:303
  58.7 1.8 %collective-permute-done.22.refs_5_ = bf16[48,1536]{1,0:T(8,128)(2,1)S(1)} collective-permute-done((bf16[48,1536]{1,0:T(8,128)(2,1)S(1)}, bf16[48,1536]{1,0:T(8,128)(2,1)S(1)}, u32[]{:S(2)}, u32[]{:S(2)}) %collective-permute-start.22) | collective-permute-done | bytes 147488 | tf_op jit(solution)/shard_map/ppermute | solution.py:303
  60.6 5.7 %collective-permute-done.13.refs_1_ = bf16[80,1536]{1,0:T(8,128)(2,1)S(1)} collective-permute-done((bf16[80,1536]{1,0:T(8,128)(2,1)S(1)}, bf16[80,1536]{1,0:T(8,128)(2,1)S(1)}, u32[]{:S(2)}, u32[]{:S(2)}) %collective-permute-start.13) | collective-permute-done | bytes 245792 | tf_op jit(solution)/shard_map/ppermute | solution.py:303
  66.3 0.7 copy-done.4
  67.0 3.3 %last_step.1 = (bf16[128,1536]{1,0:T(8,128)(2,1)}, bf16[128,1536]{1,0:T(8,128)(2,1)}) custom-call(s32[9]{0:T(128)} %pad_add_fusion.table_ref, bf16[128,1536]{1,0:T(8,128)(2,1)} %gate_ref.3, bf16[128,1536]{1,0:T(8,128)(2,1)} %up_ref.3, f32[80,1536]{1,0:T(8,128)} %convert_add_fusion.refs_0_, bf16[80,1536]{1,0:T(8,128)(2,1)} %copy-done.4, ...), custom_call_target="tpu_custom_call" | custom-call | flops 3932160 | bytes 2359296 | tf_op jit(solution)/shard_map/last_step/pallas_call | solution.py:261
  70.3 7.1 %down_product.1 = bf16[1792,1536]{1,0:T(8,128)(2,1)} custom-call(s32[9]{0:T(128)S(1)} %copy-done.3, bf16[32,1792]{1,0:T(8,128)(2,1)S(1)} %constant_dynamic-update-slice_fusion.refs_0_, bf16[32,1792]{1,0:T(8,128)(2,1)S(1)} %collective-permute-done.1.refs_1_, bf16[32,1792]{1,0:T(8,128)(2,1)S(1)} %collective-permute-done.2.refs_2_, ...), custom_call_target="tpu_custom_call" | custom-call | flops 2818572288 | bytes 5505024 | tf_op jit(solution)/shard_map/down_product/pallas_call | solution.py:219
  (50 shorter events, 4.3 us)
Async XLA Ops:
  4.2 5.3 %collective-permute-start.5 = (bf16[16,1792]{1,0:T(8,128)(2,1)}, bf16[16,1792]{1,0:T(8,128)(2,1)S(1)}, u32[]{:S(2)}, u32[]{:S(2)}) collective-permute-start(bf16[16,1792]{1,0:T(8,128)(2,1)} %get-tuple-element.19), channel_id=1, source_target_pairs={{0,16},{1,17},{2,18},{3,19},{4,20},{5,21},{6,22},{7,23},{8,24},{9,... | collective-permute-start | bytes 172040 | tf_op jit(solution)/shard_map/ppermute | solution.py:303
  7.2 4.2 %collective-permute-start.6 = (bf16[16,1792]{1,0:T(8,128)(2,1)}, bf16[16,1792]{1,0:T(8,128)(2,1)S(1)}, u32[]{:S(2)}, u32[]{:S(2)}) collective-permute-start(bf16[16,1792]{1,0:T(8,128)(2,1)} %get-tuple-element.20), channel_id=1, source_target_pairs={{0,24},{1,25},{2,26},{3,27},{4,28},{5,29},{6,30},{7,31},{8,16},{9,... | collective-permute-start | bytes 172040 | tf_op jit(solution)/shard_map/ppermute | solution.py:303
  7.2 5.7 %collective-permute-start = (bf16[16,1792]{1,0:T(8,128)(2,1)}, bf16[16,1792]{1,0:T(8,128)(2,1)S(1)}, u32[]{:S(2)}, u32[]{:S(2)}) collective-permute-start(bf16[16,1792]{1,0:T(8,128)(2,1)} %get-tuple-element.18), channel_id=1, source_target_pairs={{0,8},{1,9},{2,10},{3,11},{4,12},{5,13},{6,14},{7,15},{8,0},{9,1},... | collective-permute-start | bytes 172040 | tf_op jit(solution)/shard_map/ppermute | solution.py:303
  11.3 6.7 %collective-permute-start.8 = (bf16[32,1792]{1,0:T(8,128)(2,1)S(1)}, bf16[32,1792]{1,0:T(8,128)(2,1)S(1)}, u32[]{:S(2)}, u32[]{:S(2)}) collective-permute-start(bf16[32,1792]{1,0:T(8,128)(2,1)S(1)} %constant_dynamic-update-slice_fusion.2.refs_5_.refs_8_), channel_id=1, source_target_pairs={{0,1},{1,3},{2,0},{3,5},{4,2},{5,7},{6,4},{7,6},{8,9},{9,11},{10,8... | collective-permute-start | bytes 344072 | tf_op jit(solution)/shard_map/ppermute | solution.py:303
  12.9 7.1 %collective-permute-start.1 = (bf16[32,1792]{1,0:T(8,128)(2,1)S(1)}, bf16[32,1792]{1,0:T(8,128)(2,1)S(1)}, u32[]{:S(2)}, u32[]{:S(2)}) collective-permute-start(bf16[32,1792]{1,0:T(8,128)(2,1)S(1)} %constant_dynamic-update-slice_fusion.refs_0_), channel_id=1, source_target_pairs={{0,2},{1,0},{2,4},{3,1},{4,6},{5,3},{6,7},{7,5},{8,10},{9,8},{10,1... | collective-permute-start | bytes 344072 | tf_op jit(solution)/shard_map/ppermute | solution.py:303
  13.4 6.7 %collective-permute-start.7 = (bf16[32,1792]{1,0:T(8,128)(2,1)S(1)}, bf16[32,1792]{1,0:T(8,128)(2,1)S(1)}, u32[]{:S(2)}, u32[]{:S(2)}) collective-permute-start(bf16[32,1792]{1,0:T(8,128)(2,1)S(1)} %constant_dynamic-update-slice_fusion.2.refs_5_.refs_8_), channel_id=1, source_target_pairs={{0,2},{1,0},{2,4},{3,1},{4,6},{5,3},{6,7},{7,5},{8,10},{9,8},{10,1... | collective-permute-start | bytes 344072 | tf_op jit(solution)/shard_map/ppermute | solution.py:303
  15.0 7.1 %collective-permute-start.2 = (bf16[32,1792]{1,0:T(8,128)(2,1)S(1)}, bf16[32,1792]{1,0:T(8,128)(2,1)S(1)}, u32[]{:S(2)}, u32[]{:S(2)}) collective-permute-start(bf16[32,1792]{1,0:T(8,128)(2,1)S(1)} %constant_dynamic-update-slice_fusion.refs_0_), channel_id=1, source_target_pairs={{0,1},{1,3},{2,0},{3,5},{4,2},{5,7},{6,4},{7,6},{8,9},{9,11},{10,8... | collective-permute-start | bytes 344072 | tf_op jit(solution)/shard_map/ppermute | solution.py:303
  17.6 23.4 %copy-start = (bf16[128,1536]{1,0:T(8,128)(2,1)S(1)}, bf16[128,1536]{1,0:T(8,128)(2,1)}, u32[]{:S(2)}) copy-start(bf16[128,1536]{1,0:T(8,128)(2,1)} %hidden_quant.1.refs_16_) | copy-start | bytes 1179652
  17.6 19.3 %collective-permute-start.24 = (bf16[128,1536]{1,0:T(8,128)(2,1)}, bf16[128,1536]{1,0:T(8,128)(2,1)S(1)}, u32[]{:S(2)}, u32[]{:S(2)}) collective-permute-start(bf16[128,1536]{1,0:T(8,128)(2,1)} %hidden_quant.1.refs_16_), channel_id=1, source_target_pairs={{0,16},{1,17},{2,18},{3,19},{4,20},{5,21},{6,22},{7,23},{8,24},{9,... | collective-permute-start | bytes 1179656 | tf_op jit(solution)/shard_map/ppermute | solution.py:303
  18.0 5.2 %collective-permute-start.10 = (bf16[32,1792]{1,0:T(8,128)(2,1)S(1)}, bf16[32,1792]{1,0:T(8,128)(2,1)S(1)}, u32[]{:S(2)}, u32[]{:S(2)}) collective-permute-start(bf16[32,1792]{1,0:T(8,128)(2,1)S(1)} %collective-permute-done.8.refs_7_.refs_10_), channel_id=1, source_target_pairs={{0,1},{1,3},{2,0},{3,5},{4,2},{5,7},{6,4},{7,6},{8,9},{9,11},{10,8... | collective-permute-start | bytes 344072 | tf_op jit(solution)/shard_map/ppermute | solution.py:303
  20.0 5.8 %collective-permute-start.3 = (bf16[32,1792]{1,0:T(8,128)(2,1)S(1)}, bf16[32,1792]{1,0:T(8,128)(2,1)S(1)}, u32[]{:S(2)}, u32[]{:S(2)}) collective-permute-start(bf16[32,1792]{1,0:T(8,128)(2,1)S(1)} %collective-permute-done.1.refs_1_), channel_id=1, source_target_pairs={{0,2},{1,0},{2,4},{3,1},{4,6},{5,3},{6,7},{7,5},{8,10},{9,8},{10,1... | collective-permute-start | bytes 344072 | tf_op jit(solution)/shard_map/ppermute | solution.py:303
  20.1 7.0 %collective-permute-start.9 = (bf16[32,1792]{1,0:T(8,128)(2,1)S(1)}, bf16[32,1792]{1,0:T(8,128)(2,1)S(1)}, u32[]{:S(2)}, u32[]{:S(2)}) collective-permute-start(bf16[32,1792]{1,0:T(8,128)(2,1)S(1)} %collective-permute-done.7.refs_6_.refs_9_), channel_id=1, source_target_pairs={{0,2},{1,0},{2,4},{3,1},{4,6},{5,3},{6,7},{7,5},{8,10},{9,8},{10,1... | collective-permute-start | bytes 344072 | tf_op jit(solution)/shard_map/ppermute | solution.py:303
  22.1 5.0 %collective-permute-start.4 = (bf16[32,1792]{1,0:T(8,128)(2,1)S(1)}, bf16[32,1792]{1,0:T(8,128)(2,1)S(1)}, u32[]{:S(2)}, u32[]{:S(2)}) collective-permute-start(bf16[32,1792]{1,0:T(8,128)(2,1)S(1)} %collective-permute-done.2.refs_2_), channel_id=1, source_target_pairs={{0,1},{1,3},{2,0},{3,5},{4,2},{5,7},{6,4},{7,6},{8,9},{9,11},{10,8... | collective-permute-start | bytes 344072 | tf_op jit(solution)/shard_map/ppermute | solution.py:303
  23.3 14.2 %collective-permute-start.18 = (bf16[32,1792]{1,0:T(8,128)(2,1)S(1)}, bf16[32,1792]{1,0:T(8,128)(2,1)S(1)}, u32[]{:S(2)}, u32[]{:S(2)}) collective-permute-start(bf16[32,1792]{1,0:T(8,128)(2,1)S(1)} %collective-permute-done.10.refs_9_.refs_12_), channel_id=1, source_target_pairs={{0,1},{1,3},{2,0},{3,5},{4,2},{5,7},{6,4},{7,6},{8,9},{9,11},{10,8... | collective-permute-start | bytes 344072 | tf_op jit(solution)/shard_map/ppermute | solution.py:303
  25.8 13.3 %collective-permute-start.14 = (bf16[32,1792]{1,0:T(8,128)(2,1)S(1)}, bf16[32,1792]{1,0:T(8,128)(2,1)S(1)}, u32[]{:S(2)}, u32[]{:S(2)}) collective-permute-start(bf16[32,1792]{1,0:T(8,128)(2,1)S(1)} %collective-permute-done.3.refs_3_), channel_id=1, source_target_pairs={{0,2},{1,0},{2,4},{3,1},{4,6},{5,3},{6,7},{7,5},{8,10},{9,8},{10,1... | collective-permute-start | bytes 344072 | tf_op jit(solution)/shard_map/ppermute | solution.py:303
  27.7 42.6 %copy-start.3 = (s32[9]{0:T(128)S(1)}, s32[9]{0:T(128)}, u32[]{:S(2)}) copy-start(s32[9]{0:T(128)} %pad_add_fusion.table_ref) | copy-start | bytes 112
  35.4 16.7 %collective-permute-start.12 = (bf16[80,1536]{1,0:T(8,128)(2,1)S(1)}, bf16[80,1536]{1,0:T(8,128)(2,1)S(1)}, u32[]{:S(2)}, u32[]{:S(2)}) collective-permute-start(bf16[80,1536]{1,0:T(8,128)(2,1)S(1)} %get-tuple-element.24), channel_id=1, source_target_pairs={{0,8},{1,9},{2,10},{3,11},{4,12},{5,13},{6,14},{7,15},{8,0},{9,1},... | collective-permute-start | bytes 737288 | tf_op jit(solution)/shard_map/ppermute | solution.py:303
  35.4 5.5 %collective-permute-start.17 = (bf16[32,1792]{1,0:T(8,128)(2,1)S(1)}, bf16[32,1792]{1,0:T(8,128)(2,1)S(1)}, u32[]{:S(2)}, u32[]{:S(2)}) collective-permute-start(bf16[32,1792]{1,0:T(8,128)(2,1)S(1)} %collective-permute-done.9.refs_8_.refs_11_), channel_id=1, source_target_pairs={{0,2},{1,0},{2,4},{3,1},{4,6},{5,3},{6,7},{7,5},{8,10},{9,8},{10,1... | collective-permute-start | bytes 344072 | tf_op jit(solution)/shard_map/ppermute | solution.py:303
  36.9 6.0 %collective-permute-start.15 = (bf16[32,1792]{1,0:T(8,128)(2,1)S(1)}, bf16[32,1792]{1,0:T(8,128)(2,1)S(1)}, u32[]{:S(2)}, u32[]{:S(2)}) collective-permute-start(bf16[32,1792]{1,0:T(8,128)(2,1)S(1)} %collective-permute-done.4.refs_4_), channel_id=1, source_target_pairs={{0,1},{1,3},{2,0},{3,5},{4,2},{5,7},{6,4},{7,6},{8,9},{9,11},{10,8... | collective-permute-start | bytes 344072 | tf_op jit(solution)/shard_map/ppermute | solution.py:303
  37.5 7.1 %collective-permute-start.19 = (bf16[32,1792]{1,0:T(8,128)(2,1)S(1)}, bf16[32,1792]{1,0:T(8,128)(2,1)S(1)}, u32[]{:S(2)}, u32[]{:S(2)}) collective-permute-start(bf16[32,1792]{1,0:T(8,128)(2,1)S(1)} %collective-permute-done.18.refs_4_.refs_14_), channel_id=1, source_target_pairs={{0,1},{1,3},{2,0},{3,5},{4,2},{5,7},{6,4},{7,6},{8,9},{9,11},{10,8... | collective-permute-start | bytes 344072 | tf_op jit(solution)/shard_map/ppermute | solution.py:303
  39.1 5.5 %collective-permute-start.16 = (bf16[32,1792]{1,0:T(8,128)(2,1)S(1)}, bf16[32,1792]{1,0:T(8,128)(2,1)S(1)}, u32[]{:S(2)}, u32[]{:S(2)}) collective-permute-start(bf16[32,1792]{1,0:T(8,128)(2,1)S(1)} %collective-permute-done.14.refs_0_.refs_5_), channel_id=1, source_target_pairs={{0,2},{1,0},{2,4},{3,1},{4,6},{5,3},{6,7},{7,5},{8,10},{9,8},{10,1... | collective-permute-start | bytes 344072 | tf_op jit(solution)/shard_map/ppermute | solution.py:303
  41.0 29.3 %collective-permute-start.23 = (bf16[128,1536]{1,0:T(8,128)(2,1)S(1)}, bf16[128,1536]{1,0:T(8,128)(2,1)S(1)}, u32[]{:S(2)}, u32[]{:S(2)}) collective-permute-start(bf16[128,1536]{1,0:T(8,128)(2,1)S(1)} %copy-done), channel_id=1, source_target_pairs={{0,8},{1,9},{2,10},{3,11},{4,12},{5,13},{6,14},{7,15},{8,0},{9,1},... | collective-permute-start | bytes 1179656 | tf_op jit(solution)/shard_map/ppermute | solution.py:303
  42.9 10.3 %collective-permute-start.11 = (bf16[80,1536]{1,0:T(8,128)(2,1)S(1)}, bf16[80,1536]{1,0:T(8,128)(2,1)S(1)}, u32[]{:S(2)}, u32[]{:S(2)}) collective-permute-start(bf16[80,1536]{1,0:T(8,128)(2,1)S(1)} %get-tuple-element.22), channel_id=1, source_target_pairs={{0,8},{1,9},{2,10},{3,11},{4,12},{5,13},{6,14},{7,15},{8,0},{9,1},... | collective-permute-start | bytes 737288 | tf_op jit(solution)/shard_map/ppermute | solution.py:303
  44.6 25.7 %collective-permute-start.25 = (bf16[128,1536]{1,0:T(8,128)(2,1)S(1)}, bf16[128,1536]{1,0:T(8,128)(2,1)S(1)}, u32[]{:S(2)}, u32[]{:S(2)}) collective-permute-start(bf16[128,1536]{1,0:T(8,128)(2,1)S(1)} %collective-permute-done.24.refs_18_), channel_id=1, source_target_pairs={{0,8},{1,9},{2,10},{3,11},{4,12},{5,13},{6,14},{7,15},{8,0},{9,1},... | collective-permute-start | bytes 1179656 | tf_op jit(solution)/shard_map/ppermute | solution.py:303
  51.4 4.2 %copy-start.1 = (bf16[48,1536]{1,0:T(8,128)(2,1)}, bf16[48,1536]{1,0:T(8,128)(2,1)S(1)}, u32[]{:S(2)}) copy-start(bf16[48,1536]{1,0:T(8,128)(2,1)S(1)} %get-tuple-element.25.refs_2_) | copy-start | bytes 442372
  51.4 2.2 %collective-permute-start.20 = (bf16[48,1536]{1,0:T(8,128)(2,1)S(1)}, bf16[48,1536]{1,0:T(8,128)(2,1)}, u32[]{:S(2)}, u32[]{:S(2)}) collective-permute-start(bf16[48,1536]{1,0:T(8,128)(2,1)S(1)} %get-tuple-element.26), channel_id=1, source_target_pairs={{0,8},{1,9},{2,10},{3,11},{4,12},{5,13},{6,14},{7,15},{8,0},{9,1},... | collective-permute-start | bytes 442376 | tf_op jit(solution)/shard_map/ppermute | solution.py:303
  52.0 6.7 %collective-permute-start.21 = (bf16[48,1536]{1,0:T(8,128)(2,1)S(1)}, bf16[48,1536]{1,0:T(8,128)(2,1)S(1)}, u32[]{:S(2)}, u32[]{:S(2)}) collective-permute-start(bf16[48,1536]{1,0:T(8,128)(2,1)S(1)} %get-tuple-element.27), channel_id=1, source_target_pairs={{0,16},{1,17},{2,18},{3,19},{4,20},{5,21},{6,22},{7,23},{8,24},{9,... | collective-permute-start | bytes 442376 | tf_op jit(solution)/shard_map/ppermute | solution.py:303
  53.2 7.3 %collective-permute-start.22 = (bf16[48,1536]{1,0:T(8,128)(2,1)S(1)}, bf16[48,1536]{1,0:T(8,128)(2,1)S(1)}, u32[]{:S(2)}, u32[]{:S(2)}) collective-permute-start(bf16[48,1536]{1,0:T(8,128)(2,1)S(1)} %get-tuple-element.28), channel_id=1, source_target_pairs={{0,24},{1,25},{2,26},{3,27},{4,28},{5,29},{6,30},{7,31},{8,16},{9,... | collective-permute-start | bytes 442376 | tf_op jit(solution)/shard_map/ppermute | solution.py:303
  53.6 12.7 %collective-permute-start.13 = (bf16[80,1536]{1,0:T(8,128)(2,1)S(1)}, bf16[80,1536]{1,0:T(8,128)(2,1)S(1)}, u32[]{:S(2)}, u32[]{:S(2)}) collective-permute-start(bf16[80,1536]{1,0:T(8,128)(2,1)S(1)} %add_convert_fusion), channel_id=1, source_target_pairs={{0,16},{1,17},{2,18},{3,19},{4,20},{5,21},{6,22},{7,23},{8,24},{9,... | collective-permute-start | bytes 737288 | tf_op jit(solution)/shard_map/ppermute | solution.py:303
  58.7 7.6 %copy-start.5 = (bf16[48,1536]{1,0:T(8,128)(2,1)}, bf16[48,1536]{1,0:T(8,128)(2,1)S(1)}, u32[]{:S(2)}) copy-start(bf16[48,1536]{1,0:T(8,128)(2,1)S(1)} %collective-permute-done.21.refs_4_) | copy-start | bytes 442372
  60.6 5.7 %copy-start.6 = (bf16[48,1536]{1,0:T(8,128)(2,1)}, bf16[48,1536]{1,0:T(8,128)(2,1)S(1)}, u32[]{:S(2)}) copy-start(bf16[48,1536]{1,0:T(8,128)(2,1)S(1)} %collective-permute-done.22.refs_5_) | copy-start | bytes 442372
  66.3 0.7 copy-start.4
  (1 other events, 0.6 us)

commit v2 on v0

--- a/solution.py
+++ b/solution.py
@@ -1,7 +1,14 @@
 import jax
 import jax.numpy as jnp
 from jax import lax
+from jax.experimental import pallas as pl
+from jax.experimental.pallas import tpu as pltpu
 from jax.sharding import PartitionSpec as P
+
+BF16 = jnp.bfloat16
+F32 = jnp.float32
+BOTH = ("dp", "tp")
+TILE = 128
 
 
 def tile_quant(values, tile_axis):
@@ -11,7 +18,14 @@
     return (payload.astype(jnp.float32) * tile_scale).astype(jnp.bfloat16)
 
 
-def per_device(out_grad, gate_pre, up_pre, down_weight, block_scales):
+def fast_quant(values, tile_axis):
+    largest = jnp.max(jnp.abs(values), axis=tile_axis, keepdims=True)
+    tile_scale = (largest + 1e-06) / 448.0
+    payload = (values * (1.0 / tile_scale)).astype(BF16)
+    return (payload.astype(F32) * tile_scale).astype(BF16)
+
+
+def any_mesh(out_grad, gate_pre, up_pre, down_weight, block_scales):
     width = down_weight.shape[0]
     hidden_units = down_weight.shape[1]
     weight_deq = (
@@ -60,7 +74,382 @@
     return (gate_grad, up_grad, summed.astype(jnp.bfloat16))
 
 
+VMEM = pl.BlockSpec(memory_space=pltpu.VMEM)
+SMEM = pl.BlockSpec(memory_space=pltpu.SMEM)
+HBM = pl.BlockSpec(memory_space=pltpu.HBM)
+MIB = 1024 * 1024
+
+
+def like(*shape, dtype=BF16):
+    return jax.ShapeDtypeStruct(shape, dtype)
+
+
+def ring_sources(n_tp, offsets):
+    half = n_tp // 2
+    me = lax.axis_index("tp")
+    odd = lax.rem(me, 2)
+    place = jnp.where(odd == 1, n_tp - 1 - me // 2, me // 2)
+    result = []
+    for offset in offsets:
+        at = lax.rem(place + offset + n_tp, n_tp)
+        result.append(jnp.where(at < half, 2 * at, 2 * (n_tp - 1 - at) + 1))
+    return result
+
+
+def split_columns(out_grad, parts):
+    rows, width = out_grad.shape
+    part = width // parts
+
+    def body(grad_ref, *refs):
+        outs, sems = refs[:parts], refs[parts]
+        me = lax.axis_index("dp")
+        copies = []
+        for j in range(parts):
+            start = pl.multiple_of((me ^ j) * part, TILE)
+            copies.append(
+                pltpu.make_async_copy(grad_ref.at[:, pl.ds(start, part)], outs[j], sems.at[j])
+            )
+            copies[-1].start()
+        for copy in copies:
+            copy.wait()
+
+    return pl.pallas_call(
+        body,
+        name="split_columns",
+        out_shape=[like(rows, part)] * parts,
+        in_specs=[HBM],
+        out_specs=[VMEM] * parts,
+        scratch_shapes=[pltpu.SemaphoreType.DMA((parts,))],
+    )(out_grad)
+
+
+def hidden_quant(gate_pre, up_pre):
+    tokens, units = gate_pre.shape
+
+    def body(gate_ref, up_ref, hidden_ref, gate_factor, up_factor):
+        for c in range(units // TILE):
+            at = (slice(None), slice(c * TILE, (c + 1) * TILE))
+            gate = gate_ref[at].astype(F32)
+            up = up_ref[at].astype(F32)
+            sigma = 1.0 / (1.0 + jnp.exp(-gate))
+            hidden_ref[at] = fast_quant(gate * sigma * up, 0)
+            gate_factor[at] = up * sigma * (1.0 + gate * (1.0 - sigma))
+            up_factor[at] = gate * sigma
+
+    return pl.pallas_call(
+        body,
+        name="hidden_quant",
+        out_shape=[like(tokens, units)] + [like(tokens, units, dtype=F32)] * 2,
+        in_specs=[VMEM] * 2,
+        out_specs=[VMEM] * 3,
+        compiler_params=pltpu.CompilerParams(vmem_limit_bytes=16 * MIB),
+        cost_estimate=pl.CostEstimate(
+            flops=20 * tokens * units, bytes_accessed=14 * tokens * units, transcendentals=tokens * units
+        ),
+    )(gate_pre, up_pre)
+
+
+def weight_rows(down_weight, scales, parts):
+    width, units = down_weight.shape
+    part = width // parts
+    chunk = 2 * TILE
+    count = part // chunk
+
+    def body(scale_ref, weight_ref, out_ref, sems):
+        me = lax.axis_index("dp")
+        copies = []
+        for i in range(count):
+            start = pl.multiple_of(me * part + i * chunk, TILE)
+            copies.append(
+                pltpu.make_async_copy(
+                    weight_ref.at[pl.ds(start, chunk)],
+                    out_ref.at[pl.ds(i * chunk, chunk)],
+                    sems.at[i],
+                )
+            )
+            copies[-1].start()
+        row0 = me * (part // TILE)
+        for i in range(count):
+            copies[i].wait()
+            for a in range(i * chunk // TILE, (i + 1) * chunk // TILE):
+                for b in range(units // TILE):
+                    at = (slice(a * TILE, (a + 1) * TILE), slice(b * TILE, (b + 1) * TILE))
+                    scale = jnp.full((TILE, TILE), scale_ref[row0 + a, b], F32).astype(BF16)
+                    out_ref[at] = out_ref[at] * scale
+
+    return pl.pallas_call(
+        body,
+        name="weight_rows",
+        out_shape=like(part, units),
+        in_specs=[SMEM, HBM],
+        out_specs=VMEM,
+        scratch_shapes=[pltpu.SemaphoreType.DMA((count,))],
+        compiler_params=pltpu.CompilerParams(vmem_limit_bytes=48 * MIB),
+        cost_estimate=pl.CostEstimate(flops=part * units, bytes_accessed=4 * part * units, transcendentals=0),
+    )(scales, down_weight)
+
+
+def partial_hidden(pieces_p, pieces_q, weight):
+    count = len(pieces_p)
+    rows2, part = pieces_p[0].shape
+    rows = rows2 // 2
+    units = weight.shape[1]
+    each = count * rows
+    step = 512 if units % 512 == 0 else 256
+
+    def body(*refs):
+        groups = refs[:count], refs[count : 2 * count]
+        weight_ref = refs[2 * count]
+        outs = refs[2 * count + 1 : 2 * count + 5]
+        quant_ref = refs[2 * count + 5]
+        for half, group in enumerate(groups):
+            for k, ref in enumerate(group):
+                for c in range(part // TILE):
+                    cols = slice(c * TILE, (c + 1) * TILE)
+                    deq = fast_quant(ref[:, cols].astype(F32), 1)
+                    for s in range(2):
+                        base = (2 * half + s) * each + k * rows
+                        quant_ref[base : base + rows, cols] = deq[s * rows : (s + 1) * rows]
+        for i in range(units // step):
+            cols = slice(i * step, (i + 1) * step)
+            result = jnp.dot(quant_ref[...], weight_ref[:, cols], preferred_element_type=F32)
+            for j, out in enumerate(outs):
+                out[:, cols] = result[j * each : (j + 1) * each].astype(BF16)
+
+    return pl.pallas_call(
+        body,
+        name="partial_hidden",
+        out_shape=[like(each, units)] * 4,
+        in_specs=[VMEM] * (2 * count + 1),
+        out_specs=[VMEM] * 4,
+        scratch_shapes=[pltpu.VMEM((4 * each, part), BF16)],
+        compiler_params=pltpu.CompilerParams(vmem_limit_bytes=24 * MIB),
+        cost_estimate=pl.CostEstimate(
+            flops=8 * each * part * units, bytes_accessed=2 * part * units, transcendentals=0
+        ),
+    )(*pieces_p, *pieces_q, weight)
+
+
+def down_product(n_tp, offsets, pieces_p, pieces_q, hiddens):
+    count = len(pieces_p)
+    rows2, part = pieces_p[0].shape
+    rows = rows2 // 2
+    tokens, units = hiddens[0].shape
+    step, slots, split = 256, 3, 4
+    steps = part // step
+
+    def body(*refs):
+        groups = refs[:count], refs[count : 2 * count]
+        h_refs = refs[2 * count : 2 * count + 4]
+        out_ref, token_ref, hid_ref, quant_ref, buffer, sems = refs[2 * count + 4 :]
+        token_ref[...] = jnp.zeros(token_ref.shape, F32)
+        starts = [pl.multiple_of(s * rows, rows) for s in ring_sources(n_tp, offsets)]
+        for j, ref in enumerate(h_refs):
+            for k, start in enumerate(starts):
+                low = j * tokens + k * rows
+                hid_ref[low : low + rows, :] = ref[pl.ds(start, rows), :]
+
+        def copies(i):
+            lines = step // split
+            return [
+                pltpu.make_async_copy(
+                    buffer.at[i % slots, pl.ds(k * lines, lines)],
+                    out_ref.at[pl.ds(i * step + k * lines, lines)],
+                    sems.at[i % slots, k],
+                )
+                for k in range(split)
+            ]
+
+        for i in range(steps):
+            if i >= slots:
+                for copy in copies(i - slots):
+                    copy.wait()
+            for c in range(step // TILE):
+                cols = slice(i * step + c * TILE, i * step + (c + 1) * TILE)
+                for j in range(4):
+                    low = (j % 2) * rows
+                    vals = [ref[low : low + rows, cols].astype(F32) for ref in groups[j // 2]]
+                    top = jnp.abs(vals[0])
+                    for v in vals[1:]:
+                        top = jnp.maximum(top, jnp.abs(v))
+                    scale = (jnp.max(top, axis=0, keepdims=True) + 1e-06) / 448.0
+                    inverse = 1.0 / scale
+                    for k, v in enumerate(vals):
+                        payload = (v * inverse).astype(BF16).astype(F32)
+                        base = j * tokens + k * rows
+                        quant_ref[base : base + rows, c * TILE : (c + 1) * TILE] = (
+                            payload * scale
+                        ).astype(BF16)
+            buffer[i % slots] = lax.dot_general(
+                quant_ref[...], hid_ref[...], (((0,), (0,)), ((), ())), preferred_element_type=F32
+            ).astype(BF16)
+            for copy in copies(i):
+                copy.start()
+        for i in range(max(0, steps - slots), steps):
+            for copy in copies(i):
+                copy.wait()
+
+    return pl.pallas_call(
+        body,
+        name="down_product",
+        out_shape=[like(part, units), like(8, TILE, dtype=F32)],
+        in_specs=[VMEM] * (2 * count + 4),
+        out_specs=[HBM, VMEM],
+        scratch_shapes=[
+            pltpu.VMEM((4 * tokens, units), BF16),
+            pltpu.VMEM((4 * tokens, step), BF16),
+            pltpu.VMEM((slots, step, units), BF16),
+            pltpu.SemaphoreType.DMA((slots, split)),
+        ],
+        compiler_params=pltpu.CompilerParams(vmem_limit_bytes=24 * MIB),
+        cost_estimate=pl.CostEstimate(
+            flops=8 * part * tokens * units, bytes_accessed=2 * part * units, transcendentals=0
+        ),
+    )(*pieces_p, *pieces_q, *hiddens)
+
+
+def last_step(n_tp, offsets, gate_factor, up_factor, groups, after):
+    tokens, units = gate_factor.shape
+    sizes = [len(g) for g in groups]
+    lengths = [g[0].shape[0] for g in groups]
+    flat = [a for g in groups for a in g]
+    rows = tokens // len(offsets)
+    split = 2
+    half = units // split
+
+    def body(gate_ref, up_ref, _, *refs):
+        ins = refs[: len(flat)]
+        gate_out, up_out, gate_buf, up_buf, sems = refs[len(flat) :]
+        starts = [pl.multiple_of(s * rows, rows) for s in ring_sources(n_tp, offsets)]
+        copies = []
+        for h in range(split):
+            cols = slice(h * half, (h + 1) * half)
+            at = piece = 0
+            for size, length in zip(sizes, lengths):
+                for first in range(0, length, rows):
+                    where = pl.ds(starts[piece], rows)
+                    grad = ins[at][first : first + rows, cols].astype(F32)
+                    for ref in ins[at + 1 : at + size]:
+                        grad = grad + ref[first : first + rows, cols].astype(F32)
+                    gate_buf[where, cols] = (grad * gate_ref[where, cols]).astype(BF16)
+                    up_buf[where, cols] = (grad * up_ref[where, cols]).astype(BF16)
+                    piece += 1
+                at += size
+            for k, (buf, out) in enumerate(((gate_buf, gate_out), (up_buf, up_out))):
+                copies.append(
+                    pltpu.make_async_copy(buf.at[:, cols], out.at[:, cols], sems.at[k, h])
+                )
+                copies[-1].start()
+        for copy in copies:
+            copy.wait()
+
+    return pl.pallas_call(
+        body,
+        name="last_step",
+        out_shape=[like(tokens, units)] * 2,
+        in_specs=[VMEM] * (3 + len(flat)),
+        out_specs=[HBM] * 2,
+        scratch_shapes=[pltpu.VMEM((tokens, units), BF16)] * 2
+        + [pltpu.SemaphoreType.DMA((2, split))],
+        compiler_params=pltpu.CompilerParams(vmem_limit_bytes=16 * MIB),
+        cost_estimate=pl.CostEstimate(
+            flops=8 * tokens * units, bytes_accessed=16 * tokens * units, transcendentals=0
+        ),
+    )(gate_factor, up_factor, after, *flat)
+
+
+def fold(own, received):
+    return (own[0].astype(F32) + received[0].astype(F32)), (
+        own[1].astype(F32) + received[1].astype(F32)
+    ).astype(BF16)
+
+
+def pair_mesh(n_tp, out_grad, gate_pre, up_pre, down_weight, block_scales):
+    half = n_tp // 2
+    order = [2 * i for i in range(half)] + [2 * (n_tp - 1 - i) + 1 for i in range(half, n_tp)]
+    up = {order[i]: order[(i + 1) % n_tp] for i in range(n_tp)}
+    down = {v: k for k, v in up.items()}
+
+    def permute(value, target):
+        pairs = []
+        for d in range(4):
+            for t in range(n_tp):
+                dd, tt = target(d, t)
+                pairs.append((d * n_tp + t, dd * n_tp + tt))
+        return lax.ppermute(value, BOTH, pairs)
+
+    def flip(value, bits):
+        return permute(value, lambda d, t: (d ^ bits, t))
+
+    def send_up(value):
+        return permute(value, lambda d, t: (d, up[t]))
+
+    def send_down(value):
+        return permute(value, lambda d, t: (d, down[t]))
+
+    offsets = [0]
+    for k in range(1, half):
+        offsets += [-k, k]
+    offsets.append(half)
+
+    parts = split_columns(out_grad, 4)
+    from_core = flip(parts[1], 1)
+    from_chip = flip(parts[2], 2)
+    from_far = flip(parts[3], 3)
+    hidden_own, gate_factor, up_factor = hidden_quant(gate_pre, up_pre)
+    weight = weight_rows(down_weight, block_scales.astype(F32), 4)
+    block_p = jnp.concatenate([parts[0], from_core], axis=0)
+    block_q = jnp.concatenate([from_chip, from_far], axis=0)
+
+    pieces_p, pieces_q = {0: block_p}, {0: block_q}
+    for k in range(1, half + 1):
+        pieces_p[-k] = send_up(pieces_p[1 - k])
+        if k < half:
+            pieces_p[k] = send_down(pieces_p[k - 1])
+            pieces_q[-k] = send_up(pieces_q[1 - k])
+        pieces_q[k] = send_down(pieces_q[k - 1])
+    pieces_p[half] = pieces_p[-half]
+    list_p = [pieces_p[o] for o in offsets]
+    list_q = [pieces_q[o] for o in offsets]
+
+    hidden_chip = flip(hidden_own, 2)
+    hidden_core = flip(hidden_own, 1)
+    hidden_far = flip(hidden_chip, 1)
+
+    first = n_tp - 3
+    groups = []
+    part1 = partial_hidden(list_p[:first], list_q[:first], weight)
+    got0, got2 = flip(part1[1], 1), flip(part1[3], 1)
+    sum0, sum2 = fold((part1[0], part1[2]), (got0, got2))
+    groups.append([sum0, flip(sum2, 2)])
+    part2 = partial_hidden(list_p[first:], list_q[first:], weight)
+    groups.append([part2[0]] + [flip(part2[j], j) for j in (1, 2, 3)])
+    down_grad, token = down_product(
+        n_tp, offsets, list_p, list_q, [hidden_own, hidden_core, hidden_chip, hidden_far]
+    )
+    gate_grad, up_grad = last_step(n_tp, offsets, gate_factor, up_factor, groups, token)
+    return gate_grad, up_grad, down_grad
+
+
 def solution(mesh):
+    n_dp, n_tp = mesh.shape["dp"], mesh.shape["tp"]
+
+    def per_device(out_grad, gate_pre, up_pre, down_weight, block_scales):
+        part = down_weight.shape[0] // n_dp
+        rows = out_grad.shape[0]
+        fits = (
+            n_dp == 4
+            and n_tp >= 4
+            and n_tp % 2 == 0
+            and rows % 16 == 0
+            and rows * n_tp == 128
+            and part % 256 == 0
+            and gate_pre.shape[1] % 256 == 0
+        )
+        if fits:
+            return pair_mesh(n_tp, out_grad, gate_pre, up_pre, down_weight, block_scales)
+        return any_mesh(out_grad, gate_pre, up_pre, down_weight, block_scales)
+
     placed = (P(("dp", "tp"), None), P("dp", "tp"), P("dp", "tp"), P(None, "tp"), P(None, "tp"))
     return jax.shard_map(
         per_device,

time: 215 us -> 57.3 us (0.27)
  other arithmetic: 59.2 us -> 0.11 us
  local copies, waits for them, and re-layouts: 44.6 us -> 3.61 us
  matrix products: 38.8 us -> 0 us
  waiting for transfers between devices: 53.3 us -> 14.8 us
  starting transfers between devices: 3.68 us -> 21.5 us
  Pallas kernels: 0 us -> 16.2 us
  between operations: 14.1 us -> 0.77 us
    add x4 -> x1, other arithmetic: 43.4 us -> 0.05 us  [fold(): own[0].astype(F32) + received[0].astype(F32)]
    dot_general x5 -> x0, matrix products: 38.8 us -> none  [the longest x4 20.2 us: one_block(): lax.dot_general(grad_block, hidden_block, (((0,), (0,)), ((), ())), prefe...]
    all_to_all x1 -> x0, waiting for transfers between devices: 30.5 us -> none  [per_device(): lax.all_to_all(grad_colq, 'dp', split_axis=1, concat_axis=0, tiled=True)]
    unnamed x10 -> x6, local copies, waits for them, and re-layouts: 31.4 us -> 2.82 us
    all_gather x2 -> x0, waiting for transfers between devices: 22 us -> none  [the longest x1 22 us: per_device(): grad_tokens = lax.all_gather(out_grad, 'tp', axis=0, tiled=True)]
    ppermute x0 -> x26, starting transfers between devices: none -> 21.5 us  [permute(): return lax.ppermute(value, BOTH, pairs)]
    pallas_call x0 -> x7, Pallas kernels: none -> 16.2 us  [the longest x1 5.31 us: down_product(): pl.pallas_call(body, name='down_product', out_shape=[like(part, units), l...]
    ppermute x0 -> x26, waiting for transfers between devices: none -> 14.8 us  [permute(): return lax.ppermute(value, BOTH, pairs)]
  transfers between devices with their start and end apart: 3 -> 26, of which waited for: 2 -> 7; matrix products, arithmetic and copies ran while one was open for 15% -> 3% of each run, Pallas kernels for 0% -> 24%
where the time goes in v2:
time: 57.3 us; the launch traced here: 57 us
  starting transfers between devices  21.5 us (38%)
  Pallas kernels  16.2 us (28%)
  waiting for transfers between devices  14.8 us (26%)
  local copies, waits for them, and re-layouts  3.61 us (6%)
  between operations  0.77 us (1%)
    ppermute x26, starting transfers between devices, permute(): return lax.ppermute(value, BOTH, pairs)  21.5 us
    ppermute x26, waiting for transfers between devices, permute(): return lax.ppermute(value, BOTH, pairs)  14.8 us
    pallas_call x1, Pallas kernels, down_product(): pl.pallas_call(body, name='down_product', out_shape=[like(part, units), l...  5.31 us
    pallas_call x2, Pallas kernels, partial_hidden(): pl.pallas_call(body, name='partial_hidden', out_shape=[like(each, units)]...  3.82 us
    pallas_call x1, Pallas kernels, weight_rows(): pl.pallas_call(body, name='weight_rows', out_shape=like(part, units), in_...  3.77 us
    unnamed x6, local copies, waits for them, and re-layouts  2.82 us
    pallas_call x1, Pallas kernels, split_columns(): pl.pallas_call(body, name='split_columns', out_shape=[like(rows, part)] *...  1.63 us
  transfers between devices with their start and end apart: 26, of which 7 were waited for; matrix products, arithmetic and copies ran while one was open for 3% of the time, Pallas kernels for 24%

profile of v2, /device:TPU:0, one launch (start us, length us, event | category | flops | bytes accessed | tf_op | source)
XLA Modules:
  0.0 57.0 jit_solution(8743727698834085094)
XLA Ops:
  0.6 1.6 %split_columns.1 = (bf16[16,1792]{1,0:T(8,128)(2,1)}, bf16[16,1792]{1,0:T(8,128)(2,1)}, bf16[16,1792]{1,0:T(8,128)(2,1)}, bf16[16,1792]{1,0:T(8,128)(2,1)}) custom-call(bf16[16,7168]{1,0:T(8,128)(2,1)} %grad_ref.1), custom_call_target="tpu_custom_call" | custom-call | tf_op jit(solution)/shard_map/split_columns/pallas_call | solution.py:116
  2.3 3.0 %collective-permute-start.8 = (bf16[16,1792]{1,0:T(8,128)(2,1)}, bf16[16,1792]{1,0:T(8,128)(2,1)S(1)}, u32[]{:S(2)}, u32[]{:S(2)}) collective-permute-start(bf16[16,1792]{1,0:T(8,128)(2,1)} %get-tuple-element.26), channel_id=1, source_target_pairs={{0,16},{1,17},{2,18},{3,19},{4,20},{5,21},{6,22},{7,23},{8,24},{9,... | collective-permute-start | bytes 172040 | tf_op jit(solution)/shard_map/ppermute | solution.py:379
  5.5 0.8 %constant_dynamic-update-slice_fusion.1 = bf16[32,1792]{1,0:T(8,128)(2,1)S(1)} fusion(bf16[16,1792]{1,0:T(8,128)(2,1)} %get-tuple-element.24), kind=kLoop, calls=%fused_computation.3 | loop fusion | bytes 114688
  6.3 1.4 %collective-permute-done.8 = bf16[16,1792]{1,0:T(8,128)(2,1)S(1)} collective-permute-done((bf16[16,1792]{1,0:T(8,128)(2,1)}, bf16[16,1792]{1,0:T(8,128)(2,1)S(1)}, u32[]{:S(2)}, u32[]{:S(2)}) %collective-permute-start.8) | collective-permute-done | bytes 57376 | tf_op jit(solution)/shard_map/ppermute | solution.py:379
  7.6 1.8 %collective-permute-done.9 = bf16[16,1792]{1,0:T(8,128)(2,1)S(1)} collective-permute-done((bf16[16,1792]{1,0:T(8,128)(2,1)}, bf16[16,1792]{1,0:T(8,128)(2,1)S(1)}, u32[]{:S(2)}, u32[]{:S(2)}) %collective-permute-start.9) | collective-permute-done | bytes 57376 | tf_op jit(solution)/shard_map/ppermute | solution.py:379
  9.4 1.5 %collective-permute-start.11 = (bf16[32,1792]{1,0:T(8,128)(2,1)S(1)}, bf16[32,1792]{1,0:T(8,128)(2,1)S(1)}, u32[]{:S(2)}, u32[]{:S(2)}) collective-permute-start(bf16[32,1792]{1,0:T(8,128)(2,1)S(1)} %constant_dynamic-update-slice_fusion.2.refs_8_.refs_5_), channel_id=1, source_target_pairs={{0,1},{1,3},{2,0},{3,5},{4,2},{5,7},{6,4},{7,6},{8,9},{9,11},{10,8... | collective-permute-start | bytes 344072 | tf_op jit(solution)/shard_map/ppermute | solution.py:379
  11.0 0.6 collective-permute-start.1
  11.5 1.6 %collective-permute-start.10 = (bf16[32,1792]{1,0:T(8,128)(2,1)S(1)}, bf16[32,1792]{1,0:T(8,128)(2,1)S(1)}, u32[]{:S(2)}, u32[]{:S(2)}) collective-permute-start(bf16[32,1792]{1,0:T(8,128)(2,1)S(1)} %constant_dynamic-update-slice_fusion.2.refs_8_.refs_5_), channel_id=1, source_target_pairs={{0,2},{1,0},{2,4},{3,1},{4,6},{5,3},{6,7},{7,5},{8,10},{9,8},{10,1... | collective-permute-start | bytes 344072 | tf_op jit(solution)/shard_map/ppermute | solution.py:379
  13.1 0.4 collective-permute-start.2
  13.6 1.0 %copy-done = bf16[128,1536]{1,0:T(8,128)(2,1)S(1)} copy-done((bf16[128,1536]{1,0:T(8,128)(2,1)S(1)}, bf16[128,1536]{1,0:T(8,128)(2,1)}, u32[]{:S(2)}) %copy-start) | copy-done | bytes 393240
  14.6 1.0 %copy-done.1 = bf16[128,1536]{1,0:T(8,128)(2,1)S(1)} copy-done((bf16[128,1536]{1,0:T(8,128)(2,1)S(1)}, bf16[128,1536]{1,0:T(8,128)(2,1)}, u32[]{:S(2)}) %copy-start.1) | copy-done | bytes 393240
  15.5 0.6 hidden_quant.1
  16.1 0.5 collective-permute-start.18
  16.6 2.0 %collective-permute-start.13 = (bf16[32,1792]{1,0:T(8,128)(2,1)S(1)}, bf16[32,1792]{1,0:T(8,128)(2,1)S(1)}, u32[]{:S(2)}, u32[]{:S(2)}) collective-permute-start(bf16[32,1792]{1,0:T(8,128)(2,1)S(1)} %collective-permute-done.11.refs_10_.refs_7_), channel_id=1, source_target_pairs={{0,1},{1,3},{2,0},{3,5},{4,2},{5,7},{6,4},{7,6},{8,9},{9,11},{10,8... | collective-permute-start | bytes 344072 | tf_op jit(solution)/shard_map/ppermute | solution.py:379
  18.7 2.0 %collective-permute-start.12 = (bf16[32,1792]{1,0:T(8,128)(2,1)S(1)}, bf16[32,1792]{1,0:T(8,128)(2,1)S(1)}, u32[]{:S(2)}, u32[]{:S(2)}) collective-permute-start(bf16[32,1792]{1,0:T(8,128)(2,1)S(1)} %collective-permute-done.10.refs_9_.refs_6_), channel_id=1, source_target_pairs={{0,2},{1,0},{2,4},{3,1},{4,6},{5,3},{6,7},{7,5},{8,10},{9,8},{10,1... | collective-permute-start | bytes 344072 | tf_op jit(solution)/shard_map/ppermute | solution.py:379
  20.7 0.8 %copy.9.scale_ref = f32[56,12]{1,0:T(8,128)S(1)} copy(bf16[56,12]{0,1:T(8,128)(2,1)} %param.9) | data formatting | bytes 4032 | tf_op jit(solution)/shard_map/convert_element_type | solution.py:400
  21.5 3.8 %weight_rows.1.refs_10_.refs_6_ = bf16[1792,1536]{1,0:T(8,128)(2,1)S(1)} custom-call(f32[56,12]{1,0:T(8,128)S(1)} %copy.9.scale_ref, bf16[7168,1536]{1,0:T(8,128)(2,1)} %weight_ref.1), custom_call_target="tpu_custom_call" | custom-call | flops 2752512 | bytes 11010048 | tf_op jit(solution)/shard_map/weight_rows/pallas_call | solution.py:180
  25.3 1.9 %collective-permute-start.15 = (bf16[32,1792]{1,0:T(8,128)(2,1)S(1)}, bf16[32,1792]{1,0:T(8,128)(2,1)S(1)}, u32[]{:S(2)}, u32[]{:S(2)}) collective-permute-start(bf16[32,1792]{1,0:T(8,128)(2,1)S(1)} %collective-permute-done.13.refs_12_.refs_9_), channel_id=1, source_target_pairs={{0,1},{1,3},{2,0},{3,5},{4,2},{5,7},{6,4},{7,6},{8,9},{9,11},{10,8... | collective-permute-start | bytes 344072 | tf_op jit(solution)/shard_map/ppermute | solution.py:379
  27.4 2.3 %partial_hidden.2 = (bf16[80,1536]{1,0:T(8,128)(2,1)S(1)}, bf16[80,1536]{1,0:T(8,128)(2,1)S(1)}, bf16[80,1536]{1,0:T(8,128)(2,1)S(1)}, bf16[80,1536]{1,0:T(8,128)(2,1)S(1)}) custom-call(bf16[32,1792]{1,0:T(8,128)(2,1)S(1)} %constant_dynamic-update-slice_fusion.refs_0_, bf16[32,1792]{1,0:T(8,128)(2,1)S(1)} %collective-permute-done.1.refs_1_, ...), custom_call_target="tpu_custom_call" | custom-call | flops 1761607680 | bytes 5505024 | tf_op jit(solution)/shard_map/partial_hidden/pallas_call | solution.py:219
  29.8 2.0 %collective-permute-start.14 = (bf16[32,1792]{1,0:T(8,128)(2,1)S(1)}, bf16[32,1792]{1,0:T(8,128)(2,1)S(1)}, u32[]{:S(2)}, u32[]{:S(2)}) collective-permute-start(bf16[32,1792]{1,0:T(8,128)(2,1)S(1)} %collective-permute-done.12.refs_11_.refs_8_), channel_id=1, source_target_pairs={{0,2},{1,0},{2,4},{3,1},{4,6},{5,3},{6,7},{7,5},{8,10},{9,8},{10,1... | collective-permute-start | bytes 344072 | tf_op jit(solution)/shard_map/ppermute | solution.py:379
  31.9 1.9 %collective-permute-start.16 = (bf16[32,1792]{1,0:T(8,128)(2,1)S(1)}, bf16[32,1792]{1,0:T(8,128)(2,1)S(1)}, u32[]{:S(2)}, u32[]{:S(2)}) collective-permute-start(bf16[32,1792]{1,0:T(8,128)(2,1)S(1)} %collective-permute-done.15.refs_14_.refs_4_), channel_id=1, source_target_pairs={{0,1},{1,3},{2,0},{3,5},{4,2},{5,7},{6,4},{7,6},{8,9},{9,11},{10,8... | collective-permute-start | bytes 344072 | tf_op jit(solution)/shard_map/ppermute | solution.py:379
  33.9 1.6 %collective-permute-done.14.refs_13_.refs_3_ = bf16[32,1792]{1,0:T(8,128)(2,1)S(1)} collective-permute-done((bf16[32,1792]{1,0:T(8,128)(2,1)S(1)}, bf16[32,1792]{1,0:T(8,128)(2,1)S(1)}, u32[]{:S(2)}, u32[]{:S(2)}) %collective-permute-start.14) | collective-permute-done | bytes 114720 | tf_op jit(solution)/shard_map/ppermute | solution.py:379
  35.5 2.3 %collective-permute-done.6.refs_6_.refs_1_ = bf16[32,1792]{1,0:T(8,128)(2,1)S(1)} collective-permute-done((bf16[32,1792]{1,0:T(8,128)(2,1)S(1)}, bf16[32,1792]{1,0:T(8,128)(2,1)S(1)}, u32[]{:S(2)}, u32[]{:S(2)}) %collective-permute-start.6) | collective-permute-done | bytes 114720 | tf_op jit(solution)/shard_map/ppermute | solution.py:379
  37.8 1.7 %collective-permute-done.16.refs_15_.refs_5_ = bf16[32,1792]{1,0:T(8,128)(2,1)S(1)} collective-permute-done((bf16[32,1792]{1,0:T(8,128)(2,1)S(1)}, bf16[32,1792]{1,0:T(8,128)(2,1)S(1)}, u32[]{:S(2)}, u32[]{:S(2)}) %collective-permute-start.16) | collective-permute-done | bytes 114720 | tf_op jit(solution)/shard_map/ppermute | solution.py:379
  39.5 1.5 %partial_hidden.3 = (bf16[48,1536]{1,0:T(8,128)(2,1)S(1)}, bf16[48,1536]{1,0:T(8,128)(2,1)S(1)}, bf16[48,1536]{1,0:T(8,128)(2,1)S(1)}, bf16[48,1536]{1,0:T(8,128)(2,1)S(1)}) custom-call(bf16[32,1792]{1,0:T(8,128)(2,1)S(1)} %collective-permute-done.5.refs_5_.refs_0_, bf16[32,1792]{1,0:T(8,128)(2,1)S(1)} %collective-permute-done.6.refs_6_.refs_1_, ...), custom_call_target="tpu_custom_call" | custom-call | flops 1056964608 | bytes 5505024 | tf_op jit(solution)/shard_map/partial_hidden/pallas_call | solution.py:219
  41.0 0.6 %collective-permute-start.23 = (bf16[48,1536]{1,0:T(8,128)(2,1)S(1)}, bf16[48,1536]{1,0:T(8,128)(2,1)S(1)}, u32[]{:S(2)}, u32[]{:S(2)}) collective-permute-start(bf16[48,1536]{1,0:T(8,128)(2,1)S(1)} %get-tuple-element.35), channel_id=1, source_target_pairs={{0,8},{1,9},{2,10},{3,11},{4,12},{5,13},{6,14},{7,15},{8,0},{9,1},... | collective-permute-start | bytes 442376 | tf_op jit(solution)/shard_map/ppermute | solution.py:379
  41.6 1.1 %collective-permute-start.24 = (bf16[48,1536]{1,0:T(8,128)(2,1)S(1)}, bf16[48,1536]{1,0:T(8,128)(2,1)S(1)}, u32[]{:S(2)}, u32[]{:S(2)}) collective-permute-start(bf16[48,1536]{1,0:T(8,128)(2,1)S(1)} %get-tuple-element.36), channel_id=1, source_target_pairs={{0,16},{1,17},{2,18},{3,19},{4,20},{5,21},{6,22},{7,23},{8,24},{9,... | collective-permute-start | bytes 442376 | tf_op jit(solution)/shard_map/ppermute | solution.py:379
  42.8 0.4 collective-permute-start.25
  43.2 1.2 %collective-permute-start.22 = (bf16[80,1536]{1,0:T(8,128)(2,1)S(1)}, bf16[80,1536]{1,0:T(8,128)(2,1)S(1)}, u32[]{:S(2)}, u32[]{:S(2)}) collective-permute-start(bf16[80,1536]{1,0:T(8,128)(2,1)S(1)} %add_convert_fusion), channel_id=1, source_target_pairs={{0,16},{1,17},{2,18},{3,19},{4,20},{5,21},{6,22},{7,23},{8,24},{9,... | collective-permute-start | bytes 737288 | tf_op jit(solution)/shard_map/ppermute | solution.py:379
  44.4 5.3 %down_product.1 = (bf16[1792,1536]{1,0:T(8,128)(2,1)}, f32[8,128]{1,0:T(8,128)S(1)}) custom-call(bf16[32,1792]{1,0:T(8,128)(2,1)S(1)} %constant_dynamic-update-slice_fusion.refs_0_, bf16[32,1792]{1,0:T(8,128)(2,1)S(1)} %collective-permute-done.1.refs_1_, bf16[32,1792]{1,0:T(8,128)(2,1)S(1)} %collective-permute-done.2.refs_2_, ...), custom_call_target="tpu_custom_call" | custom-call | flops 2818572288 | bytes 5505024 | tf_op jit(solution)/shard_map/down_product/pallas_call | solution.py:292
  50.1 5.7 %collective-permute-done.22.refs_1_ = bf16[80,1536]{1,0:T(8,128)(2,1)S(1)} collective-permute-done((bf16[80,1536]{1,0:T(8,128)(2,1)S(1)}, bf16[80,1536]{1,0:T(8,128)(2,1)S(1)}, u32[]{:S(2)}, u32[]{:S(2)}) %collective-permute-start.22) | collective-permute-done | bytes 245792 | tf_op jit(solution)/shard_map/ppermute | solution.py:379
  55.9 1.1 %last_step.1 = (bf16[128,1536]{1,0:T(8,128)(2,1)}, bf16[128,1536]{1,0:T(8,128)(2,1)}) custom-call(f32[128,1536]{1,0:T(8,128)S(1)} %get-tuple-element.22.gate_ref, f32[128,1536]{1,0:T(8,128)S(1)} %get-tuple-element.23.up_ref, f32[8,128]{1,0:T(8,128)S(1)} %get-tuple-element.29._, f32[80,1536]{1,0:T(8,128)S(1)} %convert_add_fusion.refs_0_, ...), custom_call_target="tpu_custom_call" | custom-call | flops 1572864 | bytes 3145728 | tf_op jit(solution)/shard_map/last_step/pallas_call | solution.py:346
  (38 shorter events, 1.3 us)
Async XLA Ops:
  2.3 5.4 %collective-permute-start.8 = (bf16[16,1792]{1,0:T(8,128)(2,1)}, bf16[16,1792]{1,0:T(8,128)(2,1)S(1)}, u32[]{:S(2)}, u32[]{:S(2)}) collective-permute-start(bf16[16,1792]{1,0:T(8,128)(2,1)} %get-tuple-element.26), channel_id=1, source_target_pairs={{0,16},{1,17},{2,18},{3,19},{4,20},{5,21},{6,22},{7,23},{8,24},{9,... | collective-permute-start | bytes 172040 | tf_op jit(solution)/shard_map/ppermute | solution.py:379
  5.3 4.2 %collective-permute-start.9 = (bf16[16,1792]{1,0:T(8,128)(2,1)}, bf16[16,1792]{1,0:T(8,128)(2,1)S(1)}, u32[]{:S(2)}, u32[]{:S(2)}) collective-permute-start(bf16[16,1792]{1,0:T(8,128)(2,1)} %get-tuple-element.27), channel_id=1, source_target_pairs={{0,24},{1,25},{2,26},{3,27},{4,28},{5,29},{6,30},{7,31},{8,16},{9,... | collective-permute-start | bytes 172040 | tf_op jit(solution)/shard_map/ppermute | solution.py:379
  5.3 5.7 %collective-permute-start = (bf16[16,1792]{1,0:T(8,128)(2,1)}, bf16[16,1792]{1,0:T(8,128)(2,1)S(1)}, u32[]{:S(2)}, u32[]{:S(2)}) collective-permute-start(bf16[16,1792]{1,0:T(8,128)(2,1)} %get-tuple-element.25), channel_id=1, source_target_pairs={{0,8},{1,9},{2,10},{3,11},{4,12},{5,13},{6,14},{7,15},{8,0},{9,1},... | collective-permute-start | bytes 172040 | tf_op jit(solution)/shard_map/ppermute | solution.py:379
  9.4 7.2 %collective-permute-start.11 = (bf16[32,1792]{1,0:T(8,128)(2,1)S(1)}, bf16[32,1792]{1,0:T(8,128)(2,1)S(1)}, u32[]{:S(2)}, u32[]{:S(2)}) collective-permute-start(bf16[32,1792]{1,0:T(8,128)(2,1)S(1)} %constant_dynamic-update-slice_fusion.2.refs_8_.refs_5_), channel_id=1, source_target_pairs={{0,1},{1,3},{2,0},{3,5},{4,2},{5,7},{6,4},{7,6},{8,9},{9,11},{10,8... | collective-permute-start | bytes 344072 | tf_op jit(solution)/shard_map/ppermute | solution.py:379
  11.0 7.6 %collective-permute-start.1 = (bf16[32,1792]{1,0:T(8,128)(2,1)S(1)}, bf16[32,1792]{1,0:T(8,128)(2,1)S(1)}, u32[]{:S(2)}, u32[]{:S(2)}) collective-permute-start(bf16[32,1792]{1,0:T(8,128)(2,1)S(1)} %constant_dynamic-update-slice_fusion.refs_0_), channel_id=1, source_target_pairs={{0,2},{1,0},{2,4},{3,1},{4,6},{5,3},{6,7},{7,5},{8,10},{9,8},{10,1... | collective-permute-start | bytes 344072 | tf_op jit(solution)/shard_map/ppermute | solution.py:379
  11.5 7.2 %collective-permute-start.10 = (bf16[32,1792]{1,0:T(8,128)(2,1)S(1)}, bf16[32,1792]{1,0:T(8,128)(2,1)S(1)}, u32[]{:S(2)}, u32[]{:S(2)}) collective-permute-start(bf16[32,1792]{1,0:T(8,128)(2,1)S(1)} %constant_dynamic-update-slice_fusion.2.refs_8_.refs_5_), channel_id=1, source_target_pairs={{0,2},{1,0},{2,4},{3,1},{4,6},{5,3},{6,7},{7,5},{8,10},{9,8},{10,1... | collective-permute-start | bytes 344072 | tf_op jit(solution)/shard_map/ppermute | solution.py:379
  13.1 7.6 %collective-permute-start.2 = (bf16[32,1792]{1,0:T(8,128)(2,1)S(1)}, bf16[32,1792]{1,0:T(8,128)(2,1)S(1)}, u32[]{:S(2)}, u32[]{:S(2)}) collective-permute-start(bf16[32,1792]{1,0:T(8,128)(2,1)S(1)} %constant_dynamic-update-slice_fusion.refs_0_), channel_id=1, source_target_pairs={{0,1},{1,3},{2,0},{3,5},{4,2},{5,7},{6,4},{7,6},{8,9},{9,11},{10,8... | collective-permute-start | bytes 344072 | tf_op jit(solution)/shard_map/ppermute | solution.py:379
  13.6 1.0 %copy-start = (bf16[128,1536]{1,0:T(8,128)(2,1)S(1)}, bf16[128,1536]{1,0:T(8,128)(2,1)}, u32[]{:S(2)}) copy-start(bf16[128,1536]{1,0:T(8,128)(2,1)} %gate_ref.1) | copy-start | bytes 1179652
  14.5 1.0 %copy-start.1 = (bf16[128,1536]{1,0:T(8,128)(2,1)S(1)}, bf16[128,1536]{1,0:T(8,128)(2,1)}, u32[]{:S(2)}) copy-start(bf16[128,1536]{1,0:T(8,128)(2,1)} %up_ref.1) | copy-start | bytes 1179652
  16.1 15.7 %collective-permute-start.18 = (bf16[128,1536]{1,0:T(8,128)(2,1)S(1)}, bf16[128,1536]{1,0:T(8,128)(2,1)S(1)}, u32[]{:S(2)}, u32[]{:S(2)}) collective-permute-start(bf16[128,1536]{1,0:T(8,128)(2,1)S(1)} %get-tuple-element.28.refs_16_), channel_id=1, source_target_pairs={{0,16},{1,17},{2,18},{3,19},{4,20},{5,21},{6,22},{7,23},{8,24},{9,... | collective-permute-start | bytes 1179656 | tf_op jit(solution)/shard_map/ppermute | solution.py:379
  16.6 8.7 %collective-permute-start.13 = (bf16[32,1792]{1,0:T(8,128)(2,1)S(1)}, bf16[32,1792]{1,0:T(8,128)(2,1)S(1)}, u32[]{:S(2)}, u32[]{:S(2)}) collective-permute-start(bf16[32,1792]{1,0:T(8,128)(2,1)S(1)} %collective-permute-done.11.refs_10_.refs_7_), channel_id=1, source_target_pairs={{0,1},{1,3},{2,0},{3,5},{4,2},{5,7},{6,4},{7,6},{8,9},{9,11},{10,8... | collective-permute-start | bytes 344072 | tf_op jit(solution)/shard_map/ppermute | solution.py:379
  18.6 8.7 %collective-permute-start.3 = (bf16[32,1792]{1,0:T(8,128)(2,1)S(1)}, bf16[32,1792]{1,0:T(8,128)(2,1)S(1)}, u32[]{:S(2)}, u32[]{:S(2)}) collective-permute-start(bf16[32,1792]{1,0:T(8,128)(2,1)S(1)} %collective-permute-done.1.refs_1_), channel_id=1, source_target_pairs={{0,2},{1,0},{2,4},{3,1},{4,6},{5,3},{6,7},{7,5},{8,10},{9,8},{10,1... | collective-permute-start | bytes 344072 | tf_op jit(solution)/shard_map/ppermute | solution.py:379
  18.7 8.7 %collective-permute-start.12 = (bf16[32,1792]{1,0:T(8,128)(2,1)S(1)}, bf16[32,1792]{1,0:T(8,128)(2,1)S(1)}, u32[]{:S(2)}, u32[]{:S(2)}) collective-permute-start(bf16[32,1792]{1,0:T(8,128)(2,1)S(1)} %collective-permute-done.10.refs_9_.refs_6_), channel_id=1, source_target_pairs={{0,2},{1,0},{2,4},{3,1},{4,6},{5,3},{6,7},{7,5},{8,10},{9,8},{10,1... | collective-permute-start | bytes 344072 | tf_op jit(solution)/shard_map/ppermute | solution.py:379
  20.7 6.7 %collective-permute-start.4 = (bf16[32,1792]{1,0:T(8,128)(2,1)S(1)}, bf16[32,1792]{1,0:T(8,128)(2,1)S(1)}, u32[]{:S(2)}, u32[]{:S(2)}) collective-permute-start(bf16[32,1792]{1,0:T(8,128)(2,1)S(1)} %collective-permute-done.2.refs_2_), channel_id=1, source_target_pairs={{0,1},{1,3},{2,0},{3,5},{4,2},{5,7},{6,4},{7,6},{8,9},{9,11},{10,8... | collective-permute-start | bytes 344072 | tf_op jit(solution)/shard_map/ppermute | solution.py:379
  25.3 6.6 %collective-permute-start.15 = (bf16[32,1792]{1,0:T(8,128)(2,1)S(1)}, bf16[32,1792]{1,0:T(8,128)(2,1)S(1)}, u32[]{:S(2)}, u32[]{:S(2)}) collective-permute-start(bf16[32,1792]{1,0:T(8,128)(2,1)S(1)} %collective-permute-done.13.refs_12_.refs_9_), channel_id=1, source_target_pairs={{0,1},{1,3},{2,0},{3,5},{4,2},{5,7},{6,4},{7,6},{8,9},{9,11},{10,8... | collective-permute-start | bytes 344072 | tf_op jit(solution)/shard_map/ppermute | solution.py:379
  27.3 6.5 %collective-permute-start.5 = (bf16[32,1792]{1,0:T(8,128)(2,1)S(1)}, bf16[32,1792]{1,0:T(8,128)(2,1)S(1)}, u32[]{:S(2)}, u32[]{:S(2)}) collective-permute-start(bf16[32,1792]{1,0:T(8,128)(2,1)S(1)} %collective-permute-done.3.refs_3_), channel_id=1, source_target_pairs={{0,2},{1,0},{2,4},{3,1},{4,6},{5,3},{6,7},{7,5},{8,10},{9,8},{10,1... | collective-permute-start | bytes 344072 | tf_op jit(solution)/shard_map/ppermute | solution.py:379
  29.8 11.8 %collective-permute-start.20 = (bf16[80,1536]{1,0:T(8,128)(2,1)S(1)}, bf16[80,1536]{1,0:T(8,128)(2,1)S(1)}, u32[]{:S(2)}, u32[]{:S(2)}) collective-permute-start(bf16[80,1536]{1,0:T(8,128)(2,1)S(1)} %get-tuple-element.31), channel_id=1, source_target_pairs={{0,8},{1,9},{2,10},{3,11},{4,12},{5,13},{6,14},{7,15},{8,0},{9,1},... | collective-permute-start | bytes 737288 | tf_op jit(solution)/shard_map/ppermute | solution.py:379
  29.8 5.7 %collective-permute-start.14 = (bf16[32,1792]{1,0:T(8,128)(2,1)S(1)}, bf16[32,1792]{1,0:T(8,128)(2,1)S(1)}, u32[]{:S(2)}, u32[]{:S(2)}) collective-permute-start(bf16[32,1792]{1,0:T(8,128)(2,1)S(1)} %collective-permute-done.12.refs_11_.refs_8_), channel_id=1, source_target_pairs={{0,2},{1,0},{2,4},{3,1},{4,6},{5,3},{6,7},{7,5},{8,10},{9,8},{10,1... | collective-permute-start | bytes 344072 | tf_op jit(solution)/shard_map/ppermute | solution.py:379
  31.8 6.0 %collective-permute-start.6 = (bf16[32,1792]{1,0:T(8,128)(2,1)S(1)}, bf16[32,1792]{1,0:T(8,128)(2,1)S(1)}, u32[]{:S(2)}, u32[]{:S(2)}) collective-permute-start(bf16[32,1792]{1,0:T(8,128)(2,1)S(1)} %collective-permute-done.4.refs_4_), channel_id=1, source_target_pairs={{0,1},{1,3},{2,0},{3,5},{4,2},{5,7},{6,4},{7,6},{8,9},{9,11},{10,8... | collective-permute-start | bytes 344072 | tf_op jit(solution)/shard_map/ppermute | solution.py:379
  31.9 7.6 %collective-permute-start.16 = (bf16[32,1792]{1,0:T(8,128)(2,1)S(1)}, bf16[32,1792]{1,0:T(8,128)(2,1)S(1)}, u32[]{:S(2)}, u32[]{:S(2)}) collective-permute-start(bf16[32,1792]{1,0:T(8,128)(2,1)S(1)} %collective-permute-done.15.refs_14_.refs_4_), channel_id=1, source_target_pairs={{0,1},{1,3},{2,0},{3,5},{4,2},{5,7},{6,4},{7,6},{8,9},{9,11},{10,8... | collective-permute-start | bytes 344072 | tf_op jit(solution)/shard_map/ppermute | solution.py:379
  33.8 5.7 %collective-permute-start.7 = (bf16[32,1792]{1,0:T(8,128)(2,1)S(1)}, bf16[32,1792]{1,0:T(8,128)(2,1)S(1)}, u32[]{:S(2)}, u32[]{:S(2)}) collective-permute-start(bf16[32,1792]{1,0:T(8,128)(2,1)S(1)} %collective-permute-done.5.refs_5_.refs_0_), channel_id=1, source_target_pairs={{0,2},{1,0},{2,4},{3,1},{4,6},{5,3},{6,7},{7,5},{8,10},{9,8},{10,1... | collective-permute-start | bytes 344072 | tf_op jit(solution)/shard_map/ppermute | solution.py:379
  35.5 7.7 %collective-permute-start.17 = (bf16[128,1536]{1,0:T(8,128)(2,1)S(1)}, bf16[128,1536]{1,0:T(8,128)(2,1)S(1)}, u32[]{:S(2)}, u32[]{:S(2)}) collective-permute-start(bf16[128,1536]{1,0:T(8,128)(2,1)S(1)} %get-tuple-element.28.refs_16_), channel_id=1, source_target_pairs={{0,8},{1,9},{2,10},{3,11},{4,12},{5,13},{6,14},{7,15},{8,0},{9,1},... | collective-permute-start | bytes 1179656 | tf_op jit(solution)/shard_map/ppermute | solution.py:379
  37.8 4.9 %collective-permute-start.21 = (bf16[80,1536]{1,0:T(8,128)(2,1)S(1)}, bf16[80,1536]{1,0:T(8,128)(2,1)S(1)}, u32[]{:S(2)}, u32[]{:S(2)}) collective-permute-start(bf16[80,1536]{1,0:T(8,128)(2,1)S(1)} %get-tuple-element.33), channel_id=1, source_target_pairs={{0,8},{1,9},{2,10},{3,11},{4,12},{5,13},{6,14},{7,15},{8,0},{9,1},... | collective-permute-start | bytes 737288 | tf_op jit(solution)/shard_map/ppermute | solution.py:379
  39.5 4.9 %collective-permute-start.19 = (bf16[128,1536]{1,0:T(8,128)(2,1)S(1)}, bf16[128,1536]{1,0:T(8,128)(2,1)S(1)}, u32[]{:S(2)}, u32[]{:S(2)}) collective-permute-start(bf16[128,1536]{1,0:T(8,128)(2,1)S(1)} %collective-permute-done.18.refs_18_), channel_id=1, source_target_pairs={{0,8},{1,9},{2,10},{3,11},{4,12},{5,13},{6,14},{7,15},{8,0},{9,1},... | collective-permute-start | bytes 1179656 | tf_op jit(solution)/shard_map/ppermute | solution.py:379
  41.0 8.8 %collective-permute-start.23 = (bf16[48,1536]{1,0:T(8,128)(2,1)S(1)}, bf16[48,1536]{1,0:T(8,128)(2,1)S(1)}, u32[]{:S(2)}, u32[]{:S(2)}) collective-permute-start(bf16[48,1536]{1,0:T(8,128)(2,1)S(1)} %get-tuple-element.35), channel_id=1, source_target_pairs={{0,8},{1,9},{2,10},{3,11},{4,12},{5,13},{6,14},{7,15},{8,0},{9,1},... | collective-permute-start | bytes 442376 | tf_op jit(solution)/shard_map/ppermute | solution.py:379
  41.6 8.2 %collective-permute-start.24 = (bf16[48,1536]{1,0:T(8,128)(2,1)S(1)}, bf16[48,1536]{1,0:T(8,128)(2,1)S(1)}, u32[]{:S(2)}, u32[]{:S(2)}) collective-permute-start(bf16[48,1536]{1,0:T(8,128)(2,1)S(1)} %get-tuple-element.36), channel_id=1, source_target_pairs={{0,16},{1,17},{2,18},{3,19},{4,20},{5,21},{6,22},{7,23},{8,24},{9,... | collective-permute-start | bytes 442376 | tf_op jit(solution)/shard_map/ppermute | solution.py:379
  42.8 7.3 %collective-permute-start.25 = (bf16[48,1536]{1,0:T(8,128)(2,1)S(1)}, bf16[48,1536]{1,0:T(8,128)(2,1)S(1)}, u32[]{:S(2)}, u32[]{:S(2)}) collective-permute-start(bf16[48,1536]{1,0:T(8,128)(2,1)S(1)} %get-tuple-element.37), channel_id=1, source_target_pairs={{0,24},{1,25},{2,26},{3,27},{4,28},{5,29},{6,30},{7,31},{8,16},{9,... | collective-permute-start | bytes 442376 | tf_op jit(solution)/shard_map/ppermute | solution.py:379
  43.2 12.6 %collective-permute-start.22 = (bf16[80,1536]{1,0:T(8,128)(2,1)S(1)}, bf16[80,1536]{1,0:T(8,128)(2,1)S(1)}, u32[]{:S(2)}, u32[]{:S(2)}) collective-permute-start(bf16[80,1536]{1,0:T(8,128)(2,1)S(1)} %add_convert_fusion), channel_id=1, source_target_pairs={{0,16},{1,17},{2,18},{3,19},{4,20},{5,21},{6,22},{7,23},{8,24},{9,... | collective-permute-start | bytes 737288 | tf_op jit(solution)/shard_map/ppermute | solution.py:379

commit v3 on v2

--- a/solution.py
+++ b/solution.py
@@ -96,31 +96,41 @@
     return result
 
 
-def split_columns(out_grad, parts):
+def split_columns(out_grad, gate_pre, up_pre, parts):
     rows, width = out_grad.shape
     part = width // parts
 
-    def body(grad_ref, *refs):
-        outs, sems = refs[:parts], refs[parts]
+    def body(grad_ref, gate_ref, up_ref, own, other, send, gate_out, up_out, sems):
         me = lax.axis_index("dp")
-        copies = []
-        for j in range(parts):
-            start = pl.multiple_of((me ^ j) * part, TILE)
-            copies.append(
-                pltpu.make_async_copy(grad_ref.at[:, pl.ds(start, part)], outs[j], sems.at[j])
+        pairs = [
+            (grad_ref.at[:, pl.ds(pl.multiple_of((me ^ flips) * part, TILE), part)], target)
+            for flips, target in (
+                (2, send.at[pl.ds(0, rows)]),
+                (3, send.at[pl.ds(rows, rows)]),
+                (0, own),
+                (1, other),
             )
-            copies[-1].start()
+        ]
+        pairs += [(gate_ref, gate_out), (up_ref, up_out)]
+        copies = [
+            pltpu.make_async_copy(source, target, sems.at[i])
+            for i, (source, target) in enumerate(pairs)
+        ]
+        for copy in copies:
+            copy.start()
         for copy in copies:
             copy.wait()
 
     return pl.pallas_call(
         body,
         name="split_columns",
-        out_shape=[like(rows, part)] * parts,
-        in_specs=[HBM],
-        out_specs=[VMEM] * parts,
-        scratch_shapes=[pltpu.SemaphoreType.DMA((parts,))],
-    )(out_grad)
+        out_shape=[pltpu.VMEM((rows, part), BF16)] * 2
+        + [pltpu.VMEM((2 * rows, part), BF16)]
+        + [pltpu.VMEM(gate_pre.shape, BF16)] * 2,
+        in_specs=[HBM] * 3,
+        out_specs=[VMEM] * 5,
+        scratch_shapes=[pltpu.SemaphoreType.DMA((6,))],
+    )(out_grad, gate_pre, up_pre)
 
 
 def hidden_quant(gate_pre, up_pre):
@@ -149,14 +159,14 @@
     )(gate_pre, up_pre)
 
 
-def weight_rows(down_weight, scales, parts):
+def weight_rows(down_weight, scales, parts, flips):
     width, units = down_weight.shape
     part = width // parts
     chunk = 2 * TILE
     count = part // chunk
 
     def body(scale_ref, weight_ref, out_ref, sems):
-        me = lax.axis_index("dp")
+        me = lax.axis_index("dp") ^ flips
         copies = []
         for i in range(count):
             start = pl.multiple_of(me * part + i * chunk, TILE)
@@ -184,64 +194,80 @@
         in_specs=[SMEM, HBM],
         out_specs=VMEM,
         scratch_shapes=[pltpu.SemaphoreType.DMA((count,))],
-        compiler_params=pltpu.CompilerParams(vmem_limit_bytes=48 * MIB),
+        compiler_params=pltpu.CompilerParams(vmem_limit_bytes=44 * MIB),
         cost_estimate=pl.CostEstimate(flops=part * units, bytes_accessed=4 * part * units, transcendentals=0),
     )(scales, down_weight)
 
 
-def partial_hidden(pieces_p, pieces_q, weight):
-    count = len(pieces_p)
-    rows2, part = pieces_p[0].shape
-    rows = rows2 // 2
-    units = weight.shape[1]
-    each = count * rows
+def grouped(refs, sizes):
+    result, at = [], 0
+    for size in sizes:
+        result.append(refs[at : at + size])
+        at += size
+    return result
+
+
+def half_of(piece, h):
+    return (piece[0], h * piece[0].shape[0] // 2) if len(piece) == 1 else (piece[h], 0)
+
+
+def partial_hidden(rows, pieces, weights):
+    sizes = [len(p) for p in pieces]
+    flat = [a for p in pieces for a in p]
+    part, units = weights[0].shape
+    each = len(pieces) * rows
     step = 512 if units % 512 == 0 else 256
 
     def body(*refs):
-        groups = refs[:count], refs[count : 2 * count]
-        weight_ref = refs[2 * count]
-        outs = refs[2 * count + 1 : 2 * count + 5]
-        quant_ref = refs[2 * count + 5]
-        for half, group in enumerate(groups):
-            for k, ref in enumerate(group):
+        first_ref, second_ref, keep_ref, send_ref, quant_ref = refs[len(flat) :]
+        for k, piece in enumerate(grouped(refs, sizes)):
+            for h in range(2):
+                ref, low = half_of(piece, h)
                 for c in range(part // TILE):
                     cols = slice(c * TILE, (c + 1) * TILE)
-                    deq = fast_quant(ref[:, cols].astype(F32), 1)
+                    deq = fast_quant(ref[low : low + 2 * rows, cols].astype(F32), 1)
+                    into = slice(h * part + c * TILE, h * part + (c + 1) * TILE)
                     for s in range(2):
-                        base = (2 * half + s) * each + k * rows
-                        quant_ref[base : base + rows, cols] = deq[s * rows : (s + 1) * rows]
+                        base = s * each + k * rows
+                        quant_ref[base : base + rows, into] = deq[s * rows : (s + 1) * rows]
         for i in range(units // step):
             cols = slice(i * step, (i + 1) * step)
-            result = jnp.dot(quant_ref[...], weight_ref[:, cols], preferred_element_type=F32)
-            for j, out in enumerate(outs):
-                out[:, cols] = result[j * each : (j + 1) * each].astype(BF16)
+            result = jnp.dot(quant_ref[:, :part], first_ref[:, cols], preferred_element_type=F32)
+            result += jnp.dot(quant_ref[:, part:], second_ref[:, cols], preferred_element_type=F32)
+            keep_ref[:, cols] = result[:each].astype(keep_ref.dtype)
+            send_ref[:, cols] = result[each:].astype(BF16)
 
     return pl.pallas_call(
         body,
         name="partial_hidden",
-        out_shape=[like(each, units)] * 4,
-        in_specs=[VMEM] * (2 * count + 1),
-        out_specs=[VMEM] * 4,
-        scratch_shapes=[pltpu.VMEM((4 * each, part), BF16)],
-        compiler_params=pltpu.CompilerParams(vmem_limit_bytes=24 * MIB),
+        out_shape=[like(each, units, dtype=F32), like(each, units)],
+        in_specs=[VMEM] * (len(flat) + 2),
+        out_specs=[VMEM] * 2,
+        scratch_shapes=[pltpu.VMEM((2 * each, 2 * part), BF16)],
+        compiler_params=pltpu.CompilerParams(vmem_limit_bytes=16 * MIB),
         cost_estimate=pl.CostEstimate(
-            flops=8 * each * part * units, bytes_accessed=2 * part * units, transcendentals=0
+            flops=8 * each * part * units, bytes_accessed=4 * part * units, transcendentals=0
         ),
-    )(*pieces_p, *pieces_q, weight)
-
-
-def down_product(n_tp, offsets, pieces_p, pieces_q, hiddens):
-    count = len(pieces_p)
-    rows2, part = pieces_p[0].shape
-    rows = rows2 // 2
+    )(*flat, *weights)
+
+
+def down_product(n_tp, offsets, pieces, others, hiddens):
+    flat = [p[0] for p in pieces] + list(others)
+    part = flat[0].shape[1]
     tokens, units = hiddens[0].shape
+    rows = tokens // len(pieces)
     step, slots, split = 256, 3, 4
     steps = part // step
 
     def body(*refs):
-        groups = refs[:count], refs[count : 2 * count]
-        h_refs = refs[2 * count : 2 * count + 4]
-        out_ref, token_ref, hid_ref, quant_ref, buffer, sems = refs[2 * count + 4 :]
+        own, other = refs[: len(pieces)], refs[len(pieces) : len(flat)]
+        where = [[(ref, s * rows) for ref in own] for s in range(2)]
+        where += [
+            [(ref, low + s * rows) for ref in other for low in range(0, ref.shape[0], 2 * rows)]
+            for s in range(2)
+        ]
+        h_refs = refs[len(flat) : len(flat) + 4]
+        out_ref, token_ref, hid_ref, quant_ref, buffer, sems = refs[len(flat) + 4 :]
         token_ref[...] = jnp.zeros(token_ref.shape, F32)
         starts = [pl.multiple_of(s * rows, rows) for s in ring_sources(n_tp, offsets)]
         for j, ref in enumerate(h_refs):
@@ -267,8 +293,7 @@
             for c in range(step // TILE):
                 cols = slice(i * step + c * TILE, i * step + (c + 1) * TILE)
                 for j in range(4):
-                    low = (j % 2) * rows
-                    vals = [ref[low : low + rows, cols].astype(F32) for ref in groups[j // 2]]
+                    vals = [ref[low : low + rows, cols].astype(F32) for ref, low in where[j]]
                     top = jnp.abs(vals[0])
                     for v in vals[1:]:
                         top = jnp.maximum(top, jnp.abs(v))
@@ -293,7 +318,7 @@
         body,
         name="down_product",
         out_shape=[like(part, units), like(8, TILE, dtype=F32)],
-        in_specs=[VMEM] * (2 * count + 4),
+        in_specs=[VMEM] * (len(flat) + 4),
         out_specs=[HBM, VMEM],
         scratch_shapes=[
             pltpu.VMEM((4 * tokens, units), BF16),
@@ -305,13 +330,12 @@
         cost_estimate=pl.CostEstimate(
             flops=8 * part * tokens * units, bytes_accessed=2 * part * units, transcendentals=0
         ),
-    )(*pieces_p, *pieces_q, *hiddens)
-
-
-def last_step(n_tp, offsets, gate_factor, up_factor, groups, after):
+    )(*flat, *hiddens)
+
+
+def last_step(n_tp, offsets, gate_factor, up_factor, groups, lengths, token):
     tokens, units = gate_factor.shape
     sizes = [len(g) for g in groups]
-    lengths = [g[0].shape[0] for g in groups]
     flat = [a for g in groups for a in g]
     rows = tokens // len(offsets)
     split = 2
@@ -355,13 +379,11 @@
         cost_estimate=pl.CostEstimate(
             flops=8 * tokens * units, bytes_accessed=16 * tokens * units, transcendentals=0
         ),
-    )(gate_factor, up_factor, after, *flat)
-
-
-def fold(own, received):
-    return (own[0].astype(F32) + received[0].astype(F32)), (
-        own[1].astype(F32) + received[1].astype(F32)
-    ).astype(BF16)
+    )(gate_factor, up_factor, token, *flat)
+
+
+def after(value, *others):
+    return lax.optimization_barrier((value, *others))[0]
 
 
 def pair_mesh(n_tp, out_grad, gate_pre, up_pre, down_weight, block_scales):
@@ -387,47 +409,67 @@
     def send_down(value):
         return permute(value, lambda d, t: (d, down[t]))
 
+    rows = out_grad.shape[0]
     offsets = [0]
     for k in range(1, half):
         offsets += [-k, k]
     offsets.append(half)
 
-    parts = split_columns(out_grad, 4)
-    from_core = flip(parts[1], 1)
-    from_chip = flip(parts[2], 2)
-    from_far = flip(parts[3], 3)
-    hidden_own, gate_factor, up_factor = hidden_quant(gate_pre, up_pre)
-    weight = weight_rows(down_weight, block_scales.astype(F32), 4)
-    block_p = jnp.concatenate([parts[0], from_core], axis=0)
-    block_q = jnp.concatenate([from_chip, from_far], axis=0)
-
-    pieces_p, pieces_q = {0: block_p}, {0: block_q}
-    for k in range(1, half + 1):
-        pieces_p[-k] = send_up(pieces_p[1 - k])
-        if k < half:
-            pieces_p[k] = send_down(pieces_p[k - 1])
-            pieces_q[-k] = send_up(pieces_q[1 - k])
-        pieces_q[k] = send_down(pieces_q[k - 1])
-    pieces_p[half] = pieces_p[-half]
-    list_p = [pieces_p[o] for o in offsets]
-    list_q = [pieces_q[o] for o in offsets]
-
+    own, other, send, gate_here, up_here = split_columns(out_grad, gate_pre, up_pre, 4)
+    arrived = flip(send, 2)
+    scales = after(block_scales, own).astype(F32)
+    hidden_own, gate_factor, up_factor = hidden_quant(after(gate_here, scales), up_here)
+    arrived = after(arrived, hidden_own)
+    block = jnp.concatenate([own, arrived[:rows], other, arrived[rows:]], axis=0)
+    weight_own = weight_rows(down_weight, after(scales, block), 4, 0)
     hidden_chip = flip(hidden_own, 2)
     hidden_core = flip(hidden_own, 1)
+
+    got = {0: block}
+    weights = None
+    for k in range(1, half):
+        low, high = got[1 - k], got[k - 1]
+        if k == 2:
+            low, high = after(low, weight_own), after(high, weight_own)
+            weight_other = weight_rows(down_weight, after(scales, hidden_chip), 4, 1)
+            weights = weight_own, weight_other
+        if k == 3:
+            low, high = after(low, weights[1]), after(high, weights[1])
+        got[-k], got[k] = send_up(low), send_down(high)
+    first = n_tp - 3
     hidden_far = flip(hidden_chip, 1)
-
-    first = n_tp - 3
-    groups = []
-    part1 = partial_hidden(list_p[:first], list_q[:first], weight)
-    got0, got2 = flip(part1[1], 1), flip(part1[3], 1)
-    sum0, sum2 = fold((part1[0], part1[2]), (got0, got2))
-    groups.append([sum0, flip(sum2, 2)])
-    part2 = partial_hidden(list_p[first:], list_q[first:], weight)
-    groups.append([part2[0]] + [flip(part2[j], j) for j in (1, 2, 3)])
+    part1 = partial_hidden(
+        rows,
+        [[got[o]] for o in offsets[:first]],
+        (after(weights[0], hidden_far, hidden_core), weights[1]),
+    )
+    last = [send_up(after(got[1 - half], part1[0]))]
+    pieces = [[got[o]] for o in offsets[:-1]] + [last]
+
+    sum1 = flip(part1[1], 2)
+    other1 = flip(jnp.concatenate([got[o][2 * rows :] for o in offsets[:first]], axis=0), 1)
+    late = [after(a, sum1) for a in last]
+    other2 = flip(
+        jnp.concatenate([got[o][2 * rows :] for o in offsets[first:-1]] + [late[0][2 * rows :]], axis=0), 1
+    )
+    part2 = partial_hidden(rows, pieces[first:-1] + [late], weights)
+    sum2 = flip(part2[1], 2)
     down_grad, token = down_product(
-        n_tp, offsets, list_p, list_q, [hidden_own, hidden_core, hidden_chip, hidden_far]
-    )
-    gate_grad, up_grad = last_step(n_tp, offsets, gate_factor, up_factor, groups, token)
+        n_tp,
+        offsets,
+        pieces,
+        [other1, other2],
+        [hidden_own, hidden_chip, hidden_core, hidden_far],
+    )
+    gate_grad, up_grad = last_step(
+        n_tp,
+        offsets,
+        gate_factor,
+        up_factor,
+        [[part1[0], sum1], [part2[0], sum2]],
+        [first * rows, 3 * rows],
+        token,
+    )
     return gate_grad, up_grad, down_grad
 
 
@@ -439,7 +481,7 @@
         rows = out_grad.shape[0]
         fits = (
             n_dp == 4
-            and n_tp >= 4
+            and n_tp >= 8
             and n_tp % 2 == 0
             and rows % 16 == 0
             and rows * n_tp == 128

time: 57.3 us -> 48.9 us (0.85)
  starting transfers between devices: 21.5 us -> 15.1 us
  Pallas kernels: 16.2 us -> 20.3 us
  waiting for transfers between devices: 14.8 us -> 11.6 us
  local copies, waits for them, and re-layouts: 3.61 us -> 0.87 us
    ppermute x26 -> x15, starting transfers between devices: 21.5 us -> 15.1 us  [permute(): return lax.ppermute(value, BOTH, pairs)]
    pallas_call x1 -> x2, Pallas kernels: 3.77 us -> 7.54 us  [weight_rows(): pl.pallas_call(body, name='weight_rows', out_shape=like(part, units), in_...]
    ppermute x26 -> x15, waiting for transfers between devices: 14.8 us -> 11.6 us  [permute(): return lax.ppermute(value, BOTH, pairs)]
    unnamed x6 -> x5, local copies, waits for them, and re-layouts: 2.82 us -> 0.04 us
    optimization_barrier x0 -> x1, local copies, waits for them, and re-layouts: none -> 0.79 us  [after(): return lax.optimization_barrier((value, *others))[0]]
    convert_element_type x1 -> x0, local copies, waits for them, and re-layouts: 0.78 us -> none  [pair_mesh(): weight = weight_rows(down_weight, block_scales.astype(F32), 4)]
  transfers between devices with their start and end apart: 26 -> 15, of which waited for: 7 -> 6; matrix products, arithmetic and copies ran while one was open for 3% -> 2% of each run, Pallas kernels for 24% -> 37%
where the time goes in v3:
time: 48.9 us; the launch traced here: 48.8 us
  Pallas kernels  20.3 us (42%)
  starting transfers between devices  15.1 us (31%)
  waiting for transfers between devices  11.6 us (24%)
  local copies, waits for them, and re-layouts  0.87 us (2%)
  between operations  0.81 us (2%)
    ppermute x15, starting transfers between devices, permute(): return lax.ppermute(value, BOTH, pairs)  15.1 us
    ppermute x15, waiting for transfers between devices, permute(): return lax.ppermute(value, BOTH, pairs)  11.6 us
    pallas_call x2, Pallas kernels, weight_rows(): pl.pallas_call(body, name='weight_rows', out_shape=like(part, units), in_...  7.54 us
    pallas_call x1, Pallas kernels, down_product(): pl.pallas_call(body, name='down_product', out_shape=[like(part, units), l...  5.32 us
    pallas_call x2, Pallas kernels, partial_hidden(): pl.pallas_call(body, name='partial_hidden', out_shape=[like(each, units,...  4.42 us
    pallas_call x1, Pallas kernels, split_columns(): pl.pallas_call(body, name='split_columns', out_shape=[pltpu.VMEM((rows, p...  1.31 us
    pallas_call x1, Pallas kernels, last_step(): pl.pallas_call(body, name='last_step', out_shape=[like(tokens, units)] *...  1.11 us
  transfers between devices with their start and end apart: 15, of which 6 were waited for; matrix products, arithmetic and copies ran while one was open for 2% of the time, Pallas kernels for 37%

profile of v3, /device:TPU:0, one launch (start us, length us, event | category | flops | bytes accessed | tf_op | source)
XLA Modules:
  0.0 48.8 jit_solution(18228876550751932104)
XLA Ops:
  0.6 1.3 %split_columns.1 = (bf16[16,1792]{1,0:T(8,128)(2,1)S(1)}, bf16[16,1792]{1,0:T(8,128)(2,1)S(1)}, bf16[32,1792]{1,0:T(8,128)(2,1)S(1)}, bf16[128,1536]{1,0:T(8,128)(2,1)S(1)}, bf16[128,1536]{1,0:T(8,128)(2,1)S(1)}) custom-call(bf16[16,7168]{1,0:T(8,128)(2,1)} %grad_ref.1, bf16[128,1536]{1,0:T(8,128)(2,1)} %gate_ref.1, bf16[128,1536]{1,0:T(8,128)(2,1)} %up_ref.1), custom_call_target="tpu_custom_call" | custom-call | tf_op jit(solution)/shard_map/split_columns/pallas_call | solution.py:124
  2.0 3.0 %collective-permute-start = (bf16[32,1792]{1,0:T(8,128)(2,1)S(1)}, bf16[32,1792]{1,0:T(8,128)(2,1)S(1)}, u32[]{:S(2)}, u32[]{:S(2)}) collective-permute-start(bf16[32,1792]{1,0:T(8,128)(2,1)S(1)} %get-tuple-element.38), channel_id=1, source_target_pairs={{0,16},{1,17},{2,18},{3,19},{4,20},{5,21},{6,22},{7,23},{8,24},{9,... | collective-permute-start | bytes 344072 | tf_op jit(solution)/shard_map/ppermute | solution.py:401
  5.0 0.8 %copy.8 = bf16[56,12]{1,0:T(8,128)(2,1)S(1)} copy(bf16[56,12]{0,1:T(8,128)(2,1)} %param.9) | data formatting | bytes 2688 | tf_op jit(solution)/shard_map/optimization_barrier | solution.py:386
  5.8 0.6 %hidden_quant.1 = (bf16[128,1536]{1,0:T(8,128)(2,1)S(1)}, f32[128,1536]{1,0:T(8,128)S(1)}, f32[128,1536]{1,0:T(8,128)S(1)}) custom-call(bf16[128,1536]{1,0:T(8,128)(2,1)S(1)} %get-tuple-element.34.gate_ref, bf16[128,1536]{1,0:T(8,128)(2,1)S(1)} %get-tuple-element.35.up_ref), custom_call_target="tpu_custom_call" | custom-call | flops 3932160 | bytes 2752512 | tf_op jit(solution)/shard_map/hidden_quant/pallas_call | solution.py:149
  6.3 1.8 %collective-permute-done = bf16[32,1792]{1,0:T(8,128)(2,1)S(1)} collective-permute-done((bf16[32,1792]{1,0:T(8,128)(2,1)S(1)}, bf16[32,1792]{1,0:T(8,128)(2,1)S(1)}, u32[]{:S(2)}, u32[]{:S(2)}) %collective-permute-start) | collective-permute-done | bytes 114720 | tf_op jit(solution)/shard_map/ppermute | solution.py:401
  8.1 1.8 %collective-permute-start.2 = (bf16[64,1792]{1,0:T(8,128)(2,1)S(1)}, bf16[64,1792]{1,0:T(8,128)(2,1)S(1)}, u32[]{:S(2)}, u32[]{:S(2)}) collective-permute-start(bf16[64,1792]{1,0:T(8,128)(2,1)S(1)} %pad_maximum_fusion.1.refs_0_), channel_id=1, source_target_pairs={{0,1},{1,3},{2,0},{3,5},{4,2},{5,7},{6,4},{7,6},{8,9},{9,11},{10,8... | collective-permute-start | bytes 688136 | tf_op jit(solution)/shard_map/ppermute | solution.py:401
  10.0 0.3 collective-permute-start.1
  10.2 1.7 %collective-permute-start.5 = (bf16[128,1536]{1,0:T(8,128)(2,1)S(1)}, bf16[128,1536]{1,0:T(8,128)(2,1)S(1)}, u32[]{:S(2)}, u32[]{:S(2)}) collective-permute-start(bf16[128,1536]{1,0:T(8,128)(2,1)S(1)} %get-tuple-element.39.refs_10_), channel_id=1, source_target_pairs={{0,16},{1,17},{2,18},{3,19},{4,20},{5,21},{6,22},{7,23},{8,24},{9,... | collective-permute-start | bytes 1179656 | tf_op jit(solution)/shard_map/ppermute | solution.py:401
  12.0 0.0 collective-permute-start.9
  12.0 3.8 %weight_rows.2.refs_5_.refs_3_ = bf16[1792,1536]{1,0:T(8,128)(2,1)S(1)} custom-call(f32[56,12]{1,0:T(8,128)S(1)} %convert_element_type.3.scale_ref, bf16[7168,1536]{1,0:T(8,128)(2,1)} %weight_ref.3), custom_call_target="tpu_custom_call" | custom-call | flops 2752512 | bytes 11010048 | tf_op jit(solution)/shard_map/weight_rows/pallas_call | solution.py:190
  15.7 0.0 collective-permute-done.2.refs_2_
  15.8 1.6 %collective-permute-start.4 = (bf16[64,1792]{1,0:T(8,128)(2,1)S(1)}, bf16[64,1792]{1,0:T(8,128)(2,1)S(1)}, u32[]{:S(2)}, u32[]{:S(2)}) collective-permute-start(bf16[64,1792]{1,0:T(8,128)(2,1)S(1)} %collective-permute-done.2.refs_2_), channel_id=1, source_target_pairs={{0,1},{1,3},{2,0},{3,5},{4,2},{5,7},{6,4},{7,6},{8,9},{9,11},{10,8... | collective-permute-start | bytes 688136 | tf_op jit(solution)/shard_map/ppermute | solution.py:401
  17.3 0.5 %collective-permute-start.3 = (bf16[64,1792]{1,0:T(8,128)(2,1)S(1)}, bf16[64,1792]{1,0:T(8,128)(2,1)S(1)}, u32[]{:S(2)}, u32[]{:S(2)}) collective-permute-start(bf16[64,1792]{1,0:T(8,128)(2,1)S(1)} %collective-permute-done.1.refs_1_), channel_id=1, source_target_pairs={{0,2},{1,0},{2,4},{3,1},{4,6},{5,3},{6,7},{7,5},{8,10},{9,8},{10,1... | collective-permute-start | bytes 688136 | tf_op jit(solution)/shard_map/ppermute | solution.py:401
  17.9 2.1 %collective-permute-done.5.refs_11_ = bf16[128,1536]{1,0:T(8,128)(2,1)S(1)} collective-permute-done((bf16[128,1536]{1,0:T(8,128)(2,1)S(1)}, bf16[128,1536]{1,0:T(8,128)(2,1)S(1)}, u32[]{:S(2)}, u32[]{:S(2)}) %collective-permute-start.5) | collective-permute-done | bytes 393248 | tf_op jit(solution)/shard_map/ppermute | solution.py:401
  20.0 3.8 %weight_rows.3.refs_6_.refs_4_ = bf16[1792,1536]{1,0:T(8,128)(2,1)S(1)} custom-call(f32[56,12]{1,0:T(8,128)S(1)} %convert_element_type.3.scale_ref, bf16[7168,1536]{1,0:T(8,128)(2,1)} %weight_ref.3), custom_call_target="tpu_custom_call" | custom-call | flops 2752512 | bytes 11010048 | tf_op jit(solution)/shard_map/weight_rows/pallas_call | solution.py:190
  23.7 1.3 %collective-permute-done.3.refs_3_ = bf16[64,1792]{1,0:T(8,128)(2,1)S(1)} collective-permute-done((bf16[64,1792]{1,0:T(8,128)(2,1)S(1)}, bf16[64,1792]{1,0:T(8,128)(2,1)S(1)}, u32[]{:S(2)}, u32[]{:S(2)}) %collective-permute-start.3) | collective-permute-done | bytes 229408 | tf_op jit(solution)/shard_map/ppermute | solution.py:401
  25.1 0.5 %collective-permute-start.6 = (bf16[64,1792]{1,0:T(8,128)(2,1)S(1)}, bf16[64,1792]{1,0:T(8,128)(2,1)S(1)}, u32[]{:S(2)}, u32[]{:S(2)}) collective-permute-start(bf16[64,1792]{1,0:T(8,128)(2,1)S(1)} %collective-permute-done.3.refs_3_), channel_id=1, source_target_pairs={{0,2},{1,0},{2,4},{3,1},{4,6},{5,3},{6,7},{7,5},{8,10},{9,8},{10,1... | collective-permute-start | bytes 688136 | tf_op jit(solution)/shard_map/ppermute | solution.py:401
  25.6 1.5 %collective-permute-start.7 = (bf16[64,1792]{1,0:T(8,128)(2,1)S(1)}, bf16[64,1792]{1,0:T(8,128)(2,1)S(1)}, u32[]{:S(2)}, u32[]{:S(2)}) collective-permute-start(bf16[64,1792]{1,0:T(8,128)(2,1)S(1)} %collective-permute-done.4.refs_4_), channel_id=1, source_target_pairs={{0,1},{1,3},{2,0},{3,5},{4,2},{5,7},{6,4},{7,6},{8,9},{9,11},{10,8... | collective-permute-start | bytes 688136 | tf_op jit(solution)/shard_map/ppermute | solution.py:401
  27.1 0.0 collective-permute-done.9.refs_12_
  27.1 0.0 collective-permute-done.8.refs_13_
  27.1 2.4 %partial_hidden.2 = (f32[80,1536]{1,0:T(8,128)S(1)}, bf16[80,1536]{1,0:T(8,128)(2,1)S(1)}) custom-call(bf16[64,1792]{1,0:T(8,128)(2,1)S(1)} %pad_maximum_fusion.1.refs_0_, bf16[64,1792]{1,0:T(8,128)(2,1)S(1)} %collective-permute-done.1.refs_1_, bf16[64,1792]{1,0:T(8,128)(2,1)S(1)} %collective-permute-done.2.refs_2_, ...), custom_call_target="tpu_custom_call" | custom-call | flops 1761607680 | bytes 11010048 | tf_op jit(solution)/shard_map/partial_hidden/pallas_call | solution.py:240
  29.5 0.6 %collective-permute-start.12 = (bf16[80,1536]{1,0:T(8,128)(2,1)S(1)}, bf16[80,1536]{1,0:T(8,128)(2,1)S(1)}, u32[]{:S(2)}, u32[]{:S(2)}) collective-permute-start(bf16[80,1536]{1,0:T(8,128)(2,1)S(1)} %get-tuple-element.51), channel_id=1, source_target_pairs={{0,16},{1,17},{2,18},{3,19},{4,20},{5,21},{6,22},{7,23},{8,24},{9,... | collective-permute-start | bytes 737288 | tf_op jit(solution)/shard_map/ppermute | solution.py:401
  30.1 1.9 %collective-permute-done.6.refs_5_.refs_0_ = bf16[64,1792]{1,0:T(8,128)(2,1)S(1)} collective-permute-done((bf16[64,1792]{1,0:T(8,128)(2,1)S(1)}, bf16[64,1792]{1,0:T(8,128)(2,1)S(1)}, u32[]{:S(2)}, u32[]{:S(2)}) %collective-permute-start.6) | collective-permute-done | bytes 229408 | tf_op jit(solution)/shard_map/ppermute | solution.py:401
  32.0 1.3 %collective-permute-start.10 = (bf16[64,1792]{1,0:T(8,128)(2,1)S(1)}, bf16[64,1792]{1,0:T(8,128)(2,1)S(1)}, u32[]{:S(2)}, u32[]{:S(2)}) collective-permute-start(bf16[64,1792]{1,0:T(8,128)(2,1)S(1)} %collective-permute-done.6.refs_5_.refs_0_), channel_id=1, source_target_pairs={{0,2},{1,0},{2,4},{3,1},{4,6},{5,3},{6,7},{7,5},{8,10},{9,8},{10,1... | collective-permute-start | bytes 688136 | tf_op jit(solution)/shard_map/ppermute | solution.py:401
  33.3 0.1 collective-permute-start.11
  33.5 2.8 %collective-permute-done.12.refs_1_ = bf16[80,1536]{1,0:T(8,128)(2,1)S(1)} collective-permute-done((bf16[80,1536]{1,0:T(8,128)(2,1)S(1)}, bf16[80,1536]{1,0:T(8,128)(2,1)S(1)}, u32[]{:S(2)}, u32[]{:S(2)}) %collective-permute-start.12) | collective-permute-done | bytes 245792 | tf_op jit(solution)/shard_map/ppermute | solution.py:401
  36.3 1.7 %collective-permute-done.10.refs_7_.refs_2_ = bf16[64,1792]{1,0:T(8,128)(2,1)S(1)} collective-permute-done((bf16[64,1792]{1,0:T(8,128)(2,1)S(1)}, bf16[64,1792]{1,0:T(8,128)(2,1)S(1)}, u32[]{:S(2)}, u32[]{:S(2)}) %collective-permute-start.10) | collective-permute-done | bytes 229408 | tf_op jit(solution)/shard_map/ppermute | solution.py:401
  38.1 0.1 collective-permute-start.13
  38.1 2.0 %partial_hidden.3 = (f32[48,1536]{1,0:T(8,128)S(1)}, bf16[48,1536]{1,0:T(8,128)(2,1)S(1)}) custom-call(bf16[64,1792]{1,0:T(8,128)(2,1)S(1)} %collective-permute-done.6.refs_5_.refs_0_, bf16[64,1792]{1,0:T(8,128)(2,1)S(1)} %collective-permute-done.7.refs_6_.refs_1_, bf16[64,1792]{1,0:T(8,128)(2,1)S(1)} %collective-permute-done.10.refs_7_.refs_2_, ...), custom_call_target="tpu_custom_call" | custom-call | flops 1056964608 | bytes 11010048 | tf_op jit(solution)/shard_map/partial_hidden/pallas_call | solution.py:240
  40.2 2.1 %collective-permute-start.14 = (bf16[48,1536]{1,0:T(8,128)(2,1)S(1)}, bf16[48,1536]{1,0:T(8,128)(2,1)S(1)}, u32[]{:S(2)}, u32[]{:S(2)}) collective-permute-start(bf16[48,1536]{1,0:T(8,128)(2,1)S(1)} %get-tuple-element.55), channel_id=1, source_target_pairs={{0,16},{1,17},{2,18},{3,19},{4,20},{5,21},{6,22},{7,23},{8,24},{9,... | collective-permute-start | bytes 442376 | tf_op jit(solution)/shard_map/ppermute | solution.py:401
  42.3 5.3 %down_product.1 = (bf16[1792,1536]{1,0:T(8,128)(2,1)}, f32[8,128]{1,0:T(8,128)S(1)}) custom-call(bf16[64,1792]{1,0:T(8,128)(2,1)S(1)} %pad_maximum_fusion.1.refs_0_, bf16[64,1792]{1,0:T(8,128)(2,1)S(1)} %collective-permute-done.1.refs_1_, bf16[64,1792]{1,0:T(8,128)(2,1)S(1)} %collective-permute-done.2.refs_2_, ...), custom_call_target="tpu_custom_call" | custom-call | flops 2818572288 | bytes 5505024 | tf_op jit(solution)/shard_map/down_product/pallas_call | solution.py:317
  47.6 1.1 %last_step.1 = (bf16[128,1536]{1,0:T(8,128)(2,1)}, bf16[128,1536]{1,0:T(8,128)(2,1)}) custom-call(f32[128,1536]{1,0:T(8,128)S(1)} %get-tuple-element.36.gate_ref, f32[128,1536]{1,0:T(8,128)S(1)} %get-tuple-element.37.up_ref, f32[8,128]{1,0:T(8,128)S(1)} %get-tuple-element.53._, f32[80,1536]{1,0:T(8,128)S(1)} %get-tuple-element.49.refs_0_, ...), custom_call_target="tpu_custom_call" | custom-call | flops 1572864 | bytes 3145728 | tf_op jit(solution)/shard_map/last_step/pallas_call | solution.py:370
  (19 shorter events, 0.1 us)
Async XLA Ops:
  2.0 6.1 %collective-permute-start = (bf16[32,1792]{1,0:T(8,128)(2,1)S(1)}, bf16[32,1792]{1,0:T(8,128)(2,1)S(1)}, u32[]{:S(2)}, u32[]{:S(2)}) collective-permute-start(bf16[32,1792]{1,0:T(8,128)(2,1)S(1)} %get-tuple-element.38), channel_id=1, source_target_pairs={{0,16},{1,17},{2,18},{3,19},{4,20},{5,21},{6,22},{7,23},{8,24},{9,... | collective-permute-start | bytes 344072 | tf_op jit(solution)/shard_map/ppermute | solution.py:401
  8.1 7.6 %collective-permute-start.2 = (bf16[64,1792]{1,0:T(8,128)(2,1)S(1)}, bf16[64,1792]{1,0:T(8,128)(2,1)S(1)}, u32[]{:S(2)}, u32[]{:S(2)}) collective-permute-start(bf16[64,1792]{1,0:T(8,128)(2,1)S(1)} %pad_maximum_fusion.1.refs_0_), channel_id=1, source_target_pairs={{0,1},{1,3},{2,0},{3,5},{4,2},{5,7},{6,4},{7,6},{8,9},{9,11},{10,8... | collective-permute-start | bytes 688136 | tf_op jit(solution)/shard_map/ppermute | solution.py:401
  10.0 7.4 %collective-permute-start.1 = (bf16[64,1792]{1,0:T(8,128)(2,1)S(1)}, bf16[64,1792]{1,0:T(8,128)(2,1)S(1)}, u32[]{:S(2)}, u32[]{:S(2)}) collective-permute-start(bf16[64,1792]{1,0:T(8,128)(2,1)S(1)} %pad_maximum_fusion.1.refs_0_), channel_id=1, source_target_pairs={{0,2},{1,0},{2,4},{3,1},{4,6},{5,3},{6,7},{7,5},{8,10},{9,8},{10,1... | collective-permute-start | bytes 688136 | tf_op jit(solution)/shard_map/ppermute | solution.py:401
  10.2 9.7 %collective-permute-start.5 = (bf16[128,1536]{1,0:T(8,128)(2,1)S(1)}, bf16[128,1536]{1,0:T(8,128)(2,1)S(1)}, u32[]{:S(2)}, u32[]{:S(2)}) collective-permute-start(bf16[128,1536]{1,0:T(8,128)(2,1)S(1)} %get-tuple-element.39.refs_10_), channel_id=1, source_target_pairs={{0,16},{1,17},{2,18},{3,19},{4,20},{5,21},{6,22},{7,23},{8,24},{9,... | collective-permute-start | bytes 1179656 | tf_op jit(solution)/shard_map/ppermute | solution.py:401
  12.0 15.1 %collective-permute-start.9 = (bf16[128,1536]{1,0:T(8,128)(2,1)S(1)}, bf16[128,1536]{1,0:T(8,128)(2,1)S(1)}, u32[]{:S(2)}, u32[]{:S(2)}) collective-permute-start(bf16[128,1536]{1,0:T(8,128)(2,1)S(1)} %get-tuple-element.39.refs_10_), channel_id=1, source_target_pairs={{0,8},{1,9},{2,10},{3,11},{4,12},{5,13},{6,14},{7,15},{8,0},{9,1},... | collective-permute-start | bytes 1179656 | tf_op jit(solution)/shard_map/ppermute | solution.py:401
  15.8 9.8 %collective-permute-start.4 = (bf16[64,1792]{1,0:T(8,128)(2,1)S(1)}, bf16[64,1792]{1,0:T(8,128)(2,1)S(1)}, u32[]{:S(2)}, u32[]{:S(2)}) collective-permute-start(bf16[64,1792]{1,0:T(8,128)(2,1)S(1)} %collective-permute-done.2.refs_2_), channel_id=1, source_target_pairs={{0,1},{1,3},{2,0},{3,5},{4,2},{5,7},{6,4},{7,6},{8,9},{9,11},{10,8... | collective-permute-start | bytes 688136 | tf_op jit(solution)/shard_map/ppermute | solution.py:401
  17.3 7.7 %collective-permute-start.3 = (bf16[64,1792]{1,0:T(8,128)(2,1)S(1)}, bf16[64,1792]{1,0:T(8,128)(2,1)S(1)}, u32[]{:S(2)}, u32[]{:S(2)}) collective-permute-start(bf16[64,1792]{1,0:T(8,128)(2,1)S(1)} %collective-permute-done.1.refs_1_), channel_id=1, source_target_pairs={{0,2},{1,0},{2,4},{3,1},{4,6},{5,3},{6,7},{7,5},{8,10},{9,8},{10,1... | collective-permute-start | bytes 688136 | tf_op jit(solution)/shard_map/ppermute | solution.py:401
  20.0 7.2 %collective-permute-start.8 = (bf16[128,1536]{1,0:T(8,128)(2,1)S(1)}, bf16[128,1536]{1,0:T(8,128)(2,1)S(1)}, u32[]{:S(2)}, u32[]{:S(2)}) collective-permute-start(bf16[128,1536]{1,0:T(8,128)(2,1)S(1)} %collective-permute-done.5.refs_11_), channel_id=1, source_target_pairs={{0,8},{1,9},{2,10},{3,11},{4,12},{5,13},{6,14},{7,15},{8,0},{9,1},... | collective-permute-start | bytes 1179656 | tf_op jit(solution)/shard_map/ppermute | solution.py:401
  25.1 6.9 %collective-permute-start.6 = (bf16[64,1792]{1,0:T(8,128)(2,1)S(1)}, bf16[64,1792]{1,0:T(8,128)(2,1)S(1)}, u32[]{:S(2)}, u32[]{:S(2)}) collective-permute-start(bf16[64,1792]{1,0:T(8,128)(2,1)S(1)} %collective-permute-done.3.refs_3_), channel_id=1, source_target_pairs={{0,2},{1,0},{2,4},{3,1},{4,6},{5,3},{6,7},{7,5},{8,10},{9,8},{10,1... | collective-permute-start | bytes 688136 | tf_op jit(solution)/shard_map/ppermute | solution.py:401
  25.6 7.9 %collective-permute-start.7 = (bf16[64,1792]{1,0:T(8,128)(2,1)S(1)}, bf16[64,1792]{1,0:T(8,128)(2,1)S(1)}, u32[]{:S(2)}, u32[]{:S(2)}) collective-permute-start(bf16[64,1792]{1,0:T(8,128)(2,1)S(1)} %collective-permute-done.4.refs_4_), channel_id=1, source_target_pairs={{0,1},{1,3},{2,0},{3,5},{4,2},{5,7},{6,4},{7,6},{8,9},{9,11},{10,8... | collective-permute-start | bytes 688136 | tf_op jit(solution)/shard_map/ppermute | solution.py:401
  29.5 6.8 %collective-permute-start.12 = (bf16[80,1536]{1,0:T(8,128)(2,1)S(1)}, bf16[80,1536]{1,0:T(8,128)(2,1)S(1)}, u32[]{:S(2)}, u32[]{:S(2)}) collective-permute-start(bf16[80,1536]{1,0:T(8,128)(2,1)S(1)} %get-tuple-element.51), channel_id=1, source_target_pairs={{0,16},{1,17},{2,18},{3,19},{4,20},{5,21},{6,22},{7,23},{8,24},{9,... | collective-permute-start | bytes 737288 | tf_op jit(solution)/shard_map/ppermute | solution.py:401
  32.0 6.0 %collective-permute-start.10 = (bf16[64,1792]{1,0:T(8,128)(2,1)S(1)}, bf16[64,1792]{1,0:T(8,128)(2,1)S(1)}, u32[]{:S(2)}, u32[]{:S(2)}) collective-permute-start(bf16[64,1792]{1,0:T(8,128)(2,1)S(1)} %collective-permute-done.6.refs_5_.refs_0_), channel_id=1, source_target_pairs={{0,2},{1,0},{2,4},{3,1},{4,6},{5,3},{6,7},{7,5},{8,10},{9,8},{10,1... | collective-permute-start | bytes 688136 | tf_op jit(solution)/shard_map/ppermute | solution.py:401
  33.3 9.0 %collective-permute-start.11 = (bf16[160,1792]{1,0:T(8,128)(2,1)S(1)}, bf16[160,1792]{1,0:T(8,128)(2,1)S(1)}, u32[]{:S(2)}, u32[]{:S(2)}) collective-permute-start(bf16[160,1792]{1,0:T(8,128)(2,1)S(1)} %slice_dynamic-update-slice_fusion), channel_id=1, source_target_pairs={{0,8},{1,9},{2,10},{3,11},{4,12},{5,13},{6,14},{7,15},{8,0},{9,1},... | collective-permute-start | bytes 1720328 | tf_op jit(solution)/shard_map/ppermute | solution.py:401
  38.1 4.3 %collective-permute-start.13 = (bf16[96,1792]{1,0:T(8,128)(2,1)S(1)}, bf16[96,1792]{1,0:T(8,128)(2,1)S(1)}, u32[]{:S(2)}, u32[]{:S(2)}) collective-permute-start(bf16[96,1792]{1,0:T(8,128)(2,1)S(1)} %pad_maximum_fusion), channel_id=1, source_target_pairs={{0,8},{1,9},{2,10},{3,11},{4,12},{5,13},{6,14},{7,15},{8,0},{9,1},... | collective-permute-start | bytes 1032200 | tf_op jit(solution)/shard_map/ppermute | solution.py:401
  40.2 7.5 %collective-permute-start.14 = (bf16[48,1536]{1,0:T(8,128)(2,1)S(1)}, bf16[48,1536]{1,0:T(8,128)(2,1)S(1)}, u32[]{:S(2)}, u32[]{:S(2)}) collective-permute-start(bf16[48,1536]{1,0:T(8,128)(2,1)S(1)} %get-tuple-element.55), channel_id=1, source_target_pairs={{0,16},{1,17},{2,18},{3,19},{4,20},{5,21},{6,22},{7,23},{8,24},{9,... | collective-permute-start | bytes 442376 | tf_op jit(solution)/shard_map/ppermute | solution.py:401

commit v4 on v3

--- a/solution.py
+++ b/solution.py
@@ -159,17 +159,20 @@
     )(gate_pre, up_pre)
 
 
-def weight_rows(down_weight, scales, parts, flips):
+def weight_rows(down_weight, scales, parts, first, count):
     width, units = down_weight.shape
     part = width // parts
-    chunk = 2 * TILE
-    count = part // chunk
-
-    def body(scale_ref, weight_ref, out_ref, sems):
-        me = lax.axis_index("dp") ^ flips
-        copies = []
-        for i in range(count):
-            start = pl.multiple_of(me * part + i * chunk, TILE)
+    chunk = TILE
+
+    def body(scale_ref, weight_ref, out_ref, local_ref, scale_sem, sems):
+        me = lax.axis_index("dp")
+        get_scales = pltpu.make_async_copy(scale_ref, local_ref, scale_sem)
+        get_scales.start()
+        copies, blocks = [], []
+        for i in range(count // chunk):
+            row = first + i * chunk
+            start = pl.multiple_of((me ^ (row // part)) * part + row % part, TILE)
+            blocks.append((me ^ (row // part)) * (part // TILE) + row % part // TILE)
             copies.append(
                 pltpu.make_async_copy(
                     weight_ref.at[pl.ds(start, chunk)],
@@ -178,24 +181,27 @@
                 )
             )
             copies[-1].start()
-        row0 = me * (part // TILE)
-        for i in range(count):
+        get_scales.wait()
+        for i in range(count // chunk):
             copies[i].wait()
-            for a in range(i * chunk // TILE, (i + 1) * chunk // TILE):
-                for b in range(units // TILE):
-                    at = (slice(a * TILE, (a + 1) * TILE), slice(b * TILE, (b + 1) * TILE))
-                    scale = jnp.full((TILE, TILE), scale_ref[row0 + a, b], F32).astype(BF16)
-                    out_ref[at] = out_ref[at] * scale
+            for b in range(units // TILE):
+                at = (slice(i * chunk, (i + 1) * chunk), slice(b * TILE, (b + 1) * TILE))
+                scale = jnp.full((TILE, TILE), local_ref[blocks[i], b], F32).astype(BF16)
+                out_ref[at] = out_ref[at] * scale
 
     return pl.pallas_call(
         body,
         name="weight_rows",
-        out_shape=like(part, units),
-        in_specs=[SMEM, HBM],
+        out_shape=like(count, units),
+        in_specs=[HBM, HBM],
         out_specs=VMEM,
-        scratch_shapes=[pltpu.SemaphoreType.DMA((count,))],
+        scratch_shapes=[
+            pltpu.SMEM(scales.shape, F32),
+            pltpu.SemaphoreType.DMA,
+            pltpu.SemaphoreType.DMA((count // chunk,)),
+        ],
         compiler_params=pltpu.CompilerParams(vmem_limit_bytes=44 * MIB),
-        cost_estimate=pl.CostEstimate(flops=part * units, bytes_accessed=4 * part * units, transcendentals=0),
+        cost_estimate=pl.CostEstimate(flops=count * units, bytes_accessed=4 * count * units, transcendentals=0),
     )(scales, down_weight)
 
 
@@ -214,12 +220,14 @@
 def partial_hidden(rows, pieces, weights):
     sizes = [len(p) for p in pieces]
     flat = [a for p in pieces for a in p]
-    part, units = weights[0].shape
+    part = flat[0].shape[1]
+    units = weights[0].shape[1]
     each = len(pieces) * rows
     step = 512 if units % 512 == 0 else 256
 
     def body(*refs):
-        first_ref, second_ref, keep_ref, send_ref, quant_ref = refs[len(flat) :]
+        weight_refs = refs[len(flat) : len(flat) + len(weights)]
+        keep_ref, send_ref, quant_ref = refs[len(flat) + len(weights) :]
         for k, piece in enumerate(grouped(refs, sizes)):
             for h in range(2):
                 ref, low = half_of(piece, h)
@@ -232,8 +240,12 @@
                         quant_ref[base : base + rows, into] = deq[s * rows : (s + 1) * rows]
         for i in range(units // step):
             cols = slice(i * step, (i + 1) * step)
-            result = jnp.dot(quant_ref[:, :part], first_ref[:, cols], preferred_element_type=F32)
-            result += jnp.dot(quant_ref[:, part:], second_ref[:, cols], preferred_element_type=F32)
+            result, at = 0.0, 0
+            for ref in weight_refs:
+                result += jnp.dot(
+                    quant_ref[:, at : at + ref.shape[0]], ref[:, cols], preferred_element_type=F32
+                )
+                at += ref.shape[0]
             keep_ref[:, cols] = result[:each].astype(keep_ref.dtype)
             send_ref[:, cols] = result[each:].astype(BF16)
 
@@ -241,7 +253,7 @@
         body,
         name="partial_hidden",
         out_shape=[like(each, units, dtype=F32), like(each, units)],
-        in_specs=[VMEM] * (len(flat) + 2),
+        in_specs=[VMEM] * (len(flat) + len(weights)),
         out_specs=[VMEM] * 2,
         scratch_shapes=[pltpu.VMEM((2 * each, 2 * part), BF16)],
         compiler_params=pltpu.CompilerParams(vmem_limit_bytes=16 * MIB),
@@ -419,34 +431,42 @@
     arrived = flip(send, 2)
     scales = after(block_scales, own).astype(F32)
     hidden_own, gate_factor, up_factor = hidden_quant(after(gate_here, scales), up_here)
-    arrived = after(arrived, hidden_own)
+    part = own.shape[1]
+    tiles = 2 * part // 256
+    cuts = [0, 256 * (tiles * 3 // 14), 256 * (tiles * 10 // 14), 2 * part]
+
+    def weight_cut(i, *others):
+        return weight_rows(down_weight, after(scales, *others), 4, cuts[i], cuts[i + 1] - cuts[i])
+
+    weight0 = weight_cut(0, hidden_own)
+    arrived = after(arrived, weight0)
     block = jnp.concatenate([own, arrived[:rows], other, arrived[rows:]], axis=0)
-    weight_own = weight_rows(down_weight, after(scales, block), 4, 0)
+    weight1 = weight_cut(1, block)
     hidden_chip = flip(hidden_own, 2)
-    hidden_core = flip(hidden_own, 1)
 
     got = {0: block}
     weights = None
     for k in range(1, half):
         low, high = got[1 - k], got[k - 1]
         if k == 2:
-            low, high = after(low, weight_own), after(high, weight_own)
-            weight_other = weight_rows(down_weight, after(scales, hidden_chip), 4, 1)
-            weights = weight_own, weight_other
+            low, high = after(low, weight1), after(high, weight1)
+            weight2 = weight_cut(2, hidden_chip)
+            weights = weight0, weight1, weight2
         if k == 3:
-            low, high = after(low, weights[1]), after(high, weights[1])
+            low, high = after(low, weight2), after(high, weight2)
         got[-k], got[k] = send_up(low), send_down(high)
-    first = n_tp - 3
-    hidden_far = flip(hidden_chip, 1)
+    first = n_tp - 4
     part1 = partial_hidden(
         rows,
         [[got[o]] for o in offsets[:first]],
-        (after(weights[0], hidden_far, hidden_core), weights[1]),
+        weights,
     )
     last = [send_up(after(got[1 - half], part1[0]))]
     pieces = [[got[o]] for o in offsets[:-1]] + [last]
 
     sum1 = flip(part1[1], 2)
+    hidden_core = flip(after(hidden_own, sum1), 1)
+    hidden_far = flip(after(hidden_chip, sum1), 1)
     other1 = flip(jnp.concatenate([got[o][2 * rows :] for o in offsets[:first]], axis=0), 1)
     late = [after(a, sum1) for a in last]
     other2 = flip(
@@ -467,7 +487,7 @@
         gate_factor,
         up_factor,
         [[part1[0], sum1], [part2[0], sum2]],
-        [first * rows, 3 * rows],
+        [first * rows, (n_tp - first) * rows],
         token,
     )
     return gate_grad, up_grad, down_grad
@@ -486,6 +506,7 @@
             and rows % 16 == 0
             and rows * n_tp == 128
             and part % 256 == 0
+            and part >= 1024
             and gate_pre.shape[1] % 256 == 0
         )
         if fits:

time: 48.9 us -> 46.1 us (0.943)
  waiting for transfers between devices: 11.6 us -> 8.91 us
  Pallas kernels: 20.3 us -> 18.7 us
  starting transfers between devices: 15.1 us -> 16.5 us
    ppermute x15, waiting for transfers between devices: 11.6 us -> 8.91 us  [permute(): return lax.ppermute(value, BOTH, pairs)]
    ppermute x15, starting transfers between devices: 15.1 us -> 16.5 us  [permute(): return lax.ppermute(value, BOTH, pairs)]
    pallas_call x2 -> x3, Pallas kernels: 7.54 us -> 6.44 us  [weight_rows(): pl.pallas_call(body, name='weight_rows', out_shape=like(count, units), in...]
  transfers between devices with their start and end apart: 15 -> 15, of which waited for: 6 -> 6; matrix products, arithmetic and copies ran while one was open for 2% -> 2% of each run, Pallas kernels for 37% -> 35%
where the time goes in v4:
time: 46.1 us; the launch traced here: 45.9 us
  Pallas kernels  18.7 us (41%)
  starting transfers between devices  16.5 us (36%)
  waiting for transfers between devices  8.91 us (19%)
  local copies, waits for them, and re-layouts  0.86 us (2%)
  between operations  0.81 us (2%)
    ppermute x15, starting transfers between devices, permute(): return lax.ppermute(value, BOTH, pairs)  16.5 us
    ppermute x15, waiting for transfers between devices, permute(): return lax.ppermute(value, BOTH, pairs)  8.91 us
    pallas_call x3, Pallas kernels, weight_rows(): pl.pallas_call(body, name='weight_rows', out_shape=like(count, units), in...  6.44 us
    pallas_call x1, Pallas kernels, down_product(): pl.pallas_call(body, name='down_product', out_shape=[like(part, units), l...  5.33 us
    pallas_call x2, Pallas kernels, partial_hidden(): pl.pallas_call(body, name='partial_hidden', out_shape=[like(each, units,...  3.96 us
    pallas_call x1, Pallas kernels, split_columns(): pl.pallas_call(body, name='split_columns', out_shape=[pltpu.VMEM((rows, p...  1.31 us
    pallas_call x1, Pallas kernels, last_step(): pl.pallas_call(body, name='last_step', out_shape=[like(tokens, units)] *...  1.11 us
  transfers between devices with their start and end apart: 15, of which 6 were waited for; matrix products, arithmetic and copies ran while one was open for 2% of the time, Pallas kernels for 35%

profile of v4, /device:TPU:0, one launch (start us, length us, event | category | flops | bytes accessed | tf_op | source)
XLA Modules:
  0.0 45.9 jit_solution(17679695597206162316)
XLA Ops:
  0.6 1.3 %split_columns.1 = (bf16[16,1792]{1,0:T(8,128)(2,1)S(1)}, bf16[16,1792]{1,0:T(8,128)(2,1)S(1)}, bf16[32,1792]{1,0:T(8,128)(2,1)S(1)}, bf16[128,1536]{1,0:T(8,128)(2,1)S(1)}, bf16[128,1536]{1,0:T(8,128)(2,1)S(1)}) custom-call(bf16[16,7168]{1,0:T(8,128)(2,1)} %grad_ref.1, bf16[128,1536]{1,0:T(8,128)(2,1)} %gate_ref.1, bf16[128,1536]{1,0:T(8,128)(2,1)} %up_ref.1), custom_call_target="tpu_custom_call" | custom-call | tf_op jit(solution)/shard_map/split_columns/pallas_call | solution.py:124
  2.0 3.0 %collective-permute-start = (bf16[32,1792]{1,0:T(8,128)(2,1)S(1)}, bf16[32,1792]{1,0:T(8,128)(2,1)S(1)}, u32[]{:S(2)}, u32[]{:S(2)}) collective-permute-start(bf16[32,1792]{1,0:T(8,128)(2,1)S(1)} %get-tuple-element.40), channel_id=1, source_target_pairs={{0,16},{1,17},{2,18},{3,19},{4,20},{5,21},{6,22},{7,23},{8,24},{9,... | collective-permute-start | bytes 344072 | tf_op jit(solution)/shard_map/ppermute | solution.py:413
  5.0 0.8 %copy.8 = bf16[56,12]{1,0:T(8,128)(2,1)S(1)} copy(bf16[56,12]{0,1:T(8,128)(2,1)} %param.9) | data formatting | bytes 2688 | tf_op jit(solution)/shard_map/optimization_barrier | solution.py:398
  5.8 0.6 %hidden_quant.1 = (bf16[128,1536]{1,0:T(8,128)(2,1)S(1)}, f32[128,1536]{1,0:T(8,128)S(1)}, f32[128,1536]{1,0:T(8,128)S(1)}) custom-call(bf16[128,1536]{1,0:T(8,128)(2,1)S(1)} %get-tuple-element.36.gate_ref, bf16[128,1536]{1,0:T(8,128)(2,1)S(1)} %get-tuple-element.37.up_ref), custom_call_target="tpu_custom_call" | custom-call | flops 3932160 | bytes 2752512 | tf_op jit(solution)/shard_map/hidden_quant/pallas_call | solution.py:149
  6.3 1.7 %weight_rows.3.refs_4_ = bf16[768,1536]{1,0:T(8,128)(2,1)S(1)} custom-call(f32[56,12]{1,0:T(8,128)S(1)} %convert_element_type.3.scale_ref, bf16[7168,1536]{1,0:T(8,128)(2,1)} %weight_ref.5), custom_call_target="tpu_custom_call" | custom-call | flops 1179648 | bytes 4718592 | tf_op jit(solution)/shard_map/weight_rows/pallas_call | solution.py:192
  8.1 0.0 collective-permute-done
  8.1 1.9 %collective-permute-start.1 = (bf16[64,1792]{1,0:T(8,128)(2,1)S(1)}, bf16[64,1792]{1,0:T(8,128)(2,1)S(1)}, u32[]{:S(2)}, u32[]{:S(2)}) collective-permute-start(bf16[64,1792]{1,0:T(8,128)(2,1)S(1)} %pad_maximum_fusion.1.refs_0_), channel_id=1, source_target_pairs={{0,2},{1,0},{2,4},{3,1},{4,6},{5,3},{6,7},{7,5},{8,10},{9,8},{10,1... | collective-permute-start | bytes 688136 | tf_op jit(solution)/shard_map/ppermute | solution.py:413
  10.0 0.2 collective-permute-start.2
  10.2 1.7 %collective-permute-start.5 = (bf16[128,1536]{1,0:T(8,128)(2,1)S(1)}, bf16[128,1536]{1,0:T(8,128)(2,1)S(1)}, u32[]{:S(2)}, u32[]{:S(2)}) collective-permute-start(bf16[128,1536]{1,0:T(8,128)(2,1)S(1)} %get-tuple-element.55.refs_10_), channel_id=1, source_target_pairs={{0,16},{1,17},{2,18},{3,19},{4,20},{5,21},{6,22},{7,23},{8,24},{9,... | collective-permute-start | bytes 1179656 | tf_op jit(solution)/shard_map/ppermute | solution.py:413
  12.0 2.7 %weight_rows.4.refs_5_ = bf16[1792,1536]{1,0:T(8,128)(2,1)S(1)} custom-call(f32[56,12]{1,0:T(8,128)S(1)} %convert_element_type.3.scale_ref, bf16[7168,1536]{1,0:T(8,128)(2,1)} %weight_ref.5), custom_call_target="tpu_custom_call" | custom-call | flops 2752512 | bytes 11010048 | tf_op jit(solution)/shard_map/weight_rows/pallas_call | solution.py:192
  14.7 0.5 %collective-permute-done.1.refs_1_ = bf16[64,1792]{1,0:T(8,128)(2,1)S(1)} collective-permute-done((bf16[64,1792]{1,0:T(8,128)(2,1)S(1)}, bf16[64,1792]{1,0:T(8,128)(2,1)S(1)}, u32[]{:S(2)}, u32[]{:S(2)}) %collective-permute-start.1) | collective-permute-done | bytes 229408 | tf_op jit(solution)/shard_map/ppermute | solution.py:413
  15.2 1.6 %collective-permute-start.3 = (bf16[64,1792]{1,0:T(8,128)(2,1)S(1)}, bf16[64,1792]{1,0:T(8,128)(2,1)S(1)}, u32[]{:S(2)}, u32[]{:S(2)}) collective-permute-start(bf16[64,1792]{1,0:T(8,128)(2,1)S(1)} %collective-permute-done.1.refs_1_), channel_id=1, source_target_pairs={{0,2},{1,0},{2,4},{3,1},{4,6},{5,3},{6,7},{7,5},{8,10},{9,8},{10,1... | collective-permute-start | bytes 688136 | tf_op jit(solution)/shard_map/ppermute | solution.py:413
  16.8 0.5 collective-permute-start.4
  17.3 2.9 %collective-permute-done.5.refs_11_ = bf16[128,1536]{1,0:T(8,128)(2,1)S(1)} collective-permute-done((bf16[128,1536]{1,0:T(8,128)(2,1)S(1)}, bf16[128,1536]{1,0:T(8,128)(2,1)S(1)}, u32[]{:S(2)}, u32[]{:S(2)}) %collective-permute-start.5) | collective-permute-done | bytes 393248 | tf_op jit(solution)/shard_map/ppermute | solution.py:413
  20.2 2.0 %weight_rows.5.refs_6_ = bf16[1024,1536]{1,0:T(8,128)(2,1)S(1)} custom-call(f32[56,12]{1,0:T(8,128)S(1)} %convert_element_type.3.scale_ref, bf16[7168,1536]{1,0:T(8,128)(2,1)} %weight_ref.5), custom_call_target="tpu_custom_call" | custom-call | flops 1572864 | bytes 6291456 | tf_op jit(solution)/shard_map/weight_rows/pallas_call | solution.py:192
  22.2 1.6 %collective-permute-start.6 = (bf16[64,1792]{1,0:T(8,128)(2,1)S(1)}, bf16[64,1792]{1,0:T(8,128)(2,1)S(1)}, u32[]{:S(2)}, u32[]{:S(2)}) collective-permute-start(bf16[64,1792]{1,0:T(8,128)(2,1)S(1)} %collective-permute-done.3.refs_3_), channel_id=1, source_target_pairs={{0,2},{1,0},{2,4},{3,1},{4,6},{5,3},{6,7},{7,5},{8,10},{9,8},{10,1... | collective-permute-start | bytes 688136 | tf_op jit(solution)/shard_map/ppermute | solution.py:413
  23.8 2.0 %partial_hidden.2 = (f32[64,1536]{1,0:T(8,128)S(1)}, bf16[64,1536]{1,0:T(8,128)(2,1)S(1)}) custom-call(bf16[64,1792]{1,0:T(8,128)(2,1)S(1)} %pad_maximum_fusion.1.refs_0_, bf16[64,1792]{1,0:T(8,128)(2,1)S(1)} %collective-permute-done.1.refs_1_, bf16[64,1792]{1,0:T(8,128)(2,1)S(1)} %collective-permute-done.2.refs_2_, ...), custom_call_target="tpu_custom_call" | custom-call | flops 1409286144 | bytes 11010048 | tf_op jit(solution)/shard_map/partial_hidden/pallas_call | solution.py:252
  25.8 1.2 %collective-permute-start.10 = (bf16[64,1536]{1,0:T(8,128)(2,1)S(1)}, bf16[64,1536]{1,0:T(8,128)(2,1)S(1)}, u32[]{:S(2)}, u32[]{:S(2)}) collective-permute-start(bf16[64,1536]{1,0:T(8,128)(2,1)S(1)} %get-tuple-element.53), channel_id=1, source_target_pairs={{0,16},{1,17},{2,18},{3,19},{4,20},{5,21},{6,22},{7,23},{8,24},{9,... | collective-permute-start | bytes 589832 | tf_op jit(solution)/shard_map/ppermute | solution.py:413
  27.1 0.5 collective-permute-start.7
  27.5 1.2 %collective-permute-done.6.refs_5_.refs_1_ = bf16[64,1792]{1,0:T(8,128)(2,1)S(1)} collective-permute-done((bf16[64,1792]{1,0:T(8,128)(2,1)S(1)}, bf16[64,1792]{1,0:T(8,128)(2,1)S(1)}, u32[]{:S(2)}, u32[]{:S(2)}) %collective-permute-start.6) | collective-permute-done | bytes 229408 | tf_op jit(solution)/shard_map/ppermute | solution.py:413
  28.7 1.8 %collective-permute-start.8 = (bf16[64,1792]{1,0:T(8,128)(2,1)S(1)}, bf16[64,1792]{1,0:T(8,128)(2,1)S(1)}, u32[]{:S(2)}, u32[]{:S(2)}) collective-permute-start(bf16[64,1792]{1,0:T(8,128)(2,1)S(1)} %collective-permute-done.6.refs_5_.refs_1_), channel_id=1, source_target_pairs={{0,2},{1,0},{2,4},{3,1},{4,6},{5,3},{6,7},{7,5},{8,10},{9,8},{10,1... | collective-permute-start | bytes 688136 | tf_op jit(solution)/shard_map/ppermute | solution.py:413
  30.6 0.1 collective-permute-start.9
  30.7 2.4 %collective-permute-done.7.refs_6_.refs_2_ = bf16[64,1792]{1,0:T(8,128)(2,1)S(1)} collective-permute-done((bf16[64,1792]{1,0:T(8,128)(2,1)S(1)}, bf16[64,1792]{1,0:T(8,128)(2,1)S(1)}, u32[]{:S(2)}, u32[]{:S(2)}) %collective-permute-start.7) | collective-permute-done | bytes 229408 | tf_op jit(solution)/shard_map/ppermute | solution.py:413
  33.1 1.6 %collective-permute-done.8.refs_7_.refs_3_ = bf16[64,1792]{1,0:T(8,128)(2,1)S(1)} collective-permute-done((bf16[64,1792]{1,0:T(8,128)(2,1)S(1)}, bf16[64,1792]{1,0:T(8,128)(2,1)S(1)}, u32[]{:S(2)}, u32[]{:S(2)}) %collective-permute-start.8) | collective-permute-done | bytes 229408 | tf_op jit(solution)/shard_map/ppermute | solution.py:413
  34.8 0.1 collective-permute-start.11
  34.9 0.5 %collective-permute-start.13 = (bf16[128,1536]{1,0:T(8,128)(2,1)S(1)}, bf16[128,1536]{1,0:T(8,128)(2,1)S(1)}, u32[]{:S(2)}, u32[]{:S(2)}) collective-permute-start(bf16[128,1536]{1,0:T(8,128)(2,1)S(1)} %collective-permute-done.5.refs_11_), channel_id=1, source_target_pairs={{0,8},{1,9},{2,10},{3,11},{4,12},{5,13},{6,14},{7,15},{8,0},{9,1},... | collective-permute-start | bytes 1179656 | tf_op jit(solution)/shard_map/ppermute | solution.py:413
  35.4 0.1 collective-permute-start.12
  35.4 2.0 %partial_hidden.3 = (f32[64,1536]{1,0:T(8,128)S(1)}, bf16[64,1536]{1,0:T(8,128)(2,1)S(1)}) custom-call(bf16[64,1792]{1,0:T(8,128)(2,1)S(1)} %collective-permute-done.4.refs_4_.refs_0_, bf16[64,1792]{1,0:T(8,128)(2,1)S(1)} %collective-permute-done.6.refs_5_.refs_1_, bf16[64,1792]{1,0:T(8,128)(2,1)S(1)} %collective-permute-done.7.refs_6_.refs_2_, ...), custom_call_target="tpu_custom_call" | custom-call | flops 1409286144 | bytes 11010048 | tf_op jit(solution)/shard_map/partial_hidden/pallas_call | solution.py:252
  37.4 1.8 %collective-permute-start.14 = (bf16[64,1536]{1,0:T(8,128)(2,1)S(1)}, bf16[64,1536]{1,0:T(8,128)(2,1)S(1)}, u32[]{:S(2)}, u32[]{:S(2)}) collective-permute-start(bf16[64,1536]{1,0:T(8,128)(2,1)S(1)} %get-tuple-element.59), channel_id=1, source_target_pairs={{0,16},{1,17},{2,18},{3,19},{4,20},{5,21},{6,22},{7,23},{8,24},{9,... | collective-permute-start | bytes 589832 | tf_op jit(solution)/shard_map/ppermute | solution.py:413
  39.3 5.3 %down_product.1 = (bf16[1792,1536]{1,0:T(8,128)(2,1)}, f32[8,128]{1,0:T(8,128)S(1)}) custom-call(bf16[64,1792]{1,0:T(8,128)(2,1)S(1)} %pad_maximum_fusion.1.refs_0_, bf16[64,1792]{1,0:T(8,128)(2,1)S(1)} %collective-permute-done.1.refs_1_, bf16[64,1792]{1,0:T(8,128)(2,1)S(1)} %collective-permute-done.2.refs_2_, ...), custom_call_target="tpu_custom_call" | custom-call | flops 2818572288 | bytes 5505024 | tf_op jit(solution)/shard_map/down_product/pallas_call | solution.py:329
  44.6 0.1 collective-permute-done.14.refs_3_
  44.8 1.1 %last_step.1 = (bf16[128,1536]{1,0:T(8,128)(2,1)}, bf16[128,1536]{1,0:T(8,128)(2,1)}) custom-call(f32[128,1536]{1,0:T(8,128)S(1)} %get-tuple-element.38.gate_ref, f32[128,1536]{1,0:T(8,128)S(1)} %get-tuple-element.39.up_ref, f32[8,128]{1,0:T(8,128)S(1)} %get-tuple-element.57._, f32[64,1536]{1,0:T(8,128)S(1)} %get-tuple-element.51.refs_0_, ...), custom_call_target="tpu_custom_call" | custom-call | flops 1572864 | bytes 3145728 | tf_op jit(solution)/shard_map/last_step/pallas_call | solution.py:382
  (20 shorter events, 0.2 us)
Async XLA Ops:
  2.0 6.1 %collective-permute-start = (bf16[32,1792]{1,0:T(8,128)(2,1)S(1)}, bf16[32,1792]{1,0:T(8,128)(2,1)S(1)}, u32[]{:S(2)}, u32[]{:S(2)}) collective-permute-start(bf16[32,1792]{1,0:T(8,128)(2,1)S(1)} %get-tuple-element.40), channel_id=1, source_target_pairs={{0,16},{1,17},{2,18},{3,19},{4,20},{5,21},{6,22},{7,23},{8,24},{9,... | collective-permute-start | bytes 344072 | tf_op jit(solution)/shard_map/ppermute | solution.py:413
  8.1 7.1 %collective-permute-start.1 = (bf16[64,1792]{1,0:T(8,128)(2,1)S(1)}, bf16[64,1792]{1,0:T(8,128)(2,1)S(1)}, u32[]{:S(2)}, u32[]{:S(2)}) collective-permute-start(bf16[64,1792]{1,0:T(8,128)(2,1)S(1)} %pad_maximum_fusion.1.refs_0_), channel_id=1, source_target_pairs={{0,2},{1,0},{2,4},{3,1},{4,6},{5,3},{6,7},{7,5},{8,10},{9,8},{10,1... | collective-permute-start | bytes 688136 | tf_op jit(solution)/shard_map/ppermute | solution.py:413
  10.0 6.8 %collective-permute-start.2 = (bf16[64,1792]{1,0:T(8,128)(2,1)S(1)}, bf16[64,1792]{1,0:T(8,128)(2,1)S(1)}, u32[]{:S(2)}, u32[]{:S(2)}) collective-permute-start(bf16[64,1792]{1,0:T(8,128)(2,1)S(1)} %pad_maximum_fusion.1.refs_0_), channel_id=1, source_target_pairs={{0,1},{1,3},{2,0},{3,5},{4,2},{5,7},{6,4},{7,6},{8,9},{9,11},{10,8... | collective-permute-start | bytes 688136 | tf_op jit(solution)/shard_map/ppermute | solution.py:413
  10.2 10.0 %collective-permute-start.5 = (bf16[128,1536]{1,0:T(8,128)(2,1)S(1)}, bf16[128,1536]{1,0:T(8,128)(2,1)S(1)}, u32[]{:S(2)}, u32[]{:S(2)}) collective-permute-start(bf16[128,1536]{1,0:T(8,128)(2,1)S(1)} %get-tuple-element.55.refs_10_), channel_id=1, source_target_pairs={{0,16},{1,17},{2,18},{3,19},{4,20},{5,21},{6,22},{7,23},{8,24},{9,... | collective-permute-start | bytes 1179656 | tf_op jit(solution)/shard_map/ppermute | solution.py:413
  15.2 7.0 %collective-permute-start.3 = (bf16[64,1792]{1,0:T(8,128)(2,1)S(1)}, bf16[64,1792]{1,0:T(8,128)(2,1)S(1)}, u32[]{:S(2)}, u32[]{:S(2)}) collective-permute-start(bf16[64,1792]{1,0:T(8,128)(2,1)S(1)} %collective-permute-done.1.refs_1_), channel_id=1, source_target_pairs={{0,2},{1,0},{2,4},{3,1},{4,6},{5,3},{6,7},{7,5},{8,10},{9,8},{10,1... | collective-permute-start | bytes 688136 | tf_op jit(solution)/shard_map/ppermute | solution.py:413
  16.8 10.3 %collective-permute-start.4 = (bf16[64,1792]{1,0:T(8,128)(2,1)S(1)}, bf16[64,1792]{1,0:T(8,128)(2,1)S(1)}, u32[]{:S(2)}, u32[]{:S(2)}) collective-permute-start(bf16[64,1792]{1,0:T(8,128)(2,1)S(1)} %collective-permute-done.2.refs_2_), channel_id=1, source_target_pairs={{0,1},{1,3},{2,0},{3,5},{4,2},{5,7},{6,4},{7,6},{8,9},{9,11},{10,8... | collective-permute-start | bytes 688136 | tf_op jit(solution)/shard_map/ppermute | solution.py:413
  22.2 6.5 %collective-permute-start.6 = (bf16[64,1792]{1,0:T(8,128)(2,1)S(1)}, bf16[64,1792]{1,0:T(8,128)(2,1)S(1)}, u32[]{:S(2)}, u32[]{:S(2)}) collective-permute-start(bf16[64,1792]{1,0:T(8,128)(2,1)S(1)} %collective-permute-done.3.refs_3_), channel_id=1, source_target_pairs={{0,2},{1,0},{2,4},{3,1},{4,6},{5,3},{6,7},{7,5},{8,10},{9,8},{10,1... | collective-permute-start | bytes 688136 | tf_op jit(solution)/shard_map/ppermute | solution.py:413
  25.8 7.3 %collective-permute-start.10 = (bf16[64,1536]{1,0:T(8,128)(2,1)S(1)}, bf16[64,1536]{1,0:T(8,128)(2,1)S(1)}, u32[]{:S(2)}, u32[]{:S(2)}) collective-permute-start(bf16[64,1536]{1,0:T(8,128)(2,1)S(1)} %get-tuple-element.53), channel_id=1, source_target_pairs={{0,16},{1,17},{2,18},{3,19},{4,20},{5,21},{6,22},{7,23},{8,24},{9,... | collective-permute-start | bytes 589832 | tf_op jit(solution)/shard_map/ppermute | solution.py:413
  27.1 6.0 %collective-permute-start.7 = (bf16[64,1792]{1,0:T(8,128)(2,1)S(1)}, bf16[64,1792]{1,0:T(8,128)(2,1)S(1)}, u32[]{:S(2)}, u32[]{:S(2)}) collective-permute-start(bf16[64,1792]{1,0:T(8,128)(2,1)S(1)} %collective-permute-done.4.refs_4_.refs_0_), channel_id=1, source_target_pairs={{0,1},{1,3},{2,0},{3,5},{4,2},{5,7},{6,4},{7,6},{8,9},{9,11},{10,8... | collective-permute-start | bytes 688136 | tf_op jit(solution)/shard_map/ppermute | solution.py:413
  28.7 6.0 %collective-permute-start.8 = (bf16[64,1792]{1,0:T(8,128)(2,1)S(1)}, bf16[64,1792]{1,0:T(8,128)(2,1)S(1)}, u32[]{:S(2)}, u32[]{:S(2)}) collective-permute-start(bf16[64,1792]{1,0:T(8,128)(2,1)S(1)} %collective-permute-done.6.refs_5_.refs_1_), channel_id=1, source_target_pairs={{0,2},{1,0},{2,4},{3,1},{4,6},{5,3},{6,7},{7,5},{8,10},{9,8},{10,1... | collective-permute-start | bytes 688136 | tf_op jit(solution)/shard_map/ppermute | solution.py:413
  30.6 8.7 %collective-permute-start.9 = (bf16[128,1792]{1,0:T(8,128)(2,1)S(1)}, bf16[128,1792]{1,0:T(8,128)(2,1)S(1)}, u32[]{:S(2)}, u32[]{:S(2)}) collective-permute-start(bf16[128,1792]{1,0:T(8,128)(2,1)S(1)} %slice_dynamic-update-slice_fusion), channel_id=1, source_target_pairs={{0,8},{1,9},{2,10},{3,11},{4,12},{5,13},{6,14},{7,15},{8,0},{9,1},... | collective-permute-start | bytes 1376264 | tf_op jit(solution)/shard_map/ppermute | solution.py:413
  34.8 4.5 %collective-permute-start.11 = (bf16[128,1792]{1,0:T(8,128)(2,1)S(1)}, bf16[128,1792]{1,0:T(8,128)(2,1)S(1)}, u32[]{:S(2)}, u32[]{:S(2)}) collective-permute-start(bf16[128,1792]{1,0:T(8,128)(2,1)S(1)} %pad_maximum_fusion), channel_id=1, source_target_pairs={{0,8},{1,9},{2,10},{3,11},{4,12},{5,13},{6,14},{7,15},{8,0},{9,1},... | collective-permute-start | bytes 1376264 | tf_op jit(solution)/shard_map/ppermute | solution.py:413
  34.9 4.4 %collective-permute-start.13 = (bf16[128,1536]{1,0:T(8,128)(2,1)S(1)}, bf16[128,1536]{1,0:T(8,128)(2,1)S(1)}, u32[]{:S(2)}, u32[]{:S(2)}) collective-permute-start(bf16[128,1536]{1,0:T(8,128)(2,1)S(1)} %collective-permute-done.5.refs_11_), channel_id=1, source_target_pairs={{0,8},{1,9},{2,10},{3,11},{4,12},{5,13},{6,14},{7,15},{8,0},{9,1},... | collective-permute-start | bytes 1179656 | tf_op jit(solution)/shard_map/ppermute | solution.py:413
  35.4 3.9 %collective-permute-start.12 = (bf16[128,1536]{1,0:T(8,128)(2,1)S(1)}, bf16[128,1536]{1,0:T(8,128)(2,1)S(1)}, u32[]{:S(2)}, u32[]{:S(2)}) collective-permute-start(bf16[128,1536]{1,0:T(8,128)(2,1)S(1)} %get-tuple-element.55.refs_10_), channel_id=1, source_target_pairs={{0,8},{1,9},{2,10},{3,11},{4,12},{5,13},{6,14},{7,15},{8,0},{9,1},... | collective-permute-start | bytes 1179656 | tf_op jit(solution)/shard_map/ppermute | solution.py:413
  37.4 7.3 %collective-permute-start.14 = (bf16[64,1536]{1,0:T(8,128)(2,1)S(1)}, bf16[64,1536]{1,0:T(8,128)(2,1)S(1)}, u32[]{:S(2)}, u32[]{:S(2)}) collective-permute-start(bf16[64,1536]{1,0:T(8,128)(2,1)S(1)} %get-tuple-element.59), channel_id=1, source_target_pairs={{0,16},{1,17},{2,18},{3,19},{4,20},{5,21},{6,22},{7,23},{8,24},{9,... | collective-permute-start | bytes 589832 | tf_op jit(solution)/shard_map/ppermute | solution.py:413

commit v5 on v4

--- a/solution.py
+++ b/solution.py
@@ -268,8 +268,16 @@
     part = flat[0].shape[1]
     tokens, units = hiddens[0].shape
     rows = tokens // len(pieces)
-    step, slots, split = 256, 3, 4
-    steps = part // step
+    slots, split = 3, 4
+    step = 512 if part > 512 else 128
+    steps, at = [], 0
+    while at < part:
+        size = min(step, part - at)
+        cut = at + size == part and size > TILE
+        steps += [(at, size - TILE), (at + size - TILE, TILE)] if cut else [(at, size)]
+        at += size
+    widest = max(size for _, size in steps)
+    third = units // 3 if units % (3 * TILE) == 0 else units
 
     def body(*refs):
         own, other = refs[: len(pieces)], refs[len(pieces) : len(flat)]
@@ -288,22 +296,23 @@
                 hid_ref[low : low + rows, :] = ref[pl.ds(start, rows), :]
 
         def copies(i):
-            lines = step // split
+            at, size = steps[i]
+            lines = size // split
             return [
                 pltpu.make_async_copy(
                     buffer.at[i % slots, pl.ds(k * lines, lines)],
-                    out_ref.at[pl.ds(i * step + k * lines, lines)],
+                    out_ref.at[pl.ds(at + k * lines, lines)],
                     sems.at[i % slots, k],
                 )
                 for k in range(split)
             ]
 
-        for i in range(steps):
+        for i, (at, size) in enumerate(steps):
             if i >= slots:
                 for copy in copies(i - slots):
                     copy.wait()
-            for c in range(step // TILE):
-                cols = slice(i * step + c * TILE, i * step + (c + 1) * TILE)
+            for c in range(size // TILE):
+                cols = slice(at + c * TILE, at + (c + 1) * TILE)
                 for j in range(4):
                     vals = [ref[low : low + rows, cols].astype(F32) for ref, low in where[j]]
                     top = jnp.abs(vals[0])
@@ -317,12 +326,14 @@
                         quant_ref[base : base + rows, c * TILE : (c + 1) * TILE] = (
                             payload * scale
                         ).astype(BF16)
-            buffer[i % slots] = lax.dot_general(
-                quant_ref[...], hid_ref[...], (((0,), (0,)), ((), ())), preferred_element_type=F32
-            ).astype(BF16)
+            for low in range(0, units, third):
+                hidden = hid_ref[:, low : low + third]
+                buffer[i % slots, :size, low : low + third] = lax.dot_general(
+                    quant_ref[:, :size], hidden, (((0,), (0,)), ((), ())), preferred_element_type=F32
+                ).astype(BF16)
             for copy in copies(i):
                 copy.start()
-        for i in range(max(0, steps - slots), steps):
+        for i in range(max(0, len(steps) - slots), len(steps)):
             for copy in copies(i):
                 copy.wait()
 
@@ -334,8 +345,8 @@
         out_specs=[HBM, VMEM],
         scratch_shapes=[
             pltpu.VMEM((4 * tokens, units), BF16),
-            pltpu.VMEM((4 * tokens, step), BF16),
-            pltpu.VMEM((slots, step, units), BF16),
+            pltpu.VMEM((4 * tokens, widest), BF16),
+            pltpu.VMEM((slots, widest, units), BF16),
             pltpu.SemaphoreType.DMA((slots, split)),
         ],
         compiler_params=pltpu.CompilerParams(vmem_limit_bytes=24 * MIB),
@@ -424,7 +435,7 @@
     rows = out_grad.shape[0]
     offsets = [0]
     for k in range(1, half):
-        offsets += [-k, k]
+        offsets += [k, -k]
     offsets.append(half)
 
     own, other, send, gate_here, up_here = split_columns(out_grad, gate_pre, up_pre, 4)
@@ -443,37 +454,35 @@
     block = jnp.concatenate([own, arrived[:rows], other, arrived[rows:]], axis=0)
     weight1 = weight_cut(1, block)
     hidden_chip = flip(hidden_own, 2)
+    hidden_core = flip(hidden_own, 1)
 
     got = {0: block}
-    weights = None
     for k in range(1, half):
         low, high = got[1 - k], got[k - 1]
         if k == 2:
             low, high = after(low, weight1), after(high, weight1)
-            weight2 = weight_cut(2, hidden_chip)
+            weight2 = weight_cut(2, hidden_core)
             weights = weight0, weight1, weight2
+            part1 = partial_hidden(rows, [[got[o]] for o in offsets[:3]], weights)
         if k == 3:
-            low, high = after(low, weight2), after(high, weight2)
+            low, high = after(low, part1[0]), after(high, part1[0])
         got[-k], got[k] = send_up(low), send_down(high)
-    first = n_tp - 4
-    part1 = partial_hidden(
-        rows,
-        [[got[o]] for o in offsets[:first]],
-        weights,
-    )
-    last = [send_up(after(got[1 - half], part1[0]))]
+    first = n_tp - 3
+    part2 = partial_hidden(rows, [[got[o]] for o in offsets[3:first]], weights)
+    hidden_far = flip(after(hidden_chip, got[1 - half], got[half - 1]), 1)
+    last = [send_up(after(got[1 - half], part2[0]))]
     pieces = [[got[o]] for o in offsets[:-1]] + [last]
 
     sum1 = flip(part1[1], 2)
-    hidden_core = flip(after(hidden_own, sum1), 1)
-    hidden_far = flip(after(hidden_chip, sum1), 1)
+    sum2 = flip(part2[1], 2)
     other1 = flip(jnp.concatenate([got[o][2 * rows :] for o in offsets[:first]], axis=0), 1)
-    late = [after(a, sum1) for a in last]
+    late = [after(a, sum1, sum2) for a in last]
+    tail = after(late[0], hidden_far)
     other2 = flip(
-        jnp.concatenate([got[o][2 * rows :] for o in offsets[first:-1]] + [late[0][2 * rows :]], axis=0), 1
-    )
-    part2 = partial_hidden(rows, pieces[first:-1] + [late], weights)
-    sum2 = flip(part2[1], 2)
+        jnp.concatenate([got[o][2 * rows :] for o in offsets[first:-1]] + [tail[2 * rows :]], axis=0), 1
+    )
+    part3 = partial_hidden(rows, pieces[first:-1] + [late], weights)
+    sum3 = flip(part3[1], 2)
     down_grad, token = down_product(
         n_tp,
         offsets,
@@ -486,8 +495,8 @@
         offsets,
         gate_factor,
         up_factor,
-        [[part1[0], sum1], [part2[0], sum2]],
-        [first * rows, (n_tp - first) * rows],
+        [[part1[0], sum1], [part2[0], sum2], [part3[0], sum3]],
+        [3 * rows, (first - 3) * rows, 3 * rows],
         token,
     )
     return gate_grad, up_grad, down_grad

time: 46.1 us -> 44.9 us (0.974)
  waiting for transfers between devices: 8.91 us -> 5.93 us
  Pallas kernels: 18.7 us -> 20.3 us
    ppermute x15 -> x16, waiting for transfers between devices: 8.91 us -> 5.93 us  [permute(): return lax.ppermute(value, BOTH, pairs)]
    pallas_call x2 -> x3, Pallas kernels: 3.96 us -> 6.2 us  [partial_hidden(): pl.pallas_call(body, name='partial_hidden', out_shape=[like(each, units,...]
    pallas_call x1, Pallas kernels: 5.33 us -> 4.67 us  [down_product(): pl.pallas_call(body, name='down_product', out_shape=[like(part, units), l...]
    ppermute x15 -> x16, starting transfers between devices: 16.5 us -> 16.6 us  [permute(): return lax.ppermute(value, BOTH, pairs)]
  transfers between devices with their start and end apart: 15 -> 16, of which waited for: 6 -> 6; matrix products, arithmetic and copies ran while one was open for 2% -> 2% of each run, Pallas kernels for 35% -> 40%
where the time goes in v5:
time: 44.9 us; the launch traced here: 44.7 us
  Pallas kernels  20.3 us (45%)
  starting transfers between devices  16.6 us (37%)
  waiting for transfers between devices  5.93 us (13%)
  between operations  0.95 us (2%)
  local copies, waits for them, and re-layouts  0.87 us (2%)
    ppermute x16, starting transfers between devices, permute(): return lax.ppermute(value, BOTH, pairs)  16.6 us
    pallas_call x3, Pallas kernels, weight_rows(): pl.pallas_call(body, name='weight_rows', out_shape=like(count, units), in...  6.45 us
    pallas_call x3, Pallas kernels, partial_hidden(): pl.pallas_call(body, name='partial_hidden', out_shape=[like(each, units,...  6.2 us
    ppermute x16, waiting for transfers between devices, permute(): return lax.ppermute(value, BOTH, pairs)  5.93 us
    pallas_call x1, Pallas kernels, down_product(): pl.pallas_call(body, name='down_product', out_shape=[like(part, units), l...  4.67 us
    pallas_call x1, Pallas kernels, split_columns(): pl.pallas_call(body, name='split_columns', out_shape=[pltpu.VMEM((rows, p...  1.31 us
    pallas_call x1, Pallas kernels, last_step(): pl.pallas_call(body, name='last_step', out_shape=[like(tokens, units)] *...  1.11 us
  transfers between devices with their start and end apart: 16, of which 6 were waited for; matrix products, arithmetic and copies ran while one was open for 2% of the time, Pallas kernels for 40%

profile of v5, /device:TPU:0, one launch (start us, length us, event | category | flops | bytes accessed | tf_op | source)
XLA Modules:
  0.0 44.7 jit_solution(4968312625649007211)
XLA Ops:
  0.6 1.3 %split_columns.1 = (bf16[16,1792]{1,0:T(8,128)(2,1)S(1)}, bf16[16,1792]{1,0:T(8,128)(2,1)S(1)}, bf16[32,1792]{1,0:T(8,128)(2,1)S(1)}, bf16[128,1536]{1,0:T(8,128)(2,1)S(1)}, bf16[128,1536]{1,0:T(8,128)(2,1)S(1)}) custom-call(bf16[16,7168]{1,0:T(8,128)(2,1)} %grad_ref.1, bf16[128,1536]{1,0:T(8,128)(2,1)} %gate_ref.1, bf16[128,1536]{1,0:T(8,128)(2,1)} %up_ref.1), custom_call_target="tpu_custom_call" | custom-call | tf_op jit(solution)/shard_map/split_columns/pallas_call | solution.py:124
  2.0 3.0 %collective-permute-start = (bf16[32,1792]{1,0:T(8,128)(2,1)S(1)}, bf16[32,1792]{1,0:T(8,128)(2,1)S(1)}, u32[]{:S(2)}, u32[]{:S(2)}) collective-permute-start(bf16[32,1792]{1,0:T(8,128)(2,1)S(1)} %get-tuple-element.42), channel_id=1, source_target_pairs={{0,16},{1,17},{2,18},{3,19},{4,20},{5,21},{6,22},{7,23},{8,24},{9,... | collective-permute-start | bytes 344072 | tf_op jit(solution)/shard_map/ppermute | solution.py:424
  5.0 0.8 %copy.8 = bf16[56,12]{1,0:T(8,128)(2,1)S(1)} copy(bf16[56,12]{0,1:T(8,128)(2,1)} %param.9) | data formatting | bytes 2688 | tf_op jit(solution)/shard_map/optimization_barrier | solution.py:409
  5.8 0.6 %hidden_quant.1 = (bf16[128,1536]{1,0:T(8,128)(2,1)S(1)}, f32[128,1536]{1,0:T(8,128)S(1)}, f32[128,1536]{1,0:T(8,128)S(1)}) custom-call(bf16[128,1536]{1,0:T(8,128)(2,1)S(1)} %get-tuple-element.38.gate_ref, bf16[128,1536]{1,0:T(8,128)(2,1)S(1)} %get-tuple-element.39.up_ref), custom_call_target="tpu_custom_call" | custom-call | flops 3932160 | bytes 2752512 | tf_op jit(solution)/shard_map/hidden_quant/pallas_call | solution.py:149
  6.3 1.7 %weight_rows.3.refs_3_.refs_2_ = bf16[768,1536]{1,0:T(8,128)(2,1)S(1)} custom-call(f32[56,12]{1,0:T(8,128)S(1)} %convert_element_type.3.scale_ref, bf16[7168,1536]{1,0:T(8,128)(2,1)} %weight_ref.5), custom_call_target="tpu_custom_call" | custom-call | flops 1179648 | bytes 4718592 | tf_op jit(solution)/shard_map/weight_rows/pallas_call | solution.py:192
  8.1 0.0 collective-permute-done
  8.1 1.9 %collective-permute-start.2 = (bf16[64,1792]{1,0:T(8,128)(2,1)S(1)}, bf16[64,1792]{1,0:T(8,128)(2,1)S(1)}, u32[]{:S(2)}, u32[]{:S(2)}) collective-permute-start(bf16[64,1792]{1,0:T(8,128)(2,1)S(1)} %pad_maximum_fusion.1.refs_0_), channel_id=1, source_target_pairs={{0,2},{1,0},{2,4},{3,1},{4,6},{5,3},{6,7},{7,5},{8,10},{9,8},{10,1... | collective-permute-start | bytes 688136 | tf_op jit(solution)/shard_map/ppermute | solution.py:424
  10.0 0.2 collective-permute-start.1
  10.2 1.7 %collective-permute-start.12 = (bf16[128,1536]{1,0:T(8,128)(2,1)S(1)}, bf16[128,1536]{1,0:T(8,128)(2,1)S(1)}, u32[]{:S(2)}, u32[]{:S(2)}) collective-permute-start(bf16[128,1536]{1,0:T(8,128)(2,1)S(1)} %get-tuple-element.43.refs_10_), channel_id=1, source_target_pairs={{0,16},{1,17},{2,18},{3,19},{4,20},{5,21},{6,22},{7,23},{8,24},{9,... | collective-permute-start | bytes 1179656 | tf_op jit(solution)/shard_map/ppermute | solution.py:424
  12.0 2.7 %weight_rows.4.refs_4_.refs_3_ = bf16[1792,1536]{1,0:T(8,128)(2,1)S(1)} custom-call(f32[56,12]{1,0:T(8,128)S(1)} %convert_element_type.3.scale_ref, bf16[7168,1536]{1,0:T(8,128)(2,1)} %weight_ref.5), custom_call_target="tpu_custom_call" | custom-call | flops 2752512 | bytes 11010048 | tf_op jit(solution)/shard_map/weight_rows/pallas_call | solution.py:192
  14.7 0.5 %collective-permute-done.2.refs_2_ = bf16[64,1792]{1,0:T(8,128)(2,1)S(1)} collective-permute-done((bf16[64,1792]{1,0:T(8,128)(2,1)S(1)}, bf16[64,1792]{1,0:T(8,128)(2,1)S(1)}, u32[]{:S(2)}, u32[]{:S(2)}) %collective-permute-start.2) | collective-permute-done | bytes 229408 | tf_op jit(solution)/shard_map/ppermute | solution.py:424
  15.2 1.6 %collective-permute-start.4 = (bf16[64,1792]{1,0:T(8,128)(2,1)S(1)}, bf16[64,1792]{1,0:T(8,128)(2,1)S(1)}, u32[]{:S(2)}, u32[]{:S(2)}) collective-permute-start(bf16[64,1792]{1,0:T(8,128)(2,1)S(1)} %collective-permute-done.2.refs_2_), channel_id=1, source_target_pairs={{0,2},{1,0},{2,4},{3,1},{4,6},{5,3},{6,7},{7,5},{8,10},{9,8},{10,1... | collective-permute-start | bytes 688136 | tf_op jit(solution)/shard_map/ppermute | solution.py:424
  16.8 0.5 %collective-permute-start.3 = (bf16[64,1792]{1,0:T(8,128)(2,1)S(1)}, bf16[64,1792]{1,0:T(8,128)(2,1)S(1)}, u32[]{:S(2)}, u32[]{:S(2)}) collective-permute-start(bf16[64,1792]{1,0:T(8,128)(2,1)S(1)} %collective-permute-done.1.refs_1_), channel_id=1, source_target_pairs={{0,1},{1,3},{2,0},{3,5},{4,2},{5,7},{6,4},{7,6},{8,9},{9,11},{10,8... | collective-permute-start | bytes 688136 | tf_op jit(solution)/shard_map/ppermute | solution.py:424
  17.3 2.0 %weight_rows.5.refs_5_.refs_4_ = bf16[1024,1536]{1,0:T(8,128)(2,1)S(1)} custom-call(f32[56,12]{1,0:T(8,128)S(1)} %convert_element_type.3.scale_ref, bf16[7168,1536]{1,0:T(8,128)(2,1)} %weight_ref.5), custom_call_target="tpu_custom_call" | custom-call | flops 1572864 | bytes 6291456 | tf_op jit(solution)/shard_map/weight_rows/pallas_call | solution.py:192
  19.3 2.0 %partial_hidden.3 = (f32[48,1536]{1,0:T(8,128)S(1)}, bf16[48,1536]{1,0:T(8,128)(2,1)S(1)}) custom-call(bf16[64,1792]{1,0:T(8,128)(2,1)S(1)} %pad_maximum_fusion.1.refs_0_, bf16[64,1792]{1,0:T(8,128)(2,1)S(1)} %collective-permute-done.1.refs_1_, bf16[64,1792]{1,0:T(8,128)(2,1)S(1)} %collective-permute-done.2.refs_2_, ...), custom_call_target="tpu_custom_call" | custom-call | flops 1056964608 | bytes 11010048 | tf_op jit(solution)/shard_map/partial_hidden/pallas_call | solution.py:252
  21.3 1.2 %collective-permute-start.10 = (bf16[48,1536]{1,0:T(8,128)(2,1)S(1)}, bf16[48,1536]{1,0:T(8,128)(2,1)S(1)}, u32[]{:S(2)}, u32[]{:S(2)}) collective-permute-start(bf16[48,1536]{1,0:T(8,128)(2,1)S(1)} %get-tuple-element.56), channel_id=1, source_target_pairs={{0,16},{1,17},{2,18},{3,19},{4,20},{5,21},{6,22},{7,23},{8,24},{9,... | collective-permute-start | bytes 442376 | tf_op jit(solution)/shard_map/ppermute | solution.py:424
  22.6 1.6 %collective-permute-start.7 = (bf16[64,1792]{1,0:T(8,128)(2,1)S(1)}, bf16[64,1792]{1,0:T(8,128)(2,1)S(1)}, u32[]{:S(2)}, u32[]{:S(2)}) collective-permute-start(bf16[64,1792]{1,0:T(8,128)(2,1)S(1)} %collective-permute-done.4.refs_1_.refs_4_), channel_id=1, source_target_pairs={{0,2},{1,0},{2,4},{3,1},{4,6},{5,3},{6,7},{7,5},{8,10},{9,8},{10,1... | collective-permute-start | bytes 688136 | tf_op jit(solution)/shard_map/ppermute | solution.py:424
  24.2 2.1 %partial_hidden.4 = (f32[32,1536]{1,0:T(8,128)S(1)}, bf16[32,1536]{1,0:T(8,128)(2,1)S(1)}) custom-call(bf16[64,1792]{1,0:T(8,128)(2,1)S(1)} %collective-permute-done.3.refs_0_.refs_3_, bf16[64,1792]{1,0:T(8,128)(2,1)S(1)} %collective-permute-done.4.refs_1_.refs_4_, bf16[768,1536]{1,0:T(8,128)(2,1)S(1)} %weight_rows.3.refs_3_.refs_2_, ...), custom_call_target="tpu_custom_call" | custom-call | flops 704643072 | bytes 11010048 | tf_op jit(solution)/shard_map/partial_hidden/pallas_call | solution.py:252
  26.3 0.9 %collective-permute-start.11 = (bf16[32,1536]{1,0:T(8,128)(2,1)S(1)}, bf16[32,1536]{1,0:T(8,128)(2,1)S(1)}, u32[]{:S(2)}, u32[]{:S(2)}) collective-permute-start(bf16[32,1536]{1,0:T(8,128)(2,1)S(1)} %get-tuple-element.57), channel_id=1, source_target_pairs={{0,16},{1,17},{2,18},{3,19},{4,20},{5,21},{6,22},{7,23},{8,24},{9,... | collective-permute-start | bytes 294920 | tf_op jit(solution)/shard_map/ppermute | solution.py:424
  27.2 0.4 %collective-permute-start.6 = (bf16[64,1792]{1,0:T(8,128)(2,1)S(1)}, bf16[64,1792]{1,0:T(8,128)(2,1)S(1)}, u32[]{:S(2)}, u32[]{:S(2)}) collective-permute-start(bf16[64,1792]{1,0:T(8,128)(2,1)S(1)} %collective-permute-done.3.refs_0_.refs_3_), channel_id=1, source_target_pairs={{0,1},{1,3},{2,0},{3,5},{4,2},{5,7},{6,4},{7,6},{8,9},{9,11},{10,8... | collective-permute-start | bytes 688136 | tf_op jit(solution)/shard_map/ppermute | solution.py:424
  27.7 1.2 %collective-permute-done.7.refs_6_.refs_1_ = bf16[64,1792]{1,0:T(8,128)(2,1)S(1)} collective-permute-done((bf16[64,1792]{1,0:T(8,128)(2,1)S(1)}, bf16[64,1792]{1,0:T(8,128)(2,1)S(1)}, u32[]{:S(2)}, u32[]{:S(2)}) %collective-permute-start.7) | collective-permute-done | bytes 229408 | tf_op jit(solution)/shard_map/ppermute | solution.py:424
  28.9 1.6 %collective-permute-start.8 = (bf16[64,1792]{1,0:T(8,128)(2,1)S(1)}, bf16[64,1792]{1,0:T(8,128)(2,1)S(1)}, u32[]{:S(2)}, u32[]{:S(2)}) collective-permute-start(bf16[64,1792]{1,0:T(8,128)(2,1)S(1)} %collective-permute-done.7.refs_6_.refs_1_), channel_id=1, source_target_pairs={{0,2},{1,0},{2,4},{3,1},{4,6},{5,3},{6,7},{7,5},{8,10},{9,8},{10,1... | collective-permute-start | bytes 688136 | tf_op jit(solution)/shard_map/ppermute | solution.py:424
  30.5 2.8 %collective-permute-done.6.refs_5_.refs_0_ = bf16[64,1792]{1,0:T(8,128)(2,1)S(1)} collective-permute-done((bf16[64,1792]{1,0:T(8,128)(2,1)S(1)}, bf16[64,1792]{1,0:T(8,128)(2,1)S(1)}, u32[]{:S(2)}, u32[]{:S(2)}) %collective-permute-start.6) | collective-permute-done | bytes 229408 | tf_op jit(solution)/shard_map/ppermute | solution.py:424
  33.3 0.6 %collective-permute-start.9 = (bf16[160,1792]{1,0:T(8,128)(2,1)S(1)}, bf16[160,1792]{1,0:T(8,128)(2,1)S(1)}, u32[]{:S(2)}, u32[]{:S(2)}) collective-permute-start(bf16[160,1792]{1,0:T(8,128)(2,1)S(1)} %slice_dynamic-update-slice_fusion), channel_id=1, source_target_pairs={{0,8},{1,9},{2,10},{3,11},{4,12},{5,13},{6,14},{7,15},{8,0},{9,1},... | collective-permute-start | bytes 1720328 | tf_op jit(solution)/shard_map/ppermute | solution.py:424
  33.9 1.0 %collective-permute-done.8.refs_7_.refs_2_ = bf16[64,1792]{1,0:T(8,128)(2,1)S(1)} collective-permute-done((bf16[64,1792]{1,0:T(8,128)(2,1)S(1)}, bf16[64,1792]{1,0:T(8,128)(2,1)S(1)}, u32[]{:S(2)}, u32[]{:S(2)}) %collective-permute-start.8) | collective-permute-done | bytes 229408 | tf_op jit(solution)/shard_map/ppermute | solution.py:424
  34.9 0.1 collective-permute-done.13.refs_13_
  35.0 0.2 collective-permute-start.14
  35.2 2.0 %partial_hidden.5 = (f32[48,1536]{1,0:T(8,128)S(1)}, bf16[48,1536]{1,0:T(8,128)(2,1)S(1)}) custom-call(bf16[64,1792]{1,0:T(8,128)(2,1)S(1)} %collective-permute-done.6.refs_5_.refs_0_, bf16[64,1792]{1,0:T(8,128)(2,1)S(1)} %collective-permute-done.7.refs_6_.refs_1_, bf16[64,1792]{1,0:T(8,128)(2,1)S(1)} %collective-permute-done.8.refs_7_.refs_2_, ...), custom_call_target="tpu_custom_call" | custom-call | flops 1056964608 | bytes 11010048 | tf_op jit(solution)/shard_map/partial_hidden/pallas_call | solution.py:252
  37.3 1.2 %collective-permute-start.15 = (bf16[48,1536]{1,0:T(8,128)(2,1)S(1)}, bf16[48,1536]{1,0:T(8,128)(2,1)S(1)}, u32[]{:S(2)}, u32[]{:S(2)}) collective-permute-start(bf16[48,1536]{1,0:T(8,128)(2,1)S(1)} %get-tuple-element.63), channel_id=1, source_target_pairs={{0,16},{1,17},{2,18},{3,19},{4,20},{5,21},{6,22},{7,23},{8,24},{9,... | collective-permute-start | bytes 442376 | tf_op jit(solution)/shard_map/ppermute | solution.py:424
  38.5 4.7 %down_product.1 = (bf16[1792,1536]{1,0:T(8,128)(2,1)}, f32[8,128]{1,0:T(8,128)S(1)}) custom-call(bf16[64,1792]{1,0:T(8,128)(2,1)S(1)} %pad_maximum_fusion.1.refs_0_, bf16[64,1792]{1,0:T(8,128)(2,1)S(1)} %collective-permute-done.1.refs_1_, bf16[64,1792]{1,0:T(8,128)(2,1)S(1)} %collective-permute-done.2.refs_2_, ...), custom_call_target="tpu_custom_call" | custom-call | flops 2818572288 | bytes 5505024 | tf_op jit(solution)/shard_map/down_product/pallas_call | solution.py:340
  43.2 0.3 collective-permute-done.15.refs_5_
  43.4 1.1 %last_step.1 = (bf16[128,1536]{1,0:T(8,128)(2,1)}, bf16[128,1536]{1,0:T(8,128)(2,1)}) custom-call(f32[128,1536]{1,0:T(8,128)S(1)} %get-tuple-element.40.gate_ref, f32[128,1536]{1,0:T(8,128)S(1)} %get-tuple-element.41.up_ref, f32[8,128]{1,0:T(8,128)S(1)} %get-tuple-element.61._, f32[48,1536]{1,0:T(8,128)S(1)} %get-tuple-element.51.refs_0_, ...), custom_call_target="tpu_custom_call" | custom-call | flops 1572864 | bytes 3145728 | tf_op jit(solution)/shard_map/last_step/pallas_call | solution.py:393
  (23 shorter events, 0.2 us)
Async XLA Ops:
  2.0 6.1 %collective-permute-start = (bf16[32,1792]{1,0:T(8,128)(2,1)S(1)}, bf16[32,1792]{1,0:T(8,128)(2,1)S(1)}, u32[]{:S(2)}, u32[]{:S(2)}) collective-permute-start(bf16[32,1792]{1,0:T(8,128)(2,1)S(1)} %get-tuple-element.42), channel_id=1, source_target_pairs={{0,16},{1,17},{2,18},{3,19},{4,20},{5,21},{6,22},{7,23},{8,24},{9,... | collective-permute-start | bytes 344072 | tf_op jit(solution)/shard_map/ppermute | solution.py:424
  8.1 7.1 %collective-permute-start.2 = (bf16[64,1792]{1,0:T(8,128)(2,1)S(1)}, bf16[64,1792]{1,0:T(8,128)(2,1)S(1)}, u32[]{:S(2)}, u32[]{:S(2)}) collective-permute-start(bf16[64,1792]{1,0:T(8,128)(2,1)S(1)} %pad_maximum_fusion.1.refs_0_), channel_id=1, source_target_pairs={{0,2},{1,0},{2,4},{3,1},{4,6},{5,3},{6,7},{7,5},{8,10},{9,8},{10,1... | collective-permute-start | bytes 688136 | tf_op jit(solution)/shard_map/ppermute | solution.py:424
  10.0 6.8 %collective-permute-start.1 = (bf16[64,1792]{1,0:T(8,128)(2,1)S(1)}, bf16[64,1792]{1,0:T(8,128)(2,1)S(1)}, u32[]{:S(2)}, u32[]{:S(2)}) collective-permute-start(bf16[64,1792]{1,0:T(8,128)(2,1)S(1)} %pad_maximum_fusion.1.refs_0_), channel_id=1, source_target_pairs={{0,1},{1,3},{2,0},{3,5},{4,2},{5,7},{6,4},{7,6},{8,9},{9,11},{10,8... | collective-permute-start | bytes 688136 | tf_op jit(solution)/shard_map/ppermute | solution.py:424
  10.2 7.1 %collective-permute-start.5 = (bf16[128,1536]{1,0:T(8,128)(2,1)S(1)}, bf16[128,1536]{1,0:T(8,128)(2,1)S(1)}, u32[]{:S(2)}, u32[]{:S(2)}) collective-permute-start(bf16[128,1536]{1,0:T(8,128)(2,1)S(1)} %get-tuple-element.43.refs_10_), channel_id=1, source_target_pairs={{0,8},{1,9},{2,10},{3,11},{4,12},{5,13},{6,14},{7,15},{8,0},{9,1},... | collective-permute-start | bytes 1179656 | tf_op jit(solution)/shard_map/ppermute | solution.py:424
  10.2 20.2 %collective-permute-start.12 = (bf16[128,1536]{1,0:T(8,128)(2,1)S(1)}, bf16[128,1536]{1,0:T(8,128)(2,1)S(1)}, u32[]{:S(2)}, u32[]{:S(2)}) collective-permute-start(bf16[128,1536]{1,0:T(8,128)(2,1)S(1)} %get-tuple-element.43.refs_10_), channel_id=1, source_target_pairs={{0,16},{1,17},{2,18},{3,19},{4,20},{5,21},{6,22},{7,23},{8,24},{9,... | collective-permute-start | bytes 1179656 | tf_op jit(solution)/shard_map/ppermute | solution.py:424
  15.2 7.3 %collective-permute-start.4 = (bf16[64,1792]{1,0:T(8,128)(2,1)S(1)}, bf16[64,1792]{1,0:T(8,128)(2,1)S(1)}, u32[]{:S(2)}, u32[]{:S(2)}) collective-permute-start(bf16[64,1792]{1,0:T(8,128)(2,1)S(1)} %collective-permute-done.2.refs_2_), channel_id=1, source_target_pairs={{0,2},{1,0},{2,4},{3,1},{4,6},{5,3},{6,7},{7,5},{8,10},{9,8},{10,1... | collective-permute-start | bytes 688136 | tf_op jit(solution)/shard_map/ppermute | solution.py:424
  16.8 7.3 %collective-permute-start.3 = (bf16[64,1792]{1,0:T(8,128)(2,1)S(1)}, bf16[64,1792]{1,0:T(8,128)(2,1)S(1)}, u32[]{:S(2)}, u32[]{:S(2)}) collective-permute-start(bf16[64,1792]{1,0:T(8,128)(2,1)S(1)} %collective-permute-done.1.refs_1_), channel_id=1, source_target_pairs={{0,1},{1,3},{2,0},{3,5},{4,2},{5,7},{6,4},{7,6},{8,9},{9,11},{10,8... | collective-permute-start | bytes 688136 | tf_op jit(solution)/shard_map/ppermute | solution.py:424
  21.3 12.5 %collective-permute-start.10 = (bf16[48,1536]{1,0:T(8,128)(2,1)S(1)}, bf16[48,1536]{1,0:T(8,128)(2,1)S(1)}, u32[]{:S(2)}, u32[]{:S(2)}) collective-permute-start(bf16[48,1536]{1,0:T(8,128)(2,1)S(1)} %get-tuple-element.56), channel_id=1, source_target_pairs={{0,16},{1,17},{2,18},{3,19},{4,20},{5,21},{6,22},{7,23},{8,24},{9,... | collective-permute-start | bytes 442376 | tf_op jit(solution)/shard_map/ppermute | solution.py:424
  22.6 6.3 %collective-permute-start.7 = (bf16[64,1792]{1,0:T(8,128)(2,1)S(1)}, bf16[64,1792]{1,0:T(8,128)(2,1)S(1)}, u32[]{:S(2)}, u32[]{:S(2)}) collective-permute-start(bf16[64,1792]{1,0:T(8,128)(2,1)S(1)} %collective-permute-done.4.refs_1_.refs_4_), channel_id=1, source_target_pairs={{0,2},{1,0},{2,4},{3,1},{4,6},{5,3},{6,7},{7,5},{8,10},{9,8},{10,1... | collective-permute-start | bytes 688136 | tf_op jit(solution)/shard_map/ppermute | solution.py:424
  26.3 7.6 %collective-permute-start.11 = (bf16[32,1536]{1,0:T(8,128)(2,1)S(1)}, bf16[32,1536]{1,0:T(8,128)(2,1)S(1)}, u32[]{:S(2)}, u32[]{:S(2)}) collective-permute-start(bf16[32,1536]{1,0:T(8,128)(2,1)S(1)} %get-tuple-element.57), channel_id=1, source_target_pairs={{0,16},{1,17},{2,18},{3,19},{4,20},{5,21},{6,22},{7,23},{8,24},{9,... | collective-permute-start | bytes 294920 | tf_op jit(solution)/shard_map/ppermute | solution.py:424
  27.2 6.0 %collective-permute-start.6 = (bf16[64,1792]{1,0:T(8,128)(2,1)S(1)}, bf16[64,1792]{1,0:T(8,128)(2,1)S(1)}, u32[]{:S(2)}, u32[]{:S(2)}) collective-permute-start(bf16[64,1792]{1,0:T(8,128)(2,1)S(1)} %collective-permute-done.3.refs_0_.refs_3_), channel_id=1, source_target_pairs={{0,1},{1,3},{2,0},{3,5},{4,2},{5,7},{6,4},{7,6},{8,9},{9,11},{10,8... | collective-permute-start | bytes 688136 | tf_op jit(solution)/shard_map/ppermute | solution.py:424
  28.9 6.0 %collective-permute-start.8 = (bf16[64,1792]{1,0:T(8,128)(2,1)S(1)}, bf16[64,1792]{1,0:T(8,128)(2,1)S(1)}, u32[]{:S(2)}, u32[]{:S(2)}) collective-permute-start(bf16[64,1792]{1,0:T(8,128)(2,1)S(1)} %collective-permute-done.7.refs_6_.refs_1_), channel_id=1, source_target_pairs={{0,2},{1,0},{2,4},{3,1},{4,6},{5,3},{6,7},{7,5},{8,10},{9,8},{10,1... | collective-permute-start | bytes 688136 | tf_op jit(solution)/shard_map/ppermute | solution.py:424
  33.2 1.7 %collective-permute-start.13 = (bf16[128,1536]{1,0:T(8,128)(2,1)S(1)}, bf16[128,1536]{1,0:T(8,128)(2,1)S(1)}, u32[]{:S(2)}, u32[]{:S(2)}) collective-permute-start(bf16[128,1536]{1,0:T(8,128)(2,1)S(1)} %collective-permute-done.12.refs_11_), channel_id=1, source_target_pairs={{0,8},{1,9},{2,10},{3,11},{4,12},{5,13},{6,14},{7,15},{8,0},{9,1},... | collective-permute-start | bytes 1179656 | tf_op jit(solution)/shard_map/ppermute | solution.py:424
  33.3 5.2 %collective-permute-start.9 = (bf16[160,1792]{1,0:T(8,128)(2,1)S(1)}, bf16[160,1792]{1,0:T(8,128)(2,1)S(1)}, u32[]{:S(2)}, u32[]{:S(2)}) collective-permute-start(bf16[160,1792]{1,0:T(8,128)(2,1)S(1)} %slice_dynamic-update-slice_fusion), channel_id=1, source_target_pairs={{0,8},{1,9},{2,10},{3,11},{4,12},{5,13},{6,14},{7,15},{8,0},{9,1},... | collective-permute-start | bytes 1720328 | tf_op jit(solution)/shard_map/ppermute | solution.py:424
  35.0 3.5 %collective-permute-start.14 = (bf16[96,1792]{1,0:T(8,128)(2,1)S(1)}, bf16[96,1792]{1,0:T(8,128)(2,1)S(1)}, u32[]{:S(2)}, u32[]{:S(2)}) collective-permute-start(bf16[96,1792]{1,0:T(8,128)(2,1)S(1)} %pad_maximum_fusion), channel_id=1, source_target_pairs={{0,8},{1,9},{2,10},{3,11},{4,12},{5,13},{6,14},{7,15},{8,0},{9,1},... | collective-permute-start | bytes 1032200 | tf_op jit(solution)/shard_map/ppermute | solution.py:424
  37.3 6.2 %collective-permute-start.15 = (bf16[48,1536]{1,0:T(8,128)(2,1)S(1)}, bf16[48,1536]{1,0:T(8,128)(2,1)S(1)}, u32[]{:S(2)}, u32[]{:S(2)}) collective-permute-start(bf16[48,1536]{1,0:T(8,128)(2,1)S(1)} %get-tuple-element.63), channel_id=1, source_target_pairs={{0,16},{1,17},{2,18},{3,19},{4,20},{5,21},{6,22},{7,23},{8,24},{9,... | collective-permute-start | bytes 442376 | tf_op jit(solution)/shard_map/ppermute | solution.py:424

commit v6 on v5

--- a/solution.py
+++ b/solution.py
@@ -263,7 +263,14 @@
     )(*flat, *weights)
 
 
-def down_product(n_tp, offsets, pieces, others, hiddens):
+def hidden_rows(group, rows):
+    own, other = group
+    for low in range(0, own.shape[0], rows):
+        at = (slice(low, low + rows), slice(None))
+        yield own[at].astype(F32) + other[at].astype(F32)
+
+
+def down_product(n_tp, offsets, pieces, others, hiddens, gate_factor, up_factor, groups):
     flat = [p[0] for p in pieces] + list(others)
     part = flat[0].shape[1]
     tokens, units = hiddens[0].shape
@@ -277,6 +284,9 @@
         steps += [(at, size - TILE), (at + size - TILE, TILE)] if cut else [(at, size)]
         at += size
     widest = max(size for _, size in steps)
+    group_arrays = [a for g in groups for a in g]
+    early = sum(g[0].shape[0] for g in groups) // rows
+    inputs = len(flat) + 4 + 2 + len(group_arrays)
     third = units // 3 if units % (3 * TILE) == 0 else units
 
     def body(*refs):
@@ -287,7 +297,9 @@
             for s in range(2)
         ]
         h_refs = refs[len(flat) : len(flat) + 4]
-        out_ref, token_ref, hid_ref, quant_ref, buffer, sems = refs[len(flat) + 4 :]
+        gate_ref, up_ref, *group_refs = refs[len(flat) + 4 : inputs]
+        out_ref, gate_out, up_out, token_ref = refs[inputs : inputs + 4]
+        hid_ref, quant_ref, buffer, sems, gate_buf, up_buf, row_sems = refs[inputs + 4 :]
         token_ref[...] = jnp.zeros(token_ref.shape, F32)
         starts = [pl.multiple_of(s * rows, rows) for s in ring_sources(n_tp, offsets)]
         for j, ref in enumerate(h_refs):
@@ -306,6 +318,19 @@
                 )
                 for k in range(split)
             ]
+
+        row_copies = []
+        sums = [r for g in grouped(group_refs, [2] * len(groups)) for r in hidden_rows(g, rows)]
+        for k, grad in enumerate(sums):
+            there = pl.ds(starts[k], rows)
+            here = pl.ds(k * rows, rows)
+            gate_buf[here, :] = (grad * gate_ref[there, :]).astype(BF16)
+            up_buf[here, :] = (grad * up_ref[there, :]).astype(BF16)
+            for h, (buf, out) in enumerate(((gate_buf, gate_out), (up_buf, up_out))):
+                row_copies.append(
+                    pltpu.make_async_copy(buf.at[here], out.at[there], row_sems.at[h, k])
+                )
+                row_copies[-1].start()
 
         for i, (at, size) in enumerate(steps):
             if i >= slots:
@@ -336,56 +361,46 @@
         for i in range(max(0, len(steps) - slots), len(steps)):
             for copy in copies(i):
                 copy.wait()
+        for copy in row_copies:
+            copy.wait()
 
     return pl.pallas_call(
         body,
         name="down_product",
-        out_shape=[like(part, units), like(8, TILE, dtype=F32)],
-        in_specs=[VMEM] * (len(flat) + 4),
-        out_specs=[HBM, VMEM],
+        out_shape=[like(part, units), like(tokens, units), like(tokens, units), like(8, TILE, dtype=F32)],
+        in_specs=[VMEM] * inputs,
+        out_specs=[HBM] * 3 + [VMEM],
         scratch_shapes=[
             pltpu.VMEM((4 * tokens, units), BF16),
             pltpu.VMEM((4 * tokens, widest), BF16),
             pltpu.VMEM((slots, widest, units), BF16),
             pltpu.SemaphoreType.DMA((slots, split)),
+            pltpu.VMEM((early * rows, units), BF16),
+            pltpu.VMEM((early * rows, units), BF16),
+            pltpu.SemaphoreType.DMA((2, early)),
         ],
         compiler_params=pltpu.CompilerParams(vmem_limit_bytes=24 * MIB),
         cost_estimate=pl.CostEstimate(
             flops=8 * part * tokens * units, bytes_accessed=2 * part * units, transcendentals=0
         ),
-    )(*flat, *hiddens)
-
-
-def last_step(n_tp, offsets, gate_factor, up_factor, groups, lengths, token):
+    )(*flat, *hiddens, gate_factor, up_factor, *group_arrays)
+
+
+def last_step(n_tp, offsets, gate_factor, up_factor, group, gate_grad, up_grad, token):
     tokens, units = gate_factor.shape
-    sizes = [len(g) for g in groups]
-    flat = [a for g in groups for a in g]
     rows = tokens // len(offsets)
-    split = 2
-    half = units // split
-
-    def body(gate_ref, up_ref, _, *refs):
-        ins = refs[: len(flat)]
-        gate_out, up_out, gate_buf, up_buf, sems = refs[len(flat) :]
-        starts = [pl.multiple_of(s * rows, rows) for s in ring_sources(n_tp, offsets)]
+    count = group[0].shape[0] // rows
+
+    def body(gate_ref, up_ref, _, own, other, __, ___, gate_out, up_out, gate_buf, up_buf, sems):
+        starts = ring_sources(n_tp, offsets[len(offsets) - count :])
         copies = []
-        for h in range(split):
-            cols = slice(h * half, (h + 1) * half)
-            at = piece = 0
-            for size, length in zip(sizes, lengths):
-                for first in range(0, length, rows):
-                    where = pl.ds(starts[piece], rows)
-                    grad = ins[at][first : first + rows, cols].astype(F32)
-                    for ref in ins[at + 1 : at + size]:
-                        grad = grad + ref[first : first + rows, cols].astype(F32)
-                    gate_buf[where, cols] = (grad * gate_ref[where, cols]).astype(BF16)
-                    up_buf[where, cols] = (grad * up_ref[where, cols]).astype(BF16)
-                    piece += 1
-                at += size
-            for k, (buf, out) in enumerate(((gate_buf, gate_out), (up_buf, up_out))):
-                copies.append(
-                    pltpu.make_async_copy(buf.at[:, cols], out.at[:, cols], sems.at[k, h])
-                )
+        for k, grad in enumerate(hidden_rows((own, other), rows)):
+            where = pl.ds(pl.multiple_of(starts[k] * rows, rows), rows)
+            here = pl.ds(k * rows, rows)
+            gate_buf[here, :] = (grad * gate_ref[where, :]).astype(BF16)
+            up_buf[here, :] = (grad * up_ref[where, :]).astype(BF16)
+            for h, (buf, out) in enumerate(((gate_buf, gate_out), (up_buf, up_out))):
+                copies.append(pltpu.make_async_copy(buf.at[here], out.at[where], sems.at[h, k]))
                 copies[-1].start()
         for copy in copies:
             copy.wait()
@@ -394,15 +409,16 @@
         body,
         name="last_step",
         out_shape=[like(tokens, units)] * 2,
-        in_specs=[VMEM] * (3 + len(flat)),
+        in_specs=[VMEM] * 5 + [HBM] * 2,
         out_specs=[HBM] * 2,
-        scratch_shapes=[pltpu.VMEM((tokens, units), BF16)] * 2
-        + [pltpu.SemaphoreType.DMA((2, split))],
-        compiler_params=pltpu.CompilerParams(vmem_limit_bytes=16 * MIB),
+        input_output_aliases={5: 0, 6: 1},
+        scratch_shapes=[pltpu.VMEM((count * rows, units), BF16)] * 2
+        + [pltpu.SemaphoreType.DMA((2, count))],
+        compiler_params=pltpu.CompilerParams(vmem_limit_bytes=48 * MIB),
         cost_estimate=pl.CostEstimate(
             flops=8 * tokens * units, bytes_accessed=16 * tokens * units, transcendentals=0
         ),
-    )(gate_factor, up_factor, token, *flat)
+    )(gate_factor, up_factor, token, *group, gate_grad, up_grad)
 
 
 def after(value, *others):
@@ -483,21 +499,18 @@
     )
     part3 = partial_hidden(rows, pieces[first:-1] + [late], weights)
     sum3 = flip(part3[1], 2)
-    down_grad, token = down_product(
+    down_grad, gate_grad, up_grad, token = down_product(
         n_tp,
         offsets,
         pieces,
         [other1, other2],
         [hidden_own, hidden_chip, hidden_core, hidden_far],
-    )
-    gate_grad, up_grad = last_step(
-        n_tp,
-        offsets,
         gate_factor,
         up_factor,
-        [[part1[0], sum1], [part2[0], sum2], [part3[0], sum3]],
-        [3 * rows, (first - 3) * rows, 3 * rows],
-        token,
+        [(part1[0], sum1), (part2[0], sum2)],
+    )
+    gate_grad, up_grad = last_step(
+        n_tp, offsets, gate_factor, up_factor, (part3[0], sum3), gate_grad, up_grad, token
     )
     return gate_grad, up_grad, down_grad
 

time: 44.9 us -> 44.6 us (level)
  transfers between devices with their start and end apart: 16 -> 16, of which waited for: 6 -> 6; matrix products, arithmetic and copies ran while one was open for 2% -> 2% of each run, Pallas kernels for 40% -> 41%
where the time goes in v6:
time: 44.6 us; the launch traced here: 44.4 us
  Pallas kernels  20.1 us (45%)
  starting transfers between devices  16.6 us (37%)
  waiting for transfers between devices  5.77 us (13%)
  between operations  0.95 us (2%)
  local copies, waits for them, and re-layouts  0.87 us (2%)
    ppermute x16, starting transfers between devices, permute(): return lax.ppermute(value, BOTH, pairs)  16.6 us
    pallas_call x3, Pallas kernels, weight_rows(): pl.pallas_call(body, name='weight_rows', out_shape=like(count, units), in...  6.45 us
    pallas_call x3, Pallas kernels, partial_hidden(): pl.pallas_call(body, name='partial_hidden', out_shape=[like(each, units,...  6.2 us
    ppermute x16, waiting for transfers between devices, permute(): return lax.ppermute(value, BOTH, pairs)  5.77 us
    pallas_call x1, Pallas kernels, down_product(): pl.pallas_call(body, name='down_product', out_shape=[like(part, units), l...  4.84 us
    pallas_call x1, Pallas kernels, split_columns(): pl.pallas_call(body, name='split_columns', out_shape=[pltpu.VMEM((rows, p...  1.31 us
  transfers between devices with their start and end apart: 16, of which 6 were waited for; matrix products, arithmetic and copies ran while one was open for 2% of the time, Pallas kernels for 41%

profile of v6, /device:TPU:0, one launch (start us, length us, event | category | flops | bytes accessed | tf_op | source)
XLA Modules:
  0.0 44.4 jit_solution(18255432511038992957)
XLA Ops:
  0.6 1.3 %split_columns.1 = (bf16[16,1792]{1,0:T(8,128)(2,1)S(1)}, bf16[16,1792]{1,0:T(8,128)(2,1)S(1)}, bf16[32,1792]{1,0:T(8,128)(2,1)S(1)}, bf16[128,1536]{1,0:T(8,128)(2,1)S(1)}, bf16[128,1536]{1,0:T(8,128)(2,1)S(1)}) custom-call(bf16[16,7168]{1,0:T(8,128)(2,1)} %grad_ref.1, bf16[128,1536]{1,0:T(8,128)(2,1)} %gate_ref.1, bf16[128,1536]{1,0:T(8,128)(2,1)} %up_ref.1), custom_call_target="tpu_custom_call" | custom-call | tf_op jit(solution)/shard_map/split_columns/pallas_call | solution.py:124
  2.0 3.0 %collective-permute-start = (bf16[32,1792]{1,0:T(8,128)(2,1)S(1)}, bf16[32,1792]{1,0:T(8,128)(2,1)S(1)}, u32[]{:S(2)}, u32[]{:S(2)}) collective-permute-start(bf16[32,1792]{1,0:T(8,128)(2,1)S(1)} %get-tuple-element.44), channel_id=1, source_target_pairs={{0,16},{1,17},{2,18},{3,19},{4,20},{5,21},{6,22},{7,23},{8,24},{9,... | collective-permute-start | bytes 344072 | tf_op jit(solution)/shard_map/ppermute | solution.py:440
  5.0 0.8 %copy.10 = bf16[56,12]{1,0:T(8,128)(2,1)S(1)} copy(bf16[56,12]{0,1:T(8,128)(2,1)} %param.9) | data formatting | bytes 2688 | tf_op jit(solution)/shard_map/optimization_barrier | solution.py:425
  5.8 0.6 %hidden_quant.1 = (bf16[128,1536]{1,0:T(8,128)(2,1)S(1)}, f32[128,1536]{1,0:T(8,128)S(1)}, f32[128,1536]{1,0:T(8,128)S(1)}) custom-call(bf16[128,1536]{1,0:T(8,128)(2,1)S(1)} %get-tuple-element.40.gate_ref, bf16[128,1536]{1,0:T(8,128)(2,1)S(1)} %get-tuple-element.41.up_ref), custom_call_target="tpu_custom_call" | custom-call | flops 3932160 | bytes 2752512 | tf_op jit(solution)/shard_map/hidden_quant/pallas_call | solution.py:149
  6.3 1.7 %weight_rows.3.refs_3_.refs_2_ = bf16[768,1536]{1,0:T(8,128)(2,1)S(1)} custom-call(f32[56,12]{1,0:T(8,128)S(1)} %convert_element_type.3.scale_ref, bf16[7168,1536]{1,0:T(8,128)(2,1)} %weight_ref.5), custom_call_target="tpu_custom_call" | custom-call | flops 1179648 | bytes 4718592 | tf_op jit(solution)/shard_map/weight_rows/pallas_call | solution.py:192
  8.1 0.0 collective-permute-done
  8.1 1.9 %collective-permute-start.2 = (bf16[64,1792]{1,0:T(8,128)(2,1)S(1)}, bf16[64,1792]{1,0:T(8,128)(2,1)S(1)}, u32[]{:S(2)}, u32[]{:S(2)}) collective-permute-start(bf16[64,1792]{1,0:T(8,128)(2,1)S(1)} %pad_maximum_fusion.1.refs_0_), channel_id=1, source_target_pairs={{0,2},{1,0},{2,4},{3,1},{4,6},{5,3},{6,7},{7,5},{8,10},{9,8},{10,1... | collective-permute-start | bytes 688136 | tf_op jit(solution)/shard_map/ppermute | solution.py:440
  10.0 0.2 collective-permute-start.1
  10.2 1.7 %collective-permute-start.12 = (bf16[128,1536]{1,0:T(8,128)(2,1)S(1)}, bf16[128,1536]{1,0:T(8,128)(2,1)S(1)}, u32[]{:S(2)}, u32[]{:S(2)}) collective-permute-start(bf16[128,1536]{1,0:T(8,128)(2,1)S(1)} %get-tuple-element.45.refs_10_), channel_id=1, source_target_pairs={{0,16},{1,17},{2,18},{3,19},{4,20},{5,21},{6,22},{7,23},{8,24},{9,... | collective-permute-start | bytes 1179656 | tf_op jit(solution)/shard_map/ppermute | solution.py:440
  12.0 2.7 %weight_rows.4.refs_4_.refs_3_ = bf16[1792,1536]{1,0:T(8,128)(2,1)S(1)} custom-call(f32[56,12]{1,0:T(8,128)S(1)} %convert_element_type.3.scale_ref, bf16[7168,1536]{1,0:T(8,128)(2,1)} %weight_ref.5), custom_call_target="tpu_custom_call" | custom-call | flops 2752512 | bytes 11010048 | tf_op jit(solution)/shard_map/weight_rows/pallas_call | solution.py:192
  14.7 0.5 %collective-permute-done.2.refs_2_ = bf16[64,1792]{1,0:T(8,128)(2,1)S(1)} collective-permute-done((bf16[64,1792]{1,0:T(8,128)(2,1)S(1)}, bf16[64,1792]{1,0:T(8,128)(2,1)S(1)}, u32[]{:S(2)}, u32[]{:S(2)}) %collective-permute-start.2) | collective-permute-done | bytes 229408 | tf_op jit(solution)/shard_map/ppermute | solution.py:440
  15.2 1.6 %collective-permute-start.4 = (bf16[64,1792]{1,0:T(8,128)(2,1)S(1)}, bf16[64,1792]{1,0:T(8,128)(2,1)S(1)}, u32[]{:S(2)}, u32[]{:S(2)}) collective-permute-start(bf16[64,1792]{1,0:T(8,128)(2,1)S(1)} %collective-permute-done.2.refs_2_), channel_id=1, source_target_pairs={{0,2},{1,0},{2,4},{3,1},{4,6},{5,3},{6,7},{7,5},{8,10},{9,8},{10,1... | collective-permute-start | bytes 688136 | tf_op jit(solution)/shard_map/ppermute | solution.py:440
  16.8 0.5 %collective-permute-start.3 = (bf16[64,1792]{1,0:T(8,128)(2,1)S(1)}, bf16[64,1792]{1,0:T(8,128)(2,1)S(1)}, u32[]{:S(2)}, u32[]{:S(2)}) collective-permute-start(bf16[64,1792]{1,0:T(8,128)(2,1)S(1)} %collective-permute-done.1.refs_1_), channel_id=1, source_target_pairs={{0,1},{1,3},{2,0},{3,5},{4,2},{5,7},{6,4},{7,6},{8,9},{9,11},{10,8... | collective-permute-start | bytes 688136 | tf_op jit(solution)/shard_map/ppermute | solution.py:440
  17.3 2.0 %weight_rows.5.refs_5_.refs_4_ = bf16[1024,1536]{1,0:T(8,128)(2,1)S(1)} custom-call(f32[56,12]{1,0:T(8,128)S(1)} %convert_element_type.3.scale_ref, bf16[7168,1536]{1,0:T(8,128)(2,1)} %weight_ref.5), custom_call_target="tpu_custom_call" | custom-call | flops 1572864 | bytes 6291456 | tf_op jit(solution)/shard_map/weight_rows/pallas_call | solution.py:192
  19.3 2.0 %partial_hidden.3 = (f32[48,1536]{1,0:T(8,128)S(1)}, bf16[48,1536]{1,0:T(8,128)(2,1)S(1)}) custom-call(bf16[64,1792]{1,0:T(8,128)(2,1)S(1)} %pad_maximum_fusion.1.refs_0_, bf16[64,1792]{1,0:T(8,128)(2,1)S(1)} %collective-permute-done.1.refs_1_, bf16[64,1792]{1,0:T(8,128)(2,1)S(1)} %collective-permute-done.2.refs_2_, ...), custom_call_target="tpu_custom_call" | custom-call | flops 1056964608 | bytes 11010048 | tf_op jit(solution)/shard_map/partial_hidden/pallas_call | solution.py:252
  21.3 1.2 %collective-permute-start.10 = (bf16[48,1536]{1,0:T(8,128)(2,1)S(1)}, bf16[48,1536]{1,0:T(8,128)(2,1)S(1)}, u32[]{:S(2)}, u32[]{:S(2)}) collective-permute-start(bf16[48,1536]{1,0:T(8,128)(2,1)S(1)} %get-tuple-element.58), channel_id=1, source_target_pairs={{0,16},{1,17},{2,18},{3,19},{4,20},{5,21},{6,22},{7,23},{8,24},{9,... | collective-permute-start | bytes 442376 | tf_op jit(solution)/shard_map/ppermute | solution.py:440
  22.6 1.6 %collective-permute-start.7 = (bf16[64,1792]{1,0:T(8,128)(2,1)S(1)}, bf16[64,1792]{1,0:T(8,128)(2,1)S(1)}, u32[]{:S(2)}, u32[]{:S(2)}) collective-permute-start(bf16[64,1792]{1,0:T(8,128)(2,1)S(1)} %collective-permute-done.4.refs_1_.refs_4_), channel_id=1, source_target_pairs={{0,2},{1,0},{2,4},{3,1},{4,6},{5,3},{6,7},{7,5},{8,10},{9,8},{10,1... | collective-permute-start | bytes 688136 | tf_op jit(solution)/shard_map/ppermute | solution.py:440
  24.2 2.1 %partial_hidden.4 = (f32[32,1536]{1,0:T(8,128)S(1)}, bf16[32,1536]{1,0:T(8,128)(2,1)S(1)}) custom-call(bf16[64,1792]{1,0:T(8,128)(2,1)S(1)} %collective-permute-done.3.refs_0_.refs_3_, bf16[64,1792]{1,0:T(8,128)(2,1)S(1)} %collective-permute-done.4.refs_1_.refs_4_, bf16[768,1536]{1,0:T(8,128)(2,1)S(1)} %weight_rows.3.refs_3_.refs_2_, ...), custom_call_target="tpu_custom_call" | custom-call | flops 704643072 | bytes 11010048 | tf_op jit(solution)/shard_map/partial_hidden/pallas_call | solution.py:252
  26.3 0.9 %collective-permute-start.11 = (bf16[32,1536]{1,0:T(8,128)(2,1)S(1)}, bf16[32,1536]{1,0:T(8,128)(2,1)S(1)}, u32[]{:S(2)}, u32[]{:S(2)}) collective-permute-start(bf16[32,1536]{1,0:T(8,128)(2,1)S(1)} %get-tuple-element.59), channel_id=1, source_target_pairs={{0,16},{1,17},{2,18},{3,19},{4,20},{5,21},{6,22},{7,23},{8,24},{9,... | collective-permute-start | bytes 294920 | tf_op jit(solution)/shard_map/ppermute | solution.py:440
  27.2 0.4 collective-permute-start.6
  27.7 1.2 %collective-permute-done.7.refs_6_.refs_1_ = bf16[64,1792]{1,0:T(8,128)(2,1)S(1)} collective-permute-done((bf16[64,1792]{1,0:T(8,128)(2,1)S(1)}, bf16[64,1792]{1,0:T(8,128)(2,1)S(1)}, u32[]{:S(2)}, u32[]{:S(2)}) %collective-permute-start.7) | collective-permute-done | bytes 229408 | tf_op jit(solution)/shard_map/ppermute | solution.py:440
  28.9 1.6 %collective-permute-start.8 = (bf16[64,1792]{1,0:T(8,128)(2,1)S(1)}, bf16[64,1792]{1,0:T(8,128)(2,1)S(1)}, u32[]{:S(2)}, u32[]{:S(2)}) collective-permute-start(bf16[64,1792]{1,0:T(8,128)(2,1)S(1)} %collective-permute-done.7.refs_6_.refs_1_), channel_id=1, source_target_pairs={{0,2},{1,0},{2,4},{3,1},{4,6},{5,3},{6,7},{7,5},{8,10},{9,8},{10,1... | collective-permute-start | bytes 688136 | tf_op jit(solution)/shard_map/ppermute | solution.py:440
  30.5 2.8 %collective-permute-done.6.refs_5_.refs_0_ = bf16[64,1792]{1,0:T(8,128)(2,1)S(1)} collective-permute-done((bf16[64,1792]{1,0:T(8,128)(2,1)S(1)}, bf16[64,1792]{1,0:T(8,128)(2,1)S(1)}, u32[]{:S(2)}, u32[]{:S(2)}) %collective-permute-start.6) | collective-permute-done | bytes 229408 | tf_op jit(solution)/shard_map/ppermute | solution.py:440
  33.3 0.6 %collective-permute-start.9 = (bf16[160,1792]{1,0:T(8,128)(2,1)S(1)}, bf16[160,1792]{1,0:T(8,128)(2,1)S(1)}, u32[]{:S(2)}, u32[]{:S(2)}) collective-permute-start(bf16[160,1792]{1,0:T(8,128)(2,1)S(1)} %slice_dynamic-update-slice_fusion), channel_id=1, source_target_pairs={{0,8},{1,9},{2,10},{3,11},{4,12},{5,13},{6,14},{7,15},{8,0},{9,1},... | collective-permute-start | bytes 1720328 | tf_op jit(solution)/shard_map/ppermute | solution.py:440
  33.9 1.0 %collective-permute-done.8.refs_7_.refs_2_ = bf16[64,1792]{1,0:T(8,128)(2,1)S(1)} collective-permute-done((bf16[64,1792]{1,0:T(8,128)(2,1)S(1)}, bf16[64,1792]{1,0:T(8,128)(2,1)S(1)}, u32[]{:S(2)}, u32[]{:S(2)}) %collective-permute-start.8) | collective-permute-done | bytes 229408 | tf_op jit(solution)/shard_map/ppermute | solution.py:440
  34.9 0.1 collective-permute-done.13.refs_13_
  35.0 0.2 collective-permute-start.14
  35.2 2.0 %partial_hidden.5 = (f32[48,1536]{1,0:T(8,128)S(1)}, bf16[48,1536]{1,0:T(8,128)(2,1)S(1)}) custom-call(bf16[64,1792]{1,0:T(8,128)(2,1)S(1)} %collective-permute-done.6.refs_5_.refs_0_, bf16[64,1792]{1,0:T(8,128)(2,1)S(1)} %collective-permute-done.7.refs_6_.refs_1_, bf16[64,1792]{1,0:T(8,128)(2,1)S(1)} %collective-permute-done.8.refs_7_.refs_2_, ...), custom_call_target="tpu_custom_call" | custom-call | flops 1056964608 | bytes 11010048 | tf_op jit(solution)/shard_map/partial_hidden/pallas_call | solution.py:252
  37.3 1.2 %collective-permute-start.15 = (bf16[48,1536]{1,0:T(8,128)(2,1)S(1)}, bf16[48,1536]{1,0:T(8,128)(2,1)S(1)}, u32[]{:S(2)}, u32[]{:S(2)}) collective-permute-start(bf16[48,1536]{1,0:T(8,128)(2,1)S(1)} %get-tuple-element.65), channel_id=1, source_target_pairs={{0,16},{1,17},{2,18},{3,19},{4,20},{5,21},{6,22},{7,23},{8,24},{9,... | collective-permute-start | bytes 442376 | tf_op jit(solution)/shard_map/ppermute | solution.py:440
  38.5 4.8 %down_product.1 = (bf16[1792,1536]{1,0:T(8,128)(2,1)}, bf16[128,1536]{1,0:T(8,128)(2,1)}, bf16[128,1536]{1,0:T(8,128)(2,1)}, f32[8,128]{1,0:T(8,128)S(1)}) custom-call(bf16[64,1792]{1,0:T(8,128)(2,1)S(1)} %pad_maximum_fusion.1.refs_0_, bf16[64,1792]{1,0:T(8,128)(2,1)S(1)} %collective-permute-done.1.refs_1_, ...), custom_call_target="tpu_custom_call" | custom-call | flops 2818572288 | bytes 5505024 | tf_op jit(solution)/shard_map/down_product/pallas_call | solution.py:367
  43.4 0.1 collective-permute-done.15.other
  43.5 0.8 %last_step.1 = (bf16[128,1536]{1,0:T(8,128)(2,1)}, bf16[128,1536]{1,0:T(8,128)(2,1)}) custom-call(f32[128,1536]{1,0:T(8,128)S(1)} %get-tuple-element.42.refs_14_.gate_ref, f32[128,1536]{1,0:T(8,128)S(1)} %get-tuple-element.43.refs_15_.up_ref, f32[8,128]{1,0:T(8,128)S(1)} %get-tuple-element.63._, ...), custom_call_target="tpu_custom_call", output_to_operand_aliasing={{0}: (5, {}), {1}: (6, {})} | custom-call | flops 1572864 | bytes 3145728 | tf_op jit(solution)/shard_map/last_step/pallas_call | solution.py:408
  (23 shorter events, 0.2 us)
Async XLA Ops:
  2.0 6.1 %collective-permute-start = (bf16[32,1792]{1,0:T(8,128)(2,1)S(1)}, bf16[32,1792]{1,0:T(8,128)(2,1)S(1)}, u32[]{:S(2)}, u32[]{:S(2)}) collective-permute-start(bf16[32,1792]{1,0:T(8,128)(2,1)S(1)} %get-tuple-element.44), channel_id=1, source_target_pairs={{0,16},{1,17},{2,18},{3,19},{4,20},{5,21},{6,22},{7,23},{8,24},{9,... | collective-permute-start | bytes 344072 | tf_op jit(solution)/shard_map/ppermute | solution.py:440
  8.1 7.1 %collective-permute-start.2 = (bf16[64,1792]{1,0:T(8,128)(2,1)S(1)}, bf16[64,1792]{1,0:T(8,128)(2,1)S(1)}, u32[]{:S(2)}, u32[]{:S(2)}) collective-permute-start(bf16[64,1792]{1,0:T(8,128)(2,1)S(1)} %pad_maximum_fusion.1.refs_0_), channel_id=1, source_target_pairs={{0,2},{1,0},{2,4},{3,1},{4,6},{5,3},{6,7},{7,5},{8,10},{9,8},{10,1... | collective-permute-start | bytes 688136 | tf_op jit(solution)/shard_map/ppermute | solution.py:440
  10.0 6.8 %collective-permute-start.1 = (bf16[64,1792]{1,0:T(8,128)(2,1)S(1)}, bf16[64,1792]{1,0:T(8,128)(2,1)S(1)}, u32[]{:S(2)}, u32[]{:S(2)}) collective-permute-start(bf16[64,1792]{1,0:T(8,128)(2,1)S(1)} %pad_maximum_fusion.1.refs_0_), channel_id=1, source_target_pairs={{0,1},{1,3},{2,0},{3,5},{4,2},{5,7},{6,4},{7,6},{8,9},{9,11},{10,8... | collective-permute-start | bytes 688136 | tf_op jit(solution)/shard_map/ppermute | solution.py:440
  10.2 7.1 %collective-permute-start.5 = (bf16[128,1536]{1,0:T(8,128)(2,1)S(1)}, bf16[128,1536]{1,0:T(8,128)(2,1)S(1)}, u32[]{:S(2)}, u32[]{:S(2)}) collective-permute-start(bf16[128,1536]{1,0:T(8,128)(2,1)S(1)} %get-tuple-element.45.refs_10_), channel_id=1, source_target_pairs={{0,8},{1,9},{2,10},{3,11},{4,12},{5,13},{6,14},{7,15},{8,0},{9,1},... | collective-permute-start | bytes 1179656 | tf_op jit(solution)/shard_map/ppermute | solution.py:440
  10.2 20.2 %collective-permute-start.12 = (bf16[128,1536]{1,0:T(8,128)(2,1)S(1)}, bf16[128,1536]{1,0:T(8,128)(2,1)S(1)}, u32[]{:S(2)}, u32[]{:S(2)}) collective-permute-start(bf16[128,1536]{1,0:T(8,128)(2,1)S(1)} %get-tuple-element.45.refs_10_), channel_id=1, source_target_pairs={{0,16},{1,17},{2,18},{3,19},{4,20},{5,21},{6,22},{7,23},{8,24},{9,... | collective-permute-start | bytes 1179656 | tf_op jit(solution)/shard_map/ppermute | solution.py:440
  15.2 7.3 %collective-permute-start.4 = (bf16[64,1792]{1,0:T(8,128)(2,1)S(1)}, bf16[64,1792]{1,0:T(8,128)(2,1)S(1)}, u32[]{:S(2)}, u32[]{:S(2)}) collective-permute-start(bf16[64,1792]{1,0:T(8,128)(2,1)S(1)} %collective-permute-done.2.refs_2_), channel_id=1, source_target_pairs={{0,2},{1,0},{2,4},{3,1},{4,6},{5,3},{6,7},{7,5},{8,10},{9,8},{10,1... | collective-permute-start | bytes 688136 | tf_op jit(solution)/shard_map/ppermute | solution.py:440
  16.8 7.3 %collective-permute-start.3 = (bf16[64,1792]{1,0:T(8,128)(2,1)S(1)}, bf16[64,1792]{1,0:T(8,128)(2,1)S(1)}, u32[]{:S(2)}, u32[]{:S(2)}) collective-permute-start(bf16[64,1792]{1,0:T(8,128)(2,1)S(1)} %collective-permute-done.1.refs_1_), channel_id=1, source_target_pairs={{0,1},{1,3},{2,0},{3,5},{4,2},{5,7},{6,4},{7,6},{8,9},{9,11},{10,8... | collective-permute-start | bytes 688136 | tf_op jit(solution)/shard_map/ppermute | solution.py:440
  21.3 12.5 %collective-permute-start.10 = (bf16[48,1536]{1,0:T(8,128)(2,1)S(1)}, bf16[48,1536]{1,0:T(8,128)(2,1)S(1)}, u32[]{:S(2)}, u32[]{:S(2)}) collective-permute-start(bf16[48,1536]{1,0:T(8,128)(2,1)S(1)} %get-tuple-element.58), channel_id=1, source_target_pairs={{0,16},{1,17},{2,18},{3,19},{4,20},{5,21},{6,22},{7,23},{8,24},{9,... | collective-permute-start | bytes 442376 | tf_op jit(solution)/shard_map/ppermute | solution.py:440
  22.6 6.3 %collective-permute-start.7 = (bf16[64,1792]{1,0:T(8,128)(2,1)S(1)}, bf16[64,1792]{1,0:T(8,128)(2,1)S(1)}, u32[]{:S(2)}, u32[]{:S(2)}) collective-permute-start(bf16[64,1792]{1,0:T(8,128)(2,1)S(1)} %collective-permute-done.4.refs_1_.refs_4_), channel_id=1, source_target_pairs={{0,2},{1,0},{2,4},{3,1},{4,6},{5,3},{6,7},{7,5},{8,10},{9,8},{10,1... | collective-permute-start | bytes 688136 | tf_op jit(solution)/shard_map/ppermute | solution.py:440
  26.3 7.6 %collective-permute-start.11 = (bf16[32,1536]{1,0:T(8,128)(2,1)S(1)}, bf16[32,1536]{1,0:T(8,128)(2,1)S(1)}, u32[]{:S(2)}, u32[]{:S(2)}) collective-permute-start(bf16[32,1536]{1,0:T(8,128)(2,1)S(1)} %get-tuple-element.59), channel_id=1, source_target_pairs={{0,16},{1,17},{2,18},{3,19},{4,20},{5,21},{6,22},{7,23},{8,24},{9,... | collective-permute-start | bytes 294920 | tf_op jit(solution)/shard_map/ppermute | solution.py:440
  27.2 6.0 %collective-permute-start.6 = (bf16[64,1792]{1,0:T(8,128)(2,1)S(1)}, bf16[64,1792]{1,0:T(8,128)(2,1)S(1)}, u32[]{:S(2)}, u32[]{:S(2)}) collective-permute-start(bf16[64,1792]{1,0:T(8,128)(2,1)S(1)} %collective-permute-done.3.refs_0_.refs_3_), channel_id=1, source_target_pairs={{0,1},{1,3},{2,0},{3,5},{4,2},{5,7},{6,4},{7,6},{8,9},{9,11},{10,8... | collective-permute-start | bytes 688136 | tf_op jit(solution)/shard_map/ppermute | solution.py:440
  28.9 6.0 %collective-permute-start.8 = (bf16[64,1792]{1,0:T(8,128)(2,1)S(1)}, bf16[64,1792]{1,0:T(8,128)(2,1)S(1)}, u32[]{:S(2)}, u32[]{:S(2)}) collective-permute-start(bf16[64,1792]{1,0:T(8,128)(2,1)S(1)} %collective-permute-done.7.refs_6_.refs_1_), channel_id=1, source_target_pairs={{0,2},{1,0},{2,4},{3,1},{4,6},{5,3},{6,7},{7,5},{8,10},{9,8},{10,1... | collective-permute-start | bytes 688136 | tf_op jit(solution)/shard_map/ppermute | solution.py:440
  33.2 1.7 %collective-permute-start.13 = (bf16[128,1536]{1,0:T(8,128)(2,1)S(1)}, bf16[128,1536]{1,0:T(8,128)(2,1)S(1)}, u32[]{:S(2)}, u32[]{:S(2)}) collective-permute-start(bf16[128,1536]{1,0:T(8,128)(2,1)S(1)} %collective-permute-done.12.refs_11_), channel_id=1, source_target_pairs={{0,8},{1,9},{2,10},{3,11},{4,12},{5,13},{6,14},{7,15},{8,0},{9,1},... | collective-permute-start | bytes 1179656 | tf_op jit(solution)/shard_map/ppermute | solution.py:440
  33.3 5.2 %collective-permute-start.9 = (bf16[160,1792]{1,0:T(8,128)(2,1)S(1)}, bf16[160,1792]{1,0:T(8,128)(2,1)S(1)}, u32[]{:S(2)}, u32[]{:S(2)}) collective-permute-start(bf16[160,1792]{1,0:T(8,128)(2,1)S(1)} %slice_dynamic-update-slice_fusion), channel_id=1, source_target_pairs={{0,8},{1,9},{2,10},{3,11},{4,12},{5,13},{6,14},{7,15},{8,0},{9,1},... | collective-permute-start | bytes 1720328 | tf_op jit(solution)/shard_map/ppermute | solution.py:440
  35.0 3.5 %collective-permute-start.14 = (bf16[96,1792]{1,0:T(8,128)(2,1)S(1)}, bf16[96,1792]{1,0:T(8,128)(2,1)S(1)}, u32[]{:S(2)}, u32[]{:S(2)}) collective-permute-start(bf16[96,1792]{1,0:T(8,128)(2,1)S(1)} %pad_maximum_fusion), channel_id=1, source_target_pairs={{0,8},{1,9},{2,10},{3,11},{4,12},{5,13},{6,14},{7,15},{8,0},{9,1},... | collective-permute-start | bytes 1032200 | tf_op jit(solution)/shard_map/ppermute | solution.py:440
  37.3 6.2 %collective-permute-start.15 = (bf16[48,1536]{1,0:T(8,128)(2,1)S(1)}, bf16[48,1536]{1,0:T(8,128)(2,1)S(1)}, u32[]{:S(2)}, u32[]{:S(2)}) collective-permute-start(bf16[48,1536]{1,0:T(8,128)(2,1)S(1)} %get-tuple-element.65), channel_id=1, source_target_pairs={{0,16},{1,17},{2,18},{3,19},{4,20},{5,21},{6,22},{7,23},{8,24},{9,... | collective-permute-start | bytes 442376 | tf_op jit(solution)/shard_map/ppermute | solution.py:440

commit v7 on v6

--- a/solution.py
+++ b/solution.py
@@ -223,7 +223,7 @@
     part = flat[0].shape[1]
     units = weights[0].shape[1]
     each = len(pieces) * rows
-    step = 512 if units % 512 == 0 else 256
+    step = 256
 
     def body(*refs):
         weight_refs = refs[len(flat) : len(flat) + len(weights)]

time: 44.6 us -> 44.6 us (level)
  no operation moved by 1% of the time
where the time goes in v7:
time: 44.6 us; the launch traced here: 44.4 us
  Pallas kernels  20.1 us (45%)
  starting transfers between devices  16.6 us (37%)
  waiting for transfers between devices  5.77 us (13%)
  between operations  0.95 us (2%)
  local copies, waits for them, and re-layouts  0.87 us (2%)
    ppermute x16, starting transfers between devices, permute(): return lax.ppermute(value, BOTH, pairs)  16.6 us
    pallas_call x3, Pallas kernels, weight_rows(): pl.pallas_call(body, name='weight_rows', out_shape=like(count, units), in...  6.45 us
    pallas_call x3, Pallas kernels, partial_hidden(): pl.pallas_call(body, name='partial_hidden', out_shape=[like(each, units,...  6.2 us
    ppermute x16, waiting for transfers between devices, permute(): return lax.ppermute(value, BOTH, pairs)  5.77 us
    pallas_call x1, Pallas kernels, down_product(): pl.pallas_call(body, name='down_product', out_shape=[like(part, units), l...  4.84 us
    pallas_call x1, Pallas kernels, split_columns(): pl.pallas_call(body, name='split_columns', out_shape=[pltpu.VMEM((rows, p...  1.31 us
  transfers between devices with their start and end apart: 16, of which 6 were waited for; matrix products, arithmetic and copies ran while one was open for 2% of the time, Pallas kernels for 41%

profile of v7, /device:TPU:0, one launch (start us, length us, event | category | flops | bytes accessed | tf_op | source)
XLA Modules:
  0.0 44.4 jit_solution(16030031159660794158)
XLA Ops:
  0.6 1.3 %split_columns.1 = (bf16[16,1792]{1,0:T(8,128)(2,1)S(1)}, bf16[16,1792]{1,0:T(8,128)(2,1)S(1)}, bf16[32,1792]{1,0:T(8,128)(2,1)S(1)}, bf16[128,1536]{1,0:T(8,128)(2,1)S(1)}, bf16[128,1536]{1,0:T(8,128)(2,1)S(1)}) custom-call(bf16[16,7168]{1,0:T(8,128)(2,1)} %grad_ref.1, bf16[128,1536]{1,0:T(8,128)(2,1)} %gate_ref.1, bf16[128,1536]{1,0:T(8,128)(2,1)} %up_ref.1), custom_call_target="tpu_custom_call" | custom-call | tf_op jit(solution)/shard_map/split_columns/pallas_call | solution.py:124
  2.0 3.0 %collective-permute-start = (bf16[32,1792]{1,0:T(8,128)(2,1)S(1)}, bf16[32,1792]{1,0:T(8,128)(2,1)S(1)}, u32[]{:S(2)}, u32[]{:S(2)}) collective-permute-start(bf16[32,1792]{1,0:T(8,128)(2,1)S(1)} %get-tuple-element.44), channel_id=1, source_target_pairs={{0,16},{1,17},{2,18},{3,19},{4,20},{5,21},{6,22},{7,23},{8,24},{9,... | collective-permute-start | bytes 344072 | tf_op jit(solution)/shard_map/ppermute | solution.py:440
  5.0 0.8 %copy.10 = bf16[56,12]{1,0:T(8,128)(2,1)S(1)} copy(bf16[56,12]{0,1:T(8,128)(2,1)} %param.9) | data formatting | bytes 2688 | tf_op jit(solution)/shard_map/optimization_barrier | solution.py:425
  5.8 0.6 %hidden_quant.1 = (bf16[128,1536]{1,0:T(8,128)(2,1)S(1)}, f32[128,1536]{1,0:T(8,128)S(1)}, f32[128,1536]{1,0:T(8,128)S(1)}) custom-call(bf16[128,1536]{1,0:T(8,128)(2,1)S(1)} %get-tuple-element.40.gate_ref, bf16[128,1536]{1,0:T(8,128)(2,1)S(1)} %get-tuple-element.41.up_ref), custom_call_target="tpu_custom_call" | custom-call | flops 3932160 | bytes 2752512 | tf_op jit(solution)/shard_map/hidden_quant/pallas_call | solution.py:149
  6.3 1.7 %weight_rows.3.refs_3_.refs_2_ = bf16[768,1536]{1,0:T(8,128)(2,1)S(1)} custom-call(f32[56,12]{1,0:T(8,128)S(1)} %convert_element_type.3.scale_ref, bf16[7168,1536]{1,0:T(8,128)(2,1)} %weight_ref.5), custom_call_target="tpu_custom_call" | custom-call | flops 1179648 | bytes 4718592 | tf_op jit(solution)/shard_map/weight_rows/pallas_call | solution.py:192
  8.1 0.0 collective-permute-done
  8.1 1.9 %collective-permute-start.2 = (bf16[64,1792]{1,0:T(8,128)(2,1)S(1)}, bf16[64,1792]{1,0:T(8,128)(2,1)S(1)}, u32[]{:S(2)}, u32[]{:S(2)}) collective-permute-start(bf16[64,1792]{1,0:T(8,128)(2,1)S(1)} %pad_maximum_fusion.1.refs_0_), channel_id=1, source_target_pairs={{0,2},{1,0},{2,4},{3,1},{4,6},{5,3},{6,7},{7,5},{8,10},{9,8},{10,1... | collective-permute-start | bytes 688136 | tf_op jit(solution)/shard_map/ppermute | solution.py:440
  10.0 0.2 collective-permute-start.1
  10.2 1.7 %collective-permute-start.12 = (bf16[128,1536]{1,0:T(8,128)(2,1)S(1)}, bf16[128,1536]{1,0:T(8,128)(2,1)S(1)}, u32[]{:S(2)}, u32[]{:S(2)}) collective-permute-start(bf16[128,1536]{1,0:T(8,128)(2,1)S(1)} %get-tuple-element.45.refs_10_), channel_id=1, source_target_pairs={{0,16},{1,17},{2,18},{3,19},{4,20},{5,21},{6,22},{7,23},{8,24},{9,... | collective-permute-start | bytes 1179656 | tf_op jit(solution)/shard_map/ppermute | solution.py:440
  12.0 2.7 %weight_rows.4.refs_4_.refs_3_ = bf16[1792,1536]{1,0:T(8,128)(2,1)S(1)} custom-call(f32[56,12]{1,0:T(8,128)S(1)} %convert_element_type.3.scale_ref, bf16[7168,1536]{1,0:T(8,128)(2,1)} %weight_ref.5), custom_call_target="tpu_custom_call" | custom-call | flops 2752512 | bytes 11010048 | tf_op jit(solution)/shard_map/weight_rows/pallas_call | solution.py:192
  14.7 0.5 %collective-permute-done.2.refs_2_ = bf16[64,1792]{1,0:T(8,128)(2,1)S(1)} collective-permute-done((bf16[64,1792]{1,0:T(8,128)(2,1)S(1)}, bf16[64,1792]{1,0:T(8,128)(2,1)S(1)}, u32[]{:S(2)}, u32[]{:S(2)}) %collective-permute-start.2) | collective-permute-done | bytes 229408 | tf_op jit(solution)/shard_map/ppermute | solution.py:440
  15.2 1.6 %collective-permute-start.4 = (bf16[64,1792]{1,0:T(8,128)(2,1)S(1)}, bf16[64,1792]{1,0:T(8,128)(2,1)S(1)}, u32[]{:S(2)}, u32[]{:S(2)}) collective-permute-start(bf16[64,1792]{1,0:T(8,128)(2,1)S(1)} %collective-permute-done.2.refs_2_), channel_id=1, source_target_pairs={{0,2},{1,0},{2,4},{3,1},{4,6},{5,3},{6,7},{7,5},{8,10},{9,8},{10,1... | collective-permute-start | bytes 688136 | tf_op jit(solution)/shard_map/ppermute | solution.py:440
  16.8 0.5 %collective-permute-start.3 = (bf16[64,1792]{1,0:T(8,128)(2,1)S(1)}, bf16[64,1792]{1,0:T(8,128)(2,1)S(1)}, u32[]{:S(2)}, u32[]{:S(2)}) collective-permute-start(bf16[64,1792]{1,0:T(8,128)(2,1)S(1)} %collective-permute-done.1.refs_1_), channel_id=1, source_target_pairs={{0,1},{1,3},{2,0},{3,5},{4,2},{5,7},{6,4},{7,6},{8,9},{9,11},{10,8... | collective-permute-start | bytes 688136 | tf_op jit(solution)/shard_map/ppermute | solution.py:440
  17.3 2.0 %weight_rows.5.refs_5_.refs_4_ = bf16[1024,1536]{1,0:T(8,128)(2,1)S(1)} custom-call(f32[56,12]{1,0:T(8,128)S(1)} %convert_element_type.3.scale_ref, bf16[7168,1536]{1,0:T(8,128)(2,1)} %weight_ref.5), custom_call_target="tpu_custom_call" | custom-call | flops 1572864 | bytes 6291456 | tf_op jit(solution)/shard_map/weight_rows/pallas_call | solution.py:192
  19.3 2.0 %partial_hidden.3 = (f32[48,1536]{1,0:T(8,128)S(1)}, bf16[48,1536]{1,0:T(8,128)(2,1)S(1)}) custom-call(bf16[64,1792]{1,0:T(8,128)(2,1)S(1)} %pad_maximum_fusion.1.refs_0_, bf16[64,1792]{1,0:T(8,128)(2,1)S(1)} %collective-permute-done.1.refs_1_, bf16[64,1792]{1,0:T(8,128)(2,1)S(1)} %collective-permute-done.2.refs_2_, ...), custom_call_target="tpu_custom_call" | custom-call | flops 1056964608 | bytes 11010048 | tf_op jit(solution)/shard_map/partial_hidden/pallas_call | solution.py:252
  21.3 1.2 %collective-permute-start.10 = (bf16[48,1536]{1,0:T(8,128)(2,1)S(1)}, bf16[48,1536]{1,0:T(8,128)(2,1)S(1)}, u32[]{:S(2)}, u32[]{:S(2)}) collective-permute-start(bf16[48,1536]{1,0:T(8,128)(2,1)S(1)} %get-tuple-element.58), channel_id=1, source_target_pairs={{0,16},{1,17},{2,18},{3,19},{4,20},{5,21},{6,22},{7,23},{8,24},{9,... | collective-permute-start | bytes 442376 | tf_op jit(solution)/shard_map/ppermute | solution.py:440
  22.6 1.6 %collective-permute-start.7 = (bf16[64,1792]{1,0:T(8,128)(2,1)S(1)}, bf16[64,1792]{1,0:T(8,128)(2,1)S(1)}, u32[]{:S(2)}, u32[]{:S(2)}) collective-permute-start(bf16[64,1792]{1,0:T(8,128)(2,1)S(1)} %collective-permute-done.4.refs_1_.refs_4_), channel_id=1, source_target_pairs={{0,2},{1,0},{2,4},{3,1},{4,6},{5,3},{6,7},{7,5},{8,10},{9,8},{10,1... | collective-permute-start | bytes 688136 | tf_op jit(solution)/shard_map/ppermute | solution.py:440
  24.2 2.1 %partial_hidden.4 = (f32[32,1536]{1,0:T(8,128)S(1)}, bf16[32,1536]{1,0:T(8,128)(2,1)S(1)}) custom-call(bf16[64,1792]{1,0:T(8,128)(2,1)S(1)} %collective-permute-done.3.refs_0_.refs_3_, bf16[64,1792]{1,0:T(8,128)(2,1)S(1)} %collective-permute-done.4.refs_1_.refs_4_, bf16[768,1536]{1,0:T(8,128)(2,1)S(1)} %weight_rows.3.refs_3_.refs_2_, ...), custom_call_target="tpu_custom_call" | custom-call | flops 704643072 | bytes 11010048 | tf_op jit(solution)/shard_map/partial_hidden/pallas_call | solution.py:252
  26.3 0.9 %collective-permute-start.11 = (bf16[32,1536]{1,0:T(8,128)(2,1)S(1)}, bf16[32,1536]{1,0:T(8,128)(2,1)S(1)}, u32[]{:S(2)}, u32[]{:S(2)}) collective-permute-start(bf16[32,1536]{1,0:T(8,128)(2,1)S(1)} %get-tuple-element.59), channel_id=1, source_target_pairs={{0,16},{1,17},{2,18},{3,19},{4,20},{5,21},{6,22},{7,23},{8,24},{9,... | collective-permute-start | bytes 294920 | tf_op jit(solution)/shard_map/ppermute | solution.py:440
  27.2 0.4 collective-permute-start.6
  27.7 1.2 %collective-permute-done.7.refs_6_.refs_1_ = bf16[64,1792]{1,0:T(8,128)(2,1)S(1)} collective-permute-done((bf16[64,1792]{1,0:T(8,128)(2,1)S(1)}, bf16[64,1792]{1,0:T(8,128)(2,1)S(1)}, u32[]{:S(2)}, u32[]{:S(2)}) %collective-permute-start.7) | collective-permute-done | bytes 229408 | tf_op jit(solution)/shard_map/ppermute | solution.py:440
  28.9 1.6 %collective-permute-start.8 = (bf16[64,1792]{1,0:T(8,128)(2,1)S(1)}, bf16[64,1792]{1,0:T(8,128)(2,1)S(1)}, u32[]{:S(2)}, u32[]{:S(2)}) collective-permute-start(bf16[64,1792]{1,0:T(8,128)(2,1)S(1)} %collective-permute-done.7.refs_6_.refs_1_), channel_id=1, source_target_pairs={{0,2},{1,0},{2,4},{3,1},{4,6},{5,3},{6,7},{7,5},{8,10},{9,8},{10,1... | collective-permute-start | bytes 688136 | tf_op jit(solution)/shard_map/ppermute | solution.py:440
  30.5 2.8 %collective-permute-done.6.refs_5_.refs_0_ = bf16[64,1792]{1,0:T(8,128)(2,1)S(1)} collective-permute-done((bf16[64,1792]{1,0:T(8,128)(2,1)S(1)}, bf16[64,1792]{1,0:T(8,128)(2,1)S(1)}, u32[]{:S(2)}, u32[]{:S(2)}) %collective-permute-start.6) | collective-permute-done | bytes 229408 | tf_op jit(solution)/shard_map/ppermute | solution.py:440
  33.3 0.6 %collective-permute-start.9 = (bf16[160,1792]{1,0:T(8,128)(2,1)S(1)}, bf16[160,1792]{1,0:T(8,128)(2,1)S(1)}, u32[]{:S(2)}, u32[]{:S(2)}) collective-permute-start(bf16[160,1792]{1,0:T(8,128)(2,1)S(1)} %slice_dynamic-update-slice_fusion), channel_id=1, source_target_pairs={{0,8},{1,9},{2,10},{3,11},{4,12},{5,13},{6,14},{7,15},{8,0},{9,1},... | collective-permute-start | bytes 1720328 | tf_op jit(solution)/shard_map/ppermute | solution.py:440
  33.9 1.0 %collective-permute-done.8.refs_7_.refs_2_ = bf16[64,1792]{1,0:T(8,128)(2,1)S(1)} collective-permute-done((bf16[64,1792]{1,0:T(8,128)(2,1)S(1)}, bf16[64,1792]{1,0:T(8,128)(2,1)S(1)}, u32[]{:S(2)}, u32[]{:S(2)}) %collective-permute-start.8) | collective-permute-done | bytes 229408 | tf_op jit(solution)/shard_map/ppermute | solution.py:440
  34.9 0.1 collective-permute-done.13.refs_13_
  35.0 0.2 collective-permute-start.14
  35.2 2.0 %partial_hidden.5 = (f32[48,1536]{1,0:T(8,128)S(1)}, bf16[48,1536]{1,0:T(8,128)(2,1)S(1)}) custom-call(bf16[64,1792]{1,0:T(8,128)(2,1)S(1)} %collective-permute-done.6.refs_5_.refs_0_, bf16[64,1792]{1,0:T(8,128)(2,1)S(1)} %collective-permute-done.7.refs_6_.refs_1_, bf16[64,1792]{1,0:T(8,128)(2,1)S(1)} %collective-permute-done.8.refs_7_.refs_2_, ...), custom_call_target="tpu_custom_call" | custom-call | flops 1056964608 | bytes 11010048 | tf_op jit(solution)/shard_map/partial_hidden/pallas_call | solution.py:252
  37.3 1.2 %collective-permute-start.15 = (bf16[48,1536]{1,0:T(8,128)(2,1)S(1)}, bf16[48,1536]{1,0:T(8,128)(2,1)S(1)}, u32[]{:S(2)}, u32[]{:S(2)}) collective-permute-start(bf16[48,1536]{1,0:T(8,128)(2,1)S(1)} %get-tuple-element.65), channel_id=1, source_target_pairs={{0,16},{1,17},{2,18},{3,19},{4,20},{5,21},{6,22},{7,23},{8,24},{9,... | collective-permute-start | bytes 442376 | tf_op jit(solution)/shard_map/ppermute | solution.py:440
  38.5 4.8 %down_product.1 = (bf16[1792,1536]{1,0:T(8,128)(2,1)}, bf16[128,1536]{1,0:T(8,128)(2,1)}, bf16[128,1536]{1,0:T(8,128)(2,1)}, f32[8,128]{1,0:T(8,128)S(1)}) custom-call(bf16[64,1792]{1,0:T(8,128)(2,1)S(1)} %pad_maximum_fusion.1.refs_0_, bf16[64,1792]{1,0:T(8,128)(2,1)S(1)} %collective-permute-done.1.refs_1_, ...), custom_call_target="tpu_custom_call" | custom-call | flops 2818572288 | bytes 5505024 | tf_op jit(solution)/shard_map/down_product/pallas_call | solution.py:367
  43.4 0.1 collective-permute-done.15.other
  43.5 0.8 %last_step.1 = (bf16[128,1536]{1,0:T(8,128)(2,1)}, bf16[128,1536]{1,0:T(8,128)(2,1)}) custom-call(f32[128,1536]{1,0:T(8,128)S(1)} %get-tuple-element.42.refs_14_.gate_ref, f32[128,1536]{1,0:T(8,128)S(1)} %get-tuple-element.43.refs_15_.up_ref, f32[8,128]{1,0:T(8,128)S(1)} %get-tuple-element.63._, ...), custom_call_target="tpu_custom_call", output_to_operand_aliasing={{0}: (5, {}), {1}: (6, {})} | custom-call | flops 1572864 | bytes 3145728 | tf_op jit(solution)/shard_map/last_step/pallas_call | solution.py:408
  (23 shorter events, 0.2 us)
Async XLA Ops:
  2.0 6.1 %collective-permute-start = (bf16[32,1792]{1,0:T(8,128)(2,1)S(1)}, bf16[32,1792]{1,0:T(8,128)(2,1)S(1)}, u32[]{:S(2)}, u32[]{:S(2)}) collective-permute-start(bf16[32,1792]{1,0:T(8,128)(2,1)S(1)} %get-tuple-element.44), channel_id=1, source_target_pairs={{0,16},{1,17},{2,18},{3,19},{4,20},{5,21},{6,22},{7,23},{8,24},{9,... | collective-permute-start | bytes 344072 | tf_op jit(solution)/shard_map/ppermute | solution.py:440
  8.1 7.1 %collective-permute-start.2 = (bf16[64,1792]{1,0:T(8,128)(2,1)S(1)}, bf16[64,1792]{1,0:T(8,128)(2,1)S(1)}, u32[]{:S(2)}, u32[]{:S(2)}) collective-permute-start(bf16[64,1792]{1,0:T(8,128)(2,1)S(1)} %pad_maximum_fusion.1.refs_0_), channel_id=1, source_target_pairs={{0,2},{1,0},{2,4},{3,1},{4,6},{5,3},{6,7},{7,5},{8,10},{9,8},{10,1... | collective-permute-start | bytes 688136 | tf_op jit(solution)/shard_map/ppermute | solution.py:440
  10.0 6.8 %collective-permute-start.1 = (bf16[64,1792]{1,0:T(8,128)(2,1)S(1)}, bf16[64,1792]{1,0:T(8,128)(2,1)S(1)}, u32[]{:S(2)}, u32[]{:S(2)}) collective-permute-start(bf16[64,1792]{1,0:T(8,128)(2,1)S(1)} %pad_maximum_fusion.1.refs_0_), channel_id=1, source_target_pairs={{0,1},{1,3},{2,0},{3,5},{4,2},{5,7},{6,4},{7,6},{8,9},{9,11},{10,8... | collective-permute-start | bytes 688136 | tf_op jit(solution)/shard_map/ppermute | solution.py:440
  10.2 7.1 %collective-permute-start.5 = (bf16[128,1536]{1,0:T(8,128)(2,1)S(1)}, bf16[128,1536]{1,0:T(8,128)(2,1)S(1)}, u32[]{:S(2)}, u32[]{:S(2)}) collective-permute-start(bf16[128,1536]{1,0:T(8,128)(2,1)S(1)} %get-tuple-element.45.refs_10_), channel_id=1, source_target_pairs={{0,8},{1,9},{2,10},{3,11},{4,12},{5,13},{6,14},{7,15},{8,0},{9,1},... | collective-permute-start | bytes 1179656 | tf_op jit(solution)/shard_map/ppermute | solution.py:440
  10.2 20.2 %collective-permute-start.12 = (bf16[128,1536]{1,0:T(8,128)(2,1)S(1)}, bf16[128,1536]{1,0:T(8,128)(2,1)S(1)}, u32[]{:S(2)}, u32[]{:S(2)}) collective-permute-start(bf16[128,1536]{1,0:T(8,128)(2,1)S(1)} %get-tuple-element.45.refs_10_), channel_id=1, source_target_pairs={{0,16},{1,17},{2,18},{3,19},{4,20},{5,21},{6,22},{7,23},{8,24},{9,... | collective-permute-start | bytes 1179656 | tf_op jit(solution)/shard_map/ppermute | solution.py:440
  15.2 7.3 %collective-permute-start.4 = (bf16[64,1792]{1,0:T(8,128)(2,1)S(1)}, bf16[64,1792]{1,0:T(8,128)(2,1)S(1)}, u32[]{:S(2)}, u32[]{:S(2)}) collective-permute-start(bf16[64,1792]{1,0:T(8,128)(2,1)S(1)} %collective-permute-done.2.refs_2_), channel_id=1, source_target_pairs={{0,2},{1,0},{2,4},{3,1},{4,6},{5,3},{6,7},{7,5},{8,10},{9,8},{10,1... | collective-permute-start | bytes 688136 | tf_op jit(solution)/shard_map/ppermute | solution.py:440
  16.8 7.3 %collective-permute-start.3 = (bf16[64,1792]{1,0:T(8,128)(2,1)S(1)}, bf16[64,1792]{1,0:T(8,128)(2,1)S(1)}, u32[]{:S(2)}, u32[]{:S(2)}) collective-permute-start(bf16[64,1792]{1,0:T(8,128)(2,1)S(1)} %collective-permute-done.1.refs_1_), channel_id=1, source_target_pairs={{0,1},{1,3},{2,0},{3,5},{4,2},{5,7},{6,4},{7,6},{8,9},{9,11},{10,8... | collective-permute-start | bytes 688136 | tf_op jit(solution)/shard_map/ppermute | solution.py:440
  21.3 12.5 %collective-permute-start.10 = (bf16[48,1536]{1,0:T(8,128)(2,1)S(1)}, bf16[48,1536]{1,0:T(8,128)(2,1)S(1)}, u32[]{:S(2)}, u32[]{:S(2)}) collective-permute-start(bf16[48,1536]{1,0:T(8,128)(2,1)S(1)} %get-tuple-element.58), channel_id=1, source_target_pairs={{0,16},{1,17},{2,18},{3,19},{4,20},{5,21},{6,22},{7,23},{8,24},{9,... | collective-permute-start | bytes 442376 | tf_op jit(solution)/shard_map/ppermute | solution.py:440
  22.6 6.3 %collective-permute-start.7 = (bf16[64,1792]{1,0:T(8,128)(2,1)S(1)}, bf16[64,1792]{1,0:T(8,128)(2,1)S(1)}, u32[]{:S(2)}, u32[]{:S(2)}) collective-permute-start(bf16[64,1792]{1,0:T(8,128)(2,1)S(1)} %collective-permute-done.4.refs_1_.refs_4_), channel_id=1, source_target_pairs={{0,2},{1,0},{2,4},{3,1},{4,6},{5,3},{6,7},{7,5},{8,10},{9,8},{10,1... | collective-permute-start | bytes 688136 | tf_op jit(solution)/shard_map/ppermute | solution.py:440
  26.3 7.6 %collective-permute-start.11 = (bf16[32,1536]{1,0:T(8,128)(2,1)S(1)}, bf16[32,1536]{1,0:T(8,128)(2,1)S(1)}, u32[]{:S(2)}, u32[]{:S(2)}) collective-permute-start(bf16[32,1536]{1,0:T(8,128)(2,1)S(1)} %get-tuple-element.59), channel_id=1, source_target_pairs={{0,16},{1,17},{2,18},{3,19},{4,20},{5,21},{6,22},{7,23},{8,24},{9,... | collective-permute-start | bytes 294920 | tf_op jit(solution)/shard_map/ppermute | solution.py:440
  27.2 6.0 %collective-permute-start.6 = (bf16[64,1792]{1,0:T(8,128)(2,1)S(1)}, bf16[64,1792]{1,0:T(8,128)(2,1)S(1)}, u32[]{:S(2)}, u32[]{:S(2)}) collective-permute-start(bf16[64,1792]{1,0:T(8,128)(2,1)S(1)} %collective-permute-done.3.refs_0_.refs_3_), channel_id=1, source_target_pairs={{0,1},{1,3},{2,0},{3,5},{4,2},{5,7},{6,4},{7,6},{8,9},{9,11},{10,8... | collective-permute-start | bytes 688136 | tf_op jit(solution)/shard_map/ppermute | solution.py:440
  28.9 6.0 %collective-permute-start.8 = (bf16[64,1792]{1,0:T(8,128)(2,1)S(1)}, bf16[64,1792]{1,0:T(8,128)(2,1)S(1)}, u32[]{:S(2)}, u32[]{:S(2)}) collective-permute-start(bf16[64,1792]{1,0:T(8,128)(2,1)S(1)} %collective-permute-done.7.refs_6_.refs_1_), channel_id=1, source_target_pairs={{0,2},{1,0},{2,4},{3,1},{4,6},{5,3},{6,7},{7,5},{8,10},{9,8},{10,1... | collective-permute-start | bytes 688136 | tf_op jit(solution)/shard_map/ppermute | solution.py:440
  33.2 1.7 %collective-permute-start.13 = (bf16[128,1536]{1,0:T(8,128)(2,1)S(1)}, bf16[128,1536]{1,0:T(8,128)(2,1)S(1)}, u32[]{:S(2)}, u32[]{:S(2)}) collective-permute-start(bf16[128,1536]{1,0:T(8,128)(2,1)S(1)} %collective-permute-done.12.refs_11_), channel_id=1, source_target_pairs={{0,8},{1,9},{2,10},{3,11},{4,12},{5,13},{6,14},{7,15},{8,0},{9,1},... | collective-permute-start | bytes 1179656 | tf_op jit(solution)/shard_map/ppermute | solution.py:440
  33.3 5.2 %collective-permute-start.9 = (bf16[160,1792]{1,0:T(8,128)(2,1)S(1)}, bf16[160,1792]{1,0:T(8,128)(2,1)S(1)}, u32[]{:S(2)}, u32[]{:S(2)}) collective-permute-start(bf16[160,1792]{1,0:T(8,128)(2,1)S(1)} %slice_dynamic-update-slice_fusion), channel_id=1, source_target_pairs={{0,8},{1,9},{2,10},{3,11},{4,12},{5,13},{6,14},{7,15},{8,0},{9,1},... | collective-permute-start | bytes 1720328 | tf_op jit(solution)/shard_map/ppermute | solution.py:440
  35.0 3.5 %collective-permute-start.14 = (bf16[96,1792]{1,0:T(8,128)(2,1)S(1)}, bf16[96,1792]{1,0:T(8,128)(2,1)S(1)}, u32[]{:S(2)}, u32[]{:S(2)}) collective-permute-start(bf16[96,1792]{1,0:T(8,128)(2,1)S(1)} %pad_maximum_fusion), channel_id=1, source_target_pairs={{0,8},{1,9},{2,10},{3,11},{4,12},{5,13},{6,14},{7,15},{8,0},{9,1},... | collective-permute-start | bytes 1032200 | tf_op jit(solution)/shard_map/ppermute | solution.py:440
  37.3 6.2 %collective-permute-start.15 = (bf16[48,1536]{1,0:T(8,128)(2,1)S(1)}, bf16[48,1536]{1,0:T(8,128)(2,1)S(1)}, u32[]{:S(2)}, u32[]{:S(2)}) collective-permute-start(bf16[48,1536]{1,0:T(8,128)(2,1)S(1)} %get-tuple-element.65), channel_id=1, source_target_pairs={{0,16},{1,17},{2,18},{3,19},{4,20},{5,21},{6,22},{7,23},{8,24},{9,... | collective-permute-start | bytes 442376 | tf_op jit(solution)/shard_map/ppermute | solution.py:440
